TPU v7x, 32 devices: a whole 2x2x4 slice. The times are simulated.
32 devices in a mesh: fsdp: 32 (over z, y, x, core).
Axes of the slice: x: 2, y: 2, z: 4, core: 2. Of those that a mesh axis runs over, the one named last changes fastest.
Arguments:
- latents: float32 [32, 256, 16], P('fsdp'), may hold values from -6 to 6
- targets: float32 [32, 256, 16], P('fsdp'), may hold values from -6 to 6
- features: float32 [32, 256, 768], P('fsdp'), may hold values from -7 to 7
- time_weights: float32 [32], P('fsdp'), may hold values from 0.5 to 7.5
- timesteps: int32 [32], P('fsdp'), may hold values from 0 to 999
- classes: int32 [32], P('fsdp'), may hold values from 0 to 1000
- block_in: float32 [2, 768, 10752], P(None, 'fsdp'), may hold values from -0.21875 to 0.21875
- block_in_rows: float32 [2, 768], P(None, 'fsdp'), may hold values from 2.49084326e-14 to 6.3765587e-12
- block_in_cols: float32 [2, 10752], replicated, may hold values from 2.49084326e-14 to 6.3765587e-12
- block_down: float32 [2, 3072, 768], P(None, 'fsdp'), may hold values from -0.109375 to 0.109375
- block_down_rows: float32 [2, 3072], P(None, 'fsdp'), may hold values from 7.9706984e-11 to 3.1882794e-10
- block_down_cols: float32 [2, 768], replicated, may hold values from 7.9706984e-11 to 3.1882794e-10
- stem_main: float32 [768, 5625], P('fsdp'), may hold values from -4 to 4
- stem_main_rows: float32 [768], P('fsdp'), may hold values from 7.9706984e-11 to 3.1882794e-10
- stem_main_cols: float32 [5625], replicated, may hold values from 7.9706984e-11 to 3.1882794e-10
- stem_proj: float32 [2048, 2816], P('fsdp'), may hold values from -0.125 to 0.125
- stem_proj_rows: float32 [2048], P('fsdp'), may hold values from 2.4908433e-15 to 6.376559e-13
- stem_proj_cols: float32 [2816], replicated, may hold values from 2.4908433e-15 to 6.376559e-13
- head_weight: float32 [769, 16], replicated, may hold values from -0.21875 to 0.21875
- head_rows: float32 [769], replicated, may hold values from 7.9706984e-11 to 3.1882794e-10
- head_cols: float32 [16], replicated, may hold values from 7.9706984e-11 to 3.1882794e-10
- biases: float32 [31744], P('fsdp'), may hold values from -1.25 to 1.25
- bias_second: float32 [31744], P('fsdp'), may hold values from 7.9706984e-11 to 4e-05
Outputs:
- loss: float32 [], replicated
- grad_norm: float32 [], replicated
- new_block_in: float32 [2, 768, 10752], P(None, 'fsdp')
- clip_block_in: float32 [2, 768, 10752], P(None, 'fsdp')
- rows_block_in: float32 [2, 768], P(None, 'fsdp')
- cols_block_in: float32 [2, 10752], replicated
- copy_block_in: bfloat16 [2, 768, 10752], P(None, 'fsdp')
- new_block_down: float32 [2, 3072, 768], P(None, 'fsdp')
- clip_block_down: float32 [2, 3072, 768], P(None, 'fsdp')
- rows_block_down: float32 [2, 3072], P(None, 'fsdp')
- cols_block_down: float32 [2, 768], replicated
- copy_block_down: bfloat16 [2, 3072, 768], P(None, 'fsdp')
- new_stem_main: float32 [768, 5625], P('fsdp')
- clip_stem_main: float32 [768, 5625], P('fsdp')
- rows_stem_main: float32 [768], P('fsdp')
- cols_stem_main: float32 [5625], replicated
- copy_stem_main: bfloat16 [768, 5625], P('fsdp')
- new_stem_proj: float32 [2048, 2816], P('fsdp')
- clip_stem_proj: float32 [2048, 2816], P('fsdp')
- rows_stem_proj: float32 [2048], P('fsdp')
- cols_stem_proj: float32 [2816], replicated
- copy_stem_proj: bfloat16 [2048, 2816], P('fsdp')
- new_head: float32 [769, 16], replicated
- clip_head: float32 [769, 16], replicated
- rows_head: float32 [769], replicated
- cols_head: float32 [16], replicated
- new_biases: float32 [31744], P('fsdp')
- clip_biases: float32 [31744], P('fsdp')
- second_biases: float32 [31744], P('fsdp')
All inputs are finite; a program needn't handle non-finite values.
Results may differ from a plain program's by a relative error of at most 0.01.
Values may be sent and summed in bfloat16 or wider, within the bound.
No kernel may reach another device: no remote copies, remote signals or barrier semaphores. Data moves between devices by JAX's collectives and lax.ppermute only.
A program may use at most 448 MiB of HBM per device.

v0:
```python
import math

import jax
import jax.numpy as jnp
from jax import lax
from jax.sharding import PartitionSpec as P

D = 768
HD = 64
F = 3072
P_SIZE = 2048
Z = 768
NCLS = 1001
PD = 16
TF = 256
L = 2
GRID = 16
TOK = 256
VB = 11520


NORM_EPS = 1e-06
SCORE_SCALE = 0.125
LEARN_RATE = 0.03
DECAY_RATE = 0.5
CLIP_LIMIT = 0.05
FACTOR_EPS = 1e-30


def cut_parts(array, part_widths):
    borders = []
    running = 0
    for part_width in part_widths[:-1]:
        running += part_width
        borders.append(running)
    return jnp.split(array, borders, axis=-1)


def layer_norm(values):
    centred = values - jnp.mean(values, axis=-1, keepdims=True)
    return centred * lax.rsqrt(jnp.mean(centred * centred, axis=-1, keepdims=True) + NORM_EPS)


def modulate(values, shift_part, scale_part):
    return layer_norm(values) * (1.0 + scale_part[:, None, :]) + shift_part[:, None, :]


def positions():
    quarter = D // 4
    omega_rate = jnp.exp(-math.log(10000.0) * jnp.arange(quarter, dtype=jnp.float32) / quarter)
    token_place = jnp.arange(TOK)
    column = (token_place % GRID).astype(jnp.float32)
    row_place = (token_place // GRID).astype(jnp.float32)

    def encode(coords):
        angles = coords[:, None] * omega_rate[None, :]
        return jnp.concatenate([jnp.sin(angles), jnp.cos(angles)], axis=1)

    return jnp.concatenate([encode(column), encode(row_place)], axis=1)


def time_freq(timesteps):
    half_width = TF // 2
    freq_rate = jnp.exp(-math.log(10000.0) * jnp.arange(half_width, dtype=jnp.float32) / half_width)
    angles = timesteps.astype(jnp.float32)[:, None] * freq_rate[None, :]
    return jnp.concatenate([jnp.cos(angles), jnp.sin(angles)], axis=1)


def cosine_loss(projected, features):
    inner = jnp.sum(projected * features, axis=-1)
    lengths = jnp.sqrt(jnp.sum(projected * projected, axis=-1) + NORM_EPS) * jnp.sqrt(
        jnp.sum(features * features, axis=-1) + NORM_EPS
    )
    return -0.5 * jnp.sum(jnp.mean(inner / lengths, axis=1))


def gelu_tanh(values):
    return jax.nn.gelu(values, approximate=True)


def silu_back(before, grad_after):
    return jax.vjp(jax.nn.silu, before)[1](grad_after)[0]


def total_rows(values):
    return jnp.sum(values.reshape(-1, values.shape[-1]), axis=0)


def linear(left_side, weight_side):
    return jnp.dot(left_side, weight_side, preferred_element_type=jnp.float32)


def linear_back(grad_out, left_side, weight_side):
    grad_low = grad_out.astype(jnp.bfloat16)
    grad_left = lax.dot_general(
        grad_low,
        weight_side,
        (((grad_low.ndim - 1,), (1,)), ((), ())),
        preferred_element_type=jnp.float32,
    )
    flat_left = left_side.reshape(-1, left_side.shape[-1])
    flat_grad = grad_low.reshape(-1, grad_low.shape[-1])
    grad_weight = lax.dot_general(
        flat_left, flat_grad, (((0,), (0,)), ((), ())), preferred_element_type=jnp.float32
    )
    return (grad_left, grad_weight)


def split_heads(packed):
    heads_view = packed.reshape(packed.shape[0], packed.shape[1], 3, -1, HD).astype(jnp.bfloat16)
    return (heads_view[:, :, 0], heads_view[:, :, 1], heads_view[:, :, 2])


def attention_forward(packed):
    queries, keys_low, values_low = split_heads(packed)
    scores = (
        jnp.einsum("bqhd,bkhd->bhqk", queries, keys_low, preferred_element_type=jnp.float32)
        * SCORE_SCALE
    )
    top_score = jnp.max(scores, axis=-1, keepdims=True)
    log_total = top_score + jnp.log(jnp.sum(jnp.exp(scores - top_score), axis=-1, keepdims=True))
    attention = jnp.exp(scores - log_total).astype(jnp.bfloat16)
    attended = jnp.einsum(
        "bhqk,bkhd->bqhd", attention, values_low, preferred_element_type=jnp.float32
    )
    return (attended.reshape(packed.shape[0], packed.shape[1], -1).astype(jnp.bfloat16), log_total)


def attention_backward(grad_out, packed, log_total):
    queries, keys_low, values_low = split_heads(packed)
    grad_low = grad_out.reshape(packed.shape[0], packed.shape[1], -1, HD).astype(jnp.bfloat16)
    scores = (
        jnp.einsum("bqhd,bkhd->bhqk", queries, keys_low, preferred_element_type=jnp.float32)
        * SCORE_SCALE
    )
    attention = jnp.exp(scores - log_total)
    grad_attention = jnp.einsum(
        "bqhd,bkhd->bhqk", grad_low, values_low, preferred_element_type=jnp.float32
    )
    grad_values = jnp.einsum(
        "bhqk,bqhd->bkhd",
        attention.astype(jnp.bfloat16),
        grad_low,
        preferred_element_type=jnp.float32,
    )
    grad_scores = attention * (
        grad_attention - jnp.sum(attention * grad_attention, axis=-1, keepdims=True)
    )
    score_low = (grad_scores * SCORE_SCALE).astype(jnp.bfloat16)
    grad_queries = jnp.einsum(
        "bhqk,bkhd->bqhd", score_low, keys_low, preferred_element_type=jnp.float32
    )
    grad_keys = jnp.einsum(
        "bhqk,bqhd->bkhd", score_low, queries, preferred_element_type=jnp.float32
    )
    return jnp.stack([grad_queries, grad_keys, grad_values], axis=2).reshape(
        packed.shape[0], packed.shape[1], -1
    )


def layer_forward(hidden, cond_low, layer_low, layer_bias):
    weight_in, weight_down = layer_low
    weight_qkv, weight_proj, weight_up, weight_ada = cut_parts(weight_in, [3 * D, D, F, 6 * D])
    bias_qkv, bias_proj, bias_up, bias_ada, bias_down = cut_parts(
        layer_bias, [3 * D, D, F, 6 * D, D]
    )
    modulation = linear(cond_low, weight_ada) + bias_ada
    shift_one, scale_one, gate_one, shift_two, scale_two, gate_two = jnp.split(
        modulation, 6, axis=-1
    )
    normed_one = modulate(hidden, shift_one, scale_one).astype(jnp.bfloat16)
    packed = linear(normed_one, weight_qkv) + bias_qkv
    attended, log_total = attention_forward(packed)
    branch_one = linear(attended, weight_proj) + bias_proj
    middle = hidden + gate_one[:, None, :] * branch_one
    normed_two = modulate(middle, shift_two, scale_two).astype(jnp.bfloat16)
    pre_act = linear(normed_two, weight_up) + bias_up
    activated = gelu_tanh(pre_act).astype(jnp.bfloat16)
    branch_two = linear(activated, weight_down) + bias_down
    layer_cache = (
        modulation,
        normed_one,
        packed,
        attended,
        log_total,
        branch_one,
        middle,
        normed_two,
        pre_act,
        activated,
        branch_two,
    )
    return (middle + gate_two[:, None, :] * branch_two, layer_cache)


def layer_backward(grad_out, hidden, cond_low, layer_low, layer_cache):
    weight_in, weight_down = layer_low
    weight_qkv, weight_proj, weight_up, weight_ada = cut_parts(weight_in, [3 * D, D, F, 6 * D])
    (
        modulation,
        normed_one,
        packed,
        attended,
        log_total,
        branch_one,
        middle,
        normed_two,
        pre_act,
        activated,
        branch_two,
    ) = layer_cache
    shift_one, scale_one, gate_one, shift_two, scale_two, gate_two = jnp.split(
        modulation, 6, axis=-1
    )
    grad_gate_two = jnp.sum(grad_out * branch_two, axis=1)
    grad_branch_two = grad_out * gate_two[:, None, :]
    grad_activated, grad_weight_down = linear_back(grad_branch_two, activated, weight_down)
    grad_pre = jax.vjp(gelu_tanh, pre_act)[1](grad_activated)[0]
    grad_normed_two, grad_weight_up = linear_back(grad_pre, normed_two, weight_up)
    grad_middle, grad_shift_two, grad_scale_two = jax.vjp(modulate, middle, shift_two, scale_two)[
        1
    ](grad_normed_two)
    grad_middle = grad_middle + grad_out
    grad_gate_one = jnp.sum(grad_middle * branch_one, axis=1)
    grad_branch_one = grad_middle * gate_one[:, None, :]
    grad_attended, grad_weight_proj = linear_back(grad_branch_one, attended, weight_proj)
    grad_packed = attention_backward(grad_attended, packed, log_total)
    grad_normed_one, grad_weight_qkv = linear_back(grad_packed, normed_one, weight_qkv)
    grad_hidden, grad_shift_one, grad_scale_one = jax.vjp(modulate, hidden, shift_one, scale_one)[
        1
    ](grad_normed_one)
    grad_hidden = grad_hidden + grad_middle
    grad_modulation = jnp.concatenate(
        [
            grad_shift_one,
            grad_scale_one,
            grad_gate_one,
            grad_shift_two,
            grad_scale_two,
            grad_gate_two,
        ],
        axis=-1,
    )
    grad_cond, grad_weight_ada = linear_back(grad_modulation, cond_low, weight_ada)
    grad_in = jnp.concatenate(
        [grad_weight_qkv, grad_weight_proj, grad_weight_up, grad_weight_ada], axis=1
    )
    grad_bias = jnp.concatenate(
        [
            total_rows(grad_packed),
            total_rows(grad_branch_one),
            total_rows(grad_pre),
            total_rows(grad_modulation),
            total_rows(grad_branch_two),
        ]
    )
    return (grad_hidden, grad_cond, grad_in, grad_weight_down, grad_bias, grad_modulation)


def adafactor(weight, gradient, row_old, col_old, col_sum, row_sum, row_count):
    square = gradient * gradient + FACTOR_EPS
    row_new = DECAY_RATE * row_old + (1.0 - DECAY_RATE) * jnp.mean(square, axis=2)
    col_new = DECAY_RATE * col_old + (1.0 - DECAY_RATE) * (col_sum / row_count + FACTOR_EPS)
    estimate = row_new[:, :, None] * col_new[:, None, :] / (row_sum / row_count)[:, None, None]
    return (weight - LEARN_RATE * gradient * lax.rsqrt(estimate), row_new, col_new)


def new_row_sum(clip_grad, row_old):
    return jnp.sum(
        DECAY_RATE * row_old
        + (1.0 - DECAY_RATE) * (jnp.mean(clip_grad * clip_grad, axis=2) + FACTOR_EPS),
        axis=1,
    )


def body(
    latents,
    targets,
    features,
    time_weights,
    timesteps,
    classes,
    block_in,
    block_in_rows,
    block_in_cols,
    block_down,
    block_down_rows,
    block_down_cols,
    stem_main,
    stem_main_rows,
    stem_main_cols,
    stem_proj,
    stem_proj_rows,
    stem_proj_cols,
    head_weight,
    head_rows,
    head_cols,
    biases,
    bias_second,
):
    stem_low, proj_low, bias_low = (
        lax.all_gather(stem_main.astype(jnp.bfloat16), "fsdp", axis=0, tiled=True),
        lax.all_gather(stem_proj.astype(jnp.bfloat16), "fsdp", axis=0, tiled=True),
        lax.all_gather(biases.astype(jnp.bfloat16), "fsdp", axis=0, tiled=True),
    )
    bias_full = bias_low.astype(jnp.float32)
    block_bias = bias_full[: L * VB].reshape(L, VB)
    stem_bias = bias_full[L * VB :]
    time_out, final_ada, table_t, patch_t, proj_one, time_in = cut_parts(
        stem_low, [D, 2 * D, NCLS, PD, P_SIZE, TF]
    )
    proj_two, proj_three = cut_parts(proj_low, [P_SIZE, Z])
    bias_tin, bias_tout, bias_final, bias_patch, bias_one, bias_two, bias_three = cut_parts(
        stem_bias, [D, D, 2 * D, D, P_SIZE, P_SIZE, Z]
    )
    freq_low = time_freq(timesteps).astype(jnp.bfloat16)
    embed_hidden = (
        lax.dot_general(
            freq_low, time_in, (((1,), (1,)), ((), ())), preferred_element_type=jnp.float32
        )
        + bias_tin
    )
    embed_act = jax.nn.silu(embed_hidden).astype(jnp.bfloat16)
    one_hot = classes[:, None] == jnp.arange(NCLS)[None, :]
    class_embed = lax.dot_general(
        one_hot.astype(jnp.bfloat16),
        table_t,
        (((1,), (1,)), ((), ())),
        preferred_element_type=jnp.float32,
    )
    condition = linear(embed_act, time_out) + bias_tout + class_embed
    cond_low = jax.nn.silu(condition).astype(jnp.bfloat16)
    latent_low = latents.astype(jnp.bfloat16)
    hidden = (
        lax.dot_general(
            latent_low, patch_t, (((2,), (1,)), ((), ())), preferred_element_type=jnp.float32
        )
        + bias_patch
        + positions()
    )
    kept_layers = []
    inputs_seen = []
    saved_caches = []
    first_out = hidden
    for level_index in range(L):
        layer_low = (
            lax.all_gather(block_in[level_index].astype(jnp.bfloat16), "fsdp", axis=0, tiled=True),
            lax.all_gather(
                block_down[level_index].astype(jnp.bfloat16), "fsdp", axis=0, tiled=True
            ),
        )
        kept_layers.append(layer_low)
        inputs_seen.append(hidden)
        hidden, layer_cache = layer_forward(hidden, cond_low, layer_low, block_bias[level_index])
        saved_caches.append(layer_cache)
        if level_index == 0:
            first_out = hidden
    first_low = first_out.astype(jnp.bfloat16)
    proj_pre_one = linear(first_low, proj_one) + bias_one
    proj_act_one = jax.nn.silu(proj_pre_one).astype(jnp.bfloat16)
    proj_pre_two = linear(proj_act_one, proj_two) + bias_two
    proj_act_two = jax.nn.silu(proj_pre_two).astype(jnp.bfloat16)
    projected = linear(proj_act_two, proj_three) + bias_three
    cosine_part, cosine_pull = jax.vjp(lambda values: cosine_loss(values, features), projected)
    final_mods = linear(cond_low, final_ada) + bias_final
    shift_final, scale_final = jnp.split(final_mods, 2, axis=-1)
    final_normed, final_pull = jax.vjp(modulate, hidden, shift_final, scale_final)
    final_low = final_normed.astype(jnp.bfloat16)
    head_low = head_weight[:D].astype(jnp.bfloat16)
    output = linear(final_low, head_low) + head_weight[D]
    residual = output - targets
    local_loss = jnp.sum(time_weights * jnp.mean(residual * residual, axis=(1, 2))) + cosine_part
    grad_output = 2.0 / (TOK * PD) * time_weights[:, None, None] * residual
    grad_final, grad_head = linear_back(grad_output, final_low, head_low)
    grad_head_full = jnp.concatenate([grad_head, total_rows(grad_output)[None, :]], axis=0)
    head_sum, loss_total = lax.psum((grad_head_full, local_loss), "fsdp")
    grad_hidden, grad_shift_final, grad_scale_final = final_pull(grad_final)
    grad_final_mods = jnp.concatenate([grad_shift_final, grad_scale_final], axis=-1)
    grad_cond, grad_final_ada = linear_back(grad_final_mods, cond_low, final_ada)
    grad_projected = cosine_pull(jnp.float32(1.0))[0]
    grad_act_two, grad_proj_three = linear_back(grad_projected, proj_act_two, proj_three)
    grad_pre_two = silu_back(proj_pre_two, grad_act_two)
    grad_act_one, grad_proj_two = linear_back(grad_pre_two, proj_act_one, proj_two)
    grad_pre_one = silu_back(proj_pre_one, grad_act_one)
    grad_first, grad_proj_one = linear_back(grad_pre_one, first_low, proj_one)
    block_grads = [None] * L
    bias_grads = [None] * L
    for level_index in reversed(range(L)):
        layer_low = (
            lax.all_gather(block_in[level_index].astype(jnp.bfloat16), "fsdp", axis=0, tiled=True),
            lax.all_gather(
                block_down[level_index].astype(jnp.bfloat16), "fsdp", axis=0, tiled=True
            ),
        )
        if level_index == 0:
            grad_hidden = grad_hidden + grad_first
        grad_hidden, grad_cond_part, grad_in, grad_down, grad_bias, grad_modulation = (
            layer_backward(
                grad_hidden,
                inputs_seen[level_index],
                cond_low,
                layer_low,
                saved_caches[level_index],
            )
        )
        grad_cond = grad_cond + grad_cond_part
        block_grads[level_index] = (
            lax.psum_scatter(grad_in, "fsdp", scatter_dimension=0, tiled=True),
            lax.psum_scatter(grad_down, "fsdp", scatter_dimension=0, tiled=True),
        )
        bias_grads[level_index] = grad_bias
    grad_patch = lax.dot_general(
        grad_hidden.astype(jnp.bfloat16),
        latent_low,
        (((0, 1), (0, 1)), ((), ())),
        preferred_element_type=jnp.float32,
    )
    grad_condition = silu_back(condition, grad_cond)
    grad_table = lax.dot_general(
        grad_condition,
        one_hot.astype(jnp.float32),
        (((0,), (0,)), ((), ())),
        precision=lax.Precision.HIGHEST,
    )
    grad_embed_act, grad_time_out = linear_back(grad_condition, embed_act, time_out)
    grad_embed = silu_back(embed_hidden, grad_embed_act)
    grad_time_in = lax.dot_general(
        grad_embed.astype(jnp.bfloat16),
        freq_low,
        (((0,), (0,)), ((), ())),
        preferred_element_type=jnp.float32,
    )
    grad_proj = jnp.concatenate([grad_proj_two, grad_proj_three], axis=1)
    grad_bias_all = jnp.concatenate(
        bias_grads
        + [
            total_rows(grad_embed),
            total_rows(grad_condition),
            total_rows(grad_final_mods),
            total_rows(grad_hidden),
            total_rows(grad_pre_one),
            total_rows(grad_pre_two),
            total_rows(grad_projected),
        ]
    )
    grad_stem = jnp.concatenate(
        [grad_time_out, grad_final_ada, grad_table, grad_patch, grad_proj_one, grad_time_in], axis=1
    )
    stem_shard, proj_shard, bias_shard = (
        lax.psum_scatter(grad_stem, "fsdp", scatter_dimension=0, tiled=True),
        lax.psum_scatter(grad_proj, "fsdp", scatter_dimension=0, tiled=True),
        lax.psum_scatter(grad_bias_all, "fsdp", scatter_dimension=0, tiled=True),
    )
    raw_list = [
        jnp.stack([shard_pair[0] for shard_pair in block_grads]),
        jnp.stack([shard_pair[1] for shard_pair in block_grads]),
        stem_shard[None],
        proj_shard[None],
    ]
    weight_list = [block_in, block_down, stem_main[None], stem_proj[None]]
    row_list = [block_in_rows, block_down_rows, stem_main_rows[None], stem_proj_rows[None]]
    col_list = [block_in_cols, block_down_cols, stem_main_cols[None], stem_proj_cols[None]]
    count_list = [D, F, D, P_SIZE]
    local_square = jnp.sum(bias_shard * bias_shard)
    for raw_grad in raw_list:
        local_square = local_square + jnp.sum(raw_grad * raw_grad)
    head_square = jnp.sum(head_sum * head_sum)
    total_square = lax.psum(local_square, "fsdp") + head_square
    grad_norm = jnp.sqrt(total_square)
    clip_scale = jnp.minimum(1.0, CLIP_LIMIT / grad_norm)
    clipped = [clip_scale * raw_grad for raw_grad in raw_list]
    local_cols = tuple((jnp.sum(clip_grad * clip_grad, axis=1) for clip_grad in clipped))
    local_rows = tuple(
        (new_row_sum(clip_grad, row_old) for clip_grad, row_old in zip(clipped, row_list))
    )
    summed = lax.psum(local_cols + local_rows, "fsdp")
    col_sums = summed[:4]
    row_sums = summed[4:]
    results = []
    for slot in range(4):
        new_weight, row_new, col_new = adafactor(
            weight_list[slot],
            clipped[slot],
            row_list[slot],
            col_list[slot],
            col_sums[slot],
            row_sums[slot],
            count_list[slot],
        )
        results.append((new_weight, clipped[slot], row_new, col_new))
    new_in, clip_in, rows_in, cols_in = results[0]
    new_down, clip_down, rows_down, cols_down = results[1]
    new_main, clip_main, rows_main, cols_main = results[2]
    new_proj, clip_proj, rows_proj, cols_proj = results[3]
    head_clip = (clip_scale * head_sum)[None]
    head_col_sum = jnp.sum(head_clip * head_clip, axis=1)
    head_row_sum = new_row_sum(head_clip, head_rows[None])
    new_head, rows_head_new, cols_head_new = adafactor(
        head_weight[None],
        head_clip,
        head_rows[None],
        head_cols[None],
        head_col_sum,
        head_row_sum,
        D + 1,
    )
    clip_bias = clip_scale * bias_shard
    second_new = DECAY_RATE * bias_second + (1.0 - DECAY_RATE) * (
        clip_bias * clip_bias + FACTOR_EPS
    )
    new_bias = biases - LEARN_RATE * clip_bias * lax.rsqrt(second_new)
    return (
        loss_total,
        grad_norm,
        new_in,
        clip_in,
        rows_in,
        cols_in,
        new_in.astype(jnp.bfloat16),
        new_down,
        clip_down,
        rows_down,
        cols_down,
        new_down.astype(jnp.bfloat16),
        new_main[0],
        clip_main[0],
        rows_main[0],
        cols_main[0],
        new_main[0].astype(jnp.bfloat16),
        new_proj[0],
        clip_proj[0],
        rows_proj[0],
        cols_proj[0],
        new_proj[0].astype(jnp.bfloat16),
        new_head[0],
        head_clip[0],
        rows_head_new[0],
        cols_head_new[0],
        new_bias,
        clip_bias,
        second_new,
    )


def solution(mesh):
    return jax.shard_map(
        body,
        mesh=mesh,
        in_specs=(
            P("fsdp", None, None),
            P("fsdp", None, None),
            P("fsdp", None, None),
            P("fsdp"),
            P("fsdp"),
            P("fsdp"),
            P(None, "fsdp", None),
            P(None, "fsdp"),
            P(),
            P(None, "fsdp", None),
            P(None, "fsdp"),
            P(),
            P("fsdp", None),
            P("fsdp"),
            P(),
            P("fsdp", None),
            P("fsdp"),
            P(),
            P(),
            P(),
            P(),
            P("fsdp"),
            P("fsdp"),
        ),
        out_specs=(
            P(),
            P(),
            P(None, "fsdp", None),
            P(None, "fsdp", None),
            P(None, "fsdp"),
            P(),
            P(None, "fsdp", None),
            P(None, "fsdp", None),
            P(None, "fsdp", None),
            P(None, "fsdp"),
            P(),
            P(None, "fsdp", None),
            P("fsdp", None),
            P("fsdp", None),
            P("fsdp"),
            P(),
            P("fsdp", None),
            P("fsdp", None),
            P("fsdp", None),
            P("fsdp"),
            P(),
            P("fsdp", None),
            P(),
            P(),
            P(),
            P(),
            P("fsdp"),
            P("fsdp"),
            P("fsdp"),
        ),
        check_vma=False,
    )
```

profile of v0, /device:TPU:0, one launch (start us, length us, event | category | flops | bytes accessed | tf_op | source)
XLA Modules:
  0.0 2369.1 jit_solution(1973626769610962037)
XLA Ops:
  16.6 43.0 %all-reduce = bf16[31744]{0:T(1024)(128)(2,1)S(1)} all-reduce(bf16[31744]{0:T(1024)(128)(2,1)S(1)} %dynamic-update-slice), channel_id=1, replica_groups=mesh['fsdp'=32] {'fsdp'}, use_global_device_ids=true, to_apply=%add | all-reduce | flops 31744 | bytes 126976
  64.2 28.6 %all-gather.11.cloned.1.call-done = bf16[768,5625]{1,0:T(8,128)(2,1)} async-done(((bf16[24,5625]{1,0:T(8,128)(2,1)}), bf16[768,5625]{1,0:T(8,128)(2,1)}) %all-gather.11.cloned.1.call-update) | async-done | bytes 8640016 | tf_op jit(solution)/shard_map/all_gather | solution.py:302
  102.9 106.0 %all-gather.19.cloned.1.call-done = bf16[1,768,10752]{2,1,0:T(8,128)(2,1)} async-done(((bf16[1,24,10752]{2,1,0:T(8,128)(2,1)}), bf16[1,768,10752]{2,1,0:T(8,128)(2,1)}) %all-gather.19.cloned.1.call-update) | async-done | bytes 16515088 | tf_op jit(solution)/shard_map/all_gather | solution.py:347
  211.4 113.0 %all-gather.15.cloned.1.call-done = bf16[1,768,10752]{2,1,0:T(8,128)(2,1)} async-done(((bf16[1,24,10752]{2,1,0:T(8,128)(2,1)}), bf16[1,768,10752]{2,1,0:T(8,128)(2,1)}) %all-gather.15.cloned.1.call-update) | async-done | bytes 16515088 | tf_op jit(solution)/shard_map/all_gather | solution.py:347
  353.3 36.2 %all-gather.17.cloned.1.call-done = bf16[1,3072,768]{2,1,0:T(8,128)(2,1)} async-done(((bf16[1,96,768]{2,1,0:T(8,128)(2,1)}), bf16[1,3072,768]{2,1,0:T(8,128)(2,1)}) %all-gather.17.cloned.1.call-update) | async-done | bytes 4718608 | tf_op jit(solution)/shard_map/all_gather | solution.py:348
  417.6 37.7 %all-gather.21.cloned.1.call-done = bf16[1,3072,768]{2,1,0:T(8,128)(2,1)} async-done(((bf16[1,96,768]{2,1,0:T(8,128)(2,1)}), bf16[1,3072,768]{2,1,0:T(8,128)(2,1)}) %all-gather.21.cloned.1.call-update) | async-done | bytes 4718608 | tf_op jit(solution)/shard_map/all_gather | solution.py:348
  508.0 40.6 %all-gather.13.cloned.1.call-done = bf16[2048,2816]{1,0:T(8,128)(2,1)} async-done(((bf16[64,2816]{1,0:T(8,128)(2,1)}), bf16[2048,2816]{1,0:T(8,128)(2,1)}) %all-gather.13.cloned.1.call-update) | async-done | bytes 11534352 | tf_op jit(solution)/shard_map/all_gather | solution.py:303
  627.4 7.7 fusion.252
  636.3 7.8 fusion.203
  657.0 20.8 concatenate.74
  693.0 12.8 broadcast_multiply_fusion.1
  705.8 21.6 pad_maximum_fusion
  739.6 21.7 pad_maximum_fusion.1
  767.8 11.9 pad_maximum_fusion.2
  779.7 23.8 %copy.121 = f32[2048,2816]{1,0:T(8,128)} copy(f32[2048,2816]{0,1:T(8,128)} %pad_maximum_fusion.2) | data formatting | bytes 46137344
  809.2 79.7 %reduce-scatter.15.cloned.1.call-done = f32[96,768]{1,0:T(8,128)} async-done(((f32[3072,768]{1,0:T(8,128)}), f32[96,768]{1,0:T(8,128)}) %reduce-scatter.15.cloned.1.call-update) | async-done | bytes 294928 | tf_op jit(solution)/shard_map/reduce_scatter | solution.py:409
  888.9 141.5 %reduce-scatter.13.cloned.1.call-done = f32[96,768]{1,0:T(8,128)} async-done(((f32[3072,768]{1,0:T(8,128)}), f32[96,768]{1,0:T(8,128)}) %reduce-scatter.13.cloned.1.call-update) | async-done | bytes 294928 | tf_op jit(solution)/shard_map/reduce_scatter | solution.py:409
  1032.1 198.8 %reduce-scatter.17.cloned.1.call-done = f32[24,5625]{1,0:T(8,128)} async-done(((f32[768,5625]{1,0:T(8,128)}), f32[24,5625]{1,0:T(8,128)}) %reduce-scatter.17.cloned.1.call-update) | async-done | bytes 540016 | tf_op jit(solution)/shard_map/reduce_scatter | solution.py:450
  1232.7 322.0 %reduce-scatter.9.cloned.1.call-done = f32[24,10752]{1,0:T(8,128)} async-done(((f32[768,10752]{1,0:T(8,128)}), f32[24,10752]{1,0:T(8,128)}) %reduce-scatter.9.cloned.1.call-update) | async-done | bytes 1032208 | tf_op jit(solution)/shard_map/reduce_scatter | solution.py:408
  1554.7 324.4 %reduce-scatter.11.cloned.1.call-done = f32[24,10752]{1,0:T(8,128)} async-done(((f32[768,10752]{1,0:T(8,128)}), f32[24,10752]{1,0:T(8,128)}) %reduce-scatter.11.cloned.1.call-update) | async-done | bytes 1032208 | tf_op jit(solution)/shard_map/reduce_scatter | solution.py:408
  1884.3 243.0 %reduce-scatter.19.cloned.1.call-done = f32[64,2816]{1,0:T(8,128)} async-done(((f32[2048,2816]{1,0:T(8,128)}), f32[64,2816]{1,0:T(8,128)}) %reduce-scatter.19.cloned.1.call-update) | async-done | bytes 720912
  2130.5 45.4 %all-reduce.3 = (f32[]{:T(128)}, f32[769,16]{0,1:T(8,128)S(1)}) all-reduce(f32[]{:T(128)S(6)} %add.790, f32[769,16]{0,1:T(8,128)S(1)} %pad_maximum_fusion.7), channel_id=1, replica_groups=mesh['fsdp'=32] {'fsdp'}, use_global_device_ids=true, to_apply=%region_70.71 | all-reduce | flops 12305 | bytes 98440 | tf_op jit(solution)/shard_map/psum | solution.py:468
  2191.5 41.9 %all-reduce.2 = (f32[]{:T(128)}, f32[2]{0:T(128)}, f32[2]{0:T(128)}, f32[2,768]{1,0:T(2,128)}, f32[1]{0:T(128)}, /*index=5*/f32[1,5625]{1,0:T(1,128)}, f32[1]{0:T(128)}, f32[1,2816]{1,0:T(1,128)}) all-reduce(f32[]{:T(128)} %bitcast.25, f32[2]{0:T(128)} %get-tuple-element.269, ...), channel_id=1, replica_groups=mesh['fsdp'=32] {'fsdp'}, use_global_device_ids=true, to_apply=%region_19.20 | all-reduce | flops 9984 | bytes 79872 | tf_op jit(solution)/shard_map/psum | solution.py:376
  2255.7 100.2 %all-reduce.7.cloned.1.call-done = f32[2,10752]{1,0:T(2,128)} async-done(((f32[2,10752]{1,0:T(2,128)}), f32[2,10752]{1,0:T(2,128)}) %all-reduce.7.cloned.1.call-update) | async-done | bytes 86032 | tf_op jit(solution)/shard_map/psum | solution.py:476
  (685 shorter events, 311.1 us)
Async XLA Ops:
  7.2 85.7 %all-gather.11.cloned.1.call-start = ((), (), s32[]{:S(2)}) async-start(), calls=%async_computation.6 | async-start | bytes 8921088 | tf_op jit(solution)/shard_map/all_gather | solution.py:302
  9.1 199.9 %all-gather.19.cloned.1.call-start = ((), (), s32[]{:S(2)}) async-start(), calls=%async_computation.16 | async-start | bytes 17031168 | tf_op jit(solution)/shard_map/all_gather | solution.py:347
  11.9 312.4 %all-gather.15.cloned.1.call-start = ((), (), s32[]{:S(2)}) async-start(), calls=%async_computation.14 | async-start | bytes 17031168 | tf_op jit(solution)/shard_map/all_gather | solution.py:347
  12.7 376.8 %all-gather.17.cloned.1.call-start = ((), (), s32[]{:S(2)}) async-start(), calls=%async_computation.15 | async-start | bytes 4866048 | tf_op jit(solution)/shard_map/all_gather | solution.py:348
  13.5 441.8 %all-gather.21.cloned.1.call-start = ((), (), s32[]{:S(2)}) async-start(), calls=%async_computation.17 | async-start | bytes 4866048 | tf_op jit(solution)/shard_map/all_gather | solution.py:348
  14.1 534.5 %all-gather.13.cloned.1.call-start = ((), (), s32[]{:S(2)}) async-start(), calls=%async_computation.7 | async-start | bytes 11894784 | tf_op jit(solution)/shard_map/all_gather | solution.py:303
  15.0 792.8 %all-reduce.9.cloned.1.call-start = ((), (), s32[]{:S(2)}) async-start(), calls=%async_computation.19 | async-start | bytes 253952
  59.6 275.2 %copy-start.76 = (f32[31744]{0:T(1024)}, f32[31744]{0:T(1024)S(1)}, u32[]{:S(2)}) copy-start(f32[31744]{0:T(1024)S(1)} %convert_element_type.314) | copy-start | bytes 380932
  102.6 232.3 %copy-start.6 = (f32[256,768]{1,0:T(8,128)}, f32[256,768]{1,0:T(8,128)S(1)}, u32[]{:S(2)}) copy-start(f32[256,768]{1,0:T(8,128)S(1)} %get-tuple-element.277) | copy-start | bytes 2359300
  102.7 232.3 %copy-start.128 = (f32[256]{0:T(256)}, f32[256]{0:T(256)S(1)}, u32[]{:S(2)}) copy-start(f32[256]{0:T(256)S(1)} %broadcast_multiply_fusion.13) | copy-start | bytes 3076
  102.9 227.8 %copy-start.172 = (f32[256]{0:T(256)}, f32[256]{0:T(256)S(1)}, u32[]{:S(2)}) copy-start(f32[256]{0:T(256)S(1)} %multiply_reduce_fusion.30) | copy-start | bytes 3076
  102.9 232.0 %copy-start.154 = (f32[256]{0:T(256)}, f32[256]{0:T(256)S(1)}, u32[]{:S(2)}) copy-start(f32[256]{0:T(256)S(1)} %fusion.228) | copy-start | bytes 3076
  340.0 133.8 %copy-start.77 = (f32[768]{0:T(1024)}, f32[768]{0:T(1024)S(1)}, u32[]{:S(2)}) copy-start(f32[768]{0:T(1024)S(1)} %get-tuple-element.159) | copy-start | bytes 9220
  340.0 134.1 %copy-start.91 = (f32[768]{0:T(1024)}, f32[768]{0:T(1024)S(1)}, u32[]{:S(2)}) copy-start(f32[768]{0:T(1024)S(1)} %get-tuple-element.162) | copy-start | bytes 9220
  340.0 134.1 %copy-start.110 = (f32[768]{0:T(1024)}, f32[768]{0:T(1024)S(1)}, u32[]{:S(2)}) copy-start(f32[768]{0:T(1024)S(1)} %get-tuple-element.157) | copy-start | bytes 9220
  627.3 261.5 %reduce-scatter.15.cloned.1.call-start = ((), (), s32[]{:S(2)}) async-start(), calls=%async_computation.11 | async-start | bytes 9732096 | tf_op jit(solution)/shard_map/reduce_scatter | solution.py:409
  635.2 395.2 %reduce-scatter.13.cloned.1.call-start = ((), (), s32[]{:S(2)}) async-start(), calls=%async_computation.10 | async-start | bytes 9732096 | tf_op jit(solution)/shard_map/reduce_scatter | solution.py:409
  644.1 586.8 %reduce-scatter.17.cloned.1.call-start = ((), (), s32[]{:S(2)}) async-start(), calls=%async_computation.12 | async-start | bytes 17842176 | tf_op jit(solution)/shard_map/reduce_scatter | solution.py:450
  677.8 876.8 %reduce-scatter.9.cloned.1.call-start = ((), (), s32[]{:S(2)}) async-start(), calls=%async_computation.8 | async-start | bytes 34062336 | tf_op jit(solution)/shard_map/reduce_scatter | solution.py:408
  727.5 1151.5 %reduce-scatter.11.cloned.1.call-start = ((), (), s32[]{:S(2)}) async-start(), calls=%async_computation.9 | async-start | bytes 34062336 | tf_op jit(solution)/shard_map/reduce_scatter | solution.py:408
  761.3 1366.0 %reduce-scatter.19.cloned.1.call-start = ((), (), s32[]{:S(2)}) async-start(), calls=%async_computation.18 | async-start | bytes 23789568
  803.6 1552.2 %all-reduce.7.cloned.1.call-start = ((), (), s32[]{:S(2)}) async-start(), calls=%async_computation.13 | async-start | bytes 172032 | tf_op jit(solution)/shard_map/psum | solution.py:476
  1884.3 295.4 %copy-start.62 = (f32[96,768]{1,0:T(8,128)S(1)}, f32[96,768]{1,0:T(8,128)}, u32[]{:S(2)}) copy-start(f32[96,768]{1,0:T(8,128)} %reduce-scatter.15.cloned.1.call-done) | copy-start | bytes 884740
  1884.3 295.4 %copy-start.63 = (f32[96,768]{1,0:T(8,128)S(1)}, f32[96,768]{1,0:T(8,128)}, u32[]{:S(2)}) copy-start(f32[96,768]{1,0:T(8,128)} %reduce-scatter.13.cloned.1.call-done) | copy-start | bytes 884740
  (188 other events, 1721.5 us)
Sparse Core Ops, SparseCore 0:
  11.5 81.3 all-gather.10
  96.4 112.5 all-gather.18
  212.5 111.8 all-gather.14
  327.7 61.7 all-gather.16
  392.8 62.4 all-gather.20
  458.6 89.9 all-gather.12
  627.5 120.2 all-reduce.8
  753.6 135.1 reduce-scatter.14
  895.8 134.4 reduce-scatter.12
  1036.6 194.2 reduce-scatter.16
  1237.4 317.2 reduce-scatter.8
  1561.0 318.0 reduce-scatter.10
  1881.3 245.9 reduce-scatter.18
  2235.4 120.4 all-reduce.6
where the time goes:
time: 2380 us; the launch traced here: 2370 us
  waiting for transfers between devices  1770 us (74%)
  matrix products  215 us (9%)
  other arithmetic  142 us (6%)
  blocking collectives  130 us (5%)
  local copies, waits for them, and re-layouts  79.8 us (3%)
  between operations  28.1 us (1%)
    reduce_scatter x2, waiting for transfers between devices, body(): lax.psum_scatter(grad_in, 'fsdp', scatter_dimension=0, tiled=True)  646 us
    unnamed x16, waiting for transfers between devices  244 us
    reduce_scatter x2, waiting for transfers between devices, body(): lax.psum_scatter(grad_down, 'fsdp', scatter_dimension=0, tiled=True)  221 us
    all_gather x2, waiting for transfers between devices, body(): lax.all_gather(block_in[level_index].astype(jnp.bfloat16), 'fsdp', axis=0...  219 us
    reduce_scatter x1, waiting for transfers between devices, body(): lax.psum_scatter(grad_stem, 'fsdp', scatter_dimension=0, tiled=True)  199 us
    psum x1, waiting for transfers between devices, body(): summed = lax.psum(local_cols + local_rows, 'fsdp')  100 us
    all_gather x2, waiting for transfers between devices, body(): lax.all_gather(block_down[level_index].astype(jnp.bfloat16), 'fsdp', axis...  74 us
    dot_general x16, matrix products, linear(): return jnp.dot(left_side, weight_side, preferred_element_type=jnp.float32)  61.9 us
  transfers between devices with their start and end apart: 14, of which 13 were waited for; matrix products, arithmetic and copies ran while one was open for 14% of the time, Pallas kernels for 0%

commit v1 on v0

--- a/solution.py
+++ b/solution.py
@@ -1,3 +1,4 @@
+import functools
 import math
 
 import jax
@@ -102,7 +103,7 @@
     flat_grad = grad_low.reshape(-1, grad_low.shape[-1])
     grad_weight = lax.dot_general(
         flat_left, flat_grad, (((0,), (0,)), ((), ())), preferred_element_type=jnp.float32
-    )
+    ).astype(jnp.bfloat16)
     return (grad_left, grad_weight)
 
 
@@ -158,13 +159,10 @@
     )
 
 
-def layer_forward(hidden, cond_low, layer_low, layer_bias):
+def layer_forward(hidden, modulation, layer_low, layer_bias):
     weight_in, weight_down = layer_low
-    weight_qkv, weight_proj, weight_up, weight_ada = cut_parts(weight_in, [3 * D, D, F, 6 * D])
-    bias_qkv, bias_proj, bias_up, bias_ada, bias_down = cut_parts(
-        layer_bias, [3 * D, D, F, 6 * D, D]
-    )
-    modulation = linear(cond_low, weight_ada) + bias_ada
+    weight_qkv, weight_proj, weight_up = cut_parts(weight_in, [3 * D, D, F])
+    bias_qkv, bias_proj, bias_up, _, bias_down = cut_parts(layer_bias, [3 * D, D, F, 6 * D, D])
     shift_one, scale_one, gate_one, shift_two, scale_two, gate_two = jnp.split(
         modulation, 6, axis=-1
     )
@@ -193,9 +191,9 @@
     return (middle + gate_two[:, None, :] * branch_two, layer_cache)
 
 
-def layer_backward(grad_out, hidden, cond_low, layer_low, layer_cache):
+def layer_backward(grad_out, hidden, layer_low, layer_cache):
     weight_in, weight_down = layer_low
-    weight_qkv, weight_proj, weight_up, weight_ada = cut_parts(weight_in, [3 * D, D, F, 6 * D])
+    weight_qkv, weight_proj, weight_up = cut_parts(weight_in, [3 * D, D, F])
     (
         modulation,
         normed_one,
@@ -241,10 +239,6 @@
         ],
         axis=-1,
     )
-    grad_cond, grad_weight_ada = linear_back(grad_modulation, cond_low, weight_ada)
-    grad_in = jnp.concatenate(
-        [grad_weight_qkv, grad_weight_proj, grad_weight_up, grad_weight_ada], axis=1
-    )
     grad_bias = jnp.concatenate(
         [
             total_rows(grad_packed),
@@ -254,26 +248,103 @@
             total_rows(grad_branch_two),
         ]
     )
-    return (grad_hidden, grad_cond, grad_in, grad_weight_down, grad_bias, grad_modulation)
-
-
-def adafactor(weight, gradient, row_old, col_old, col_sum, row_sum, row_count):
-    square = gradient * gradient + FACTOR_EPS
-    row_new = DECAY_RATE * row_old + (1.0 - DECAY_RATE) * jnp.mean(square, axis=2)
-    col_new = DECAY_RATE * col_old + (1.0 - DECAY_RATE) * (col_sum / row_count + FACTOR_EPS)
-    estimate = row_new[:, :, None] * col_new[:, None, :] / (row_sum / row_count)[:, None, None]
-    return (weight - LEARN_RATE * gradient * lax.rsqrt(estimate), row_new, col_new)
-
-
-def new_row_sum(clip_grad, row_old):
-    return jnp.sum(
-        DECAY_RATE * row_old
-        + (1.0 - DECAY_RATE) * (jnp.mean(clip_grad * clip_grad, axis=2) + FACTOR_EPS),
-        axis=1,
-    )
+    weight_grads = (grad_weight_qkv, grad_weight_proj, grad_weight_up, grad_weight_down)
+    return (grad_hidden, weight_grads, grad_bias, grad_modulation)
+
+
+def swap(array, mask, count):
+    return lax.ppermute(array, "fsdp", [(place, place ^ mask) for place in range(count)])
+
+
+def bit_of(position, bit):
+    return (position >> bit) & 1
+
+
+def pick(array, bits, chosen):
+    sizes, starts, lengths = [], [], []
+    previous = None
+    for bit in bits:
+        fixed = bit in chosen
+        if fixed != previous:
+            sizes.append(1)
+            starts.append(0)
+            lengths.append(1)
+        sizes[-1] *= 2
+        if fixed:
+            starts[-1] = starts[-1] * 2 + chosen[bit]
+        else:
+            lengths[-1] *= 2
+        previous = fixed
+    tail = array.shape[1:]
+    view = array.reshape(tuple(sizes) + tail)
+    starts = [jnp.asarray(start, jnp.int32) for start in starts] + [jnp.int32(0)] * len(tail)
+    taken = lax.dynamic_slice(view, starts, tuple(lengths) + tail)
+    return taken.reshape((-1,) + tail)
+
+
+def scatter_sum(parts, bit_order, position, count, kind):
+    all_bits = list(reversed(range(count.bit_length() - 1)))
+    held = [(parts, all_bits)]
+    fixed = {}
+
+    def total(chosen):
+        summed = None
+        for arrays, bits in held:
+            wanted = {bit: value for bit, value in chosen.items() if bit in bits}
+            piece = [pick(array, bits, wanted).astype(jnp.float32) for array in arrays]
+            piece = piece[0] if len(piece) == 1 else jnp.concatenate(piece, axis=-1)
+            summed = piece if summed is None else summed + piece
+        return summed
+
+    for bit in bit_order:
+        mine = bit_of(position, bit)
+        sent = total({**fixed, bit: 1 - mine}).astype(kind)
+        received = swap(sent, 1 << bit, count)
+        fixed[bit] = mine
+        held.append(([received], [other for other in all_bits if other not in fixed]))
+    return total(fixed)[0]
+
+
+def gather_all(array, count):
+    blocks = array[None]
+    mask = 1
+    while mask < count:
+        blocks = jnp.concatenate([blocks, swap(blocks, mask, count)], axis=0)
+        mask *= 2
+    return blocks
+
+
+def sum_all(array, count):
+    mask = 1
+    while mask < count:
+        array = array + swap(array, mask, count)
+        mask *= 2
+    return array
+
+
+def split_high(values):
+    return (values // 32).astype(jnp.bfloat16), (values % 32).astype(jnp.bfloat16)
+
+
+def factored(weight, raw, row_old, col_old, row_square, col_square, row_old_sum, rows_all, clip):
+    columns = weight.shape[-1]
+    row_new = DECAY_RATE * row_old + (1.0 - DECAY_RATE) * (
+        clip * (clip * (row_square / columns)) + FACTOR_EPS
+    )
+    col_new = DECAY_RATE * col_old + (1.0 - DECAY_RATE) * (
+        clip * (clip * (col_square / rows_all)) + FACTOR_EPS
+    )
+    row_mean = (
+        DECAY_RATE * row_old_sum
+        + (1.0 - DECAY_RATE) * (clip * (clip * (jnp.sum(col_square) / columns)))
+    ) / rows_all + (1.0 - DECAY_RATE) * FACTOR_EPS
+    clipped = clip * raw
+    estimate = row_new[:, None] * col_new[None, :] / row_mean
+    return (weight - LEARN_RATE * clipped * lax.rsqrt(estimate), clipped, row_new, col_new)
 
 
 def body(
+    count,
     latents,
     targets,
     features,
@@ -298,22 +369,71 @@
     biases,
     bias_second,
 ):
-    stem_low, proj_low, bias_low = (
-        lax.all_gather(stem_main.astype(jnp.bfloat16), "fsdp", axis=0, tiled=True),
-        lax.all_gather(stem_proj.astype(jnp.bfloat16), "fsdp", axis=0, tiled=True),
-        lax.all_gather(biases.astype(jnp.bfloat16), "fsdp", axis=0, tiled=True),
-    )
-    bias_full = bias_low.astype(jnp.float32)
+    position = lax.axis_index("fsdp")
+    images = count * latents.shape[0]
+    width_rows = block_in.shape[1]
+    down_rows = block_down.shape[1]
+    proj_rows = stem_proj.shape[0]
+    bias_part = biases.shape[0]
+    bias_cols = -(-bias_part // width_rows)
+    bits = count.bit_length() - 1
+    deep_bits = list(reversed(range(3, bits)))
+    order_a = [bit for bit in (0, 1, 2) if bit < bits] + deep_bits
+    order_b = [bit for bit in (0, 2, 1) if bit < bits] + deep_bits
+    to_canonical = (
+        (jnp.arange(count)[:, None] ^ jnp.arange(count)[None, :]) == position
+    ).astype(jnp.bfloat16)
+
+    def gather_ordered(array):
+        blocks = gather_all(array, count)
+        flat = blocks.reshape(count, -1)
+        ordered = jnp.dot(to_canonical, flat, preferred_element_type=jnp.float32)
+        return ordered.astype(jnp.bfloat16).reshape(blocks.shape)
+
+    def bias_blocks(values):
+        return jnp.pad(values, ((0, 0), (0, width_rows * bias_cols - bias_part))).reshape(
+            values.shape[0], width_rows, bias_cols
+        )
+
+    time_out_part, final_ada_part, table_part, patch_part, proj_one_part, time_in_part = cut_parts(
+        stem_main, [D, 2 * D, NCLS, PD, P_SIZE, TF]
+    )
+    time_high, time_low = split_high(timesteps)
+    class_high, class_low = split_high(classes)
+    marks = jnp.stack([time_high, time_low, class_high, class_low], axis=1)
+    marks = jnp.broadcast_to(marks.reshape(1, 4), (width_rows, 4))
+    small_pack = jnp.concatenate(
+        [
+            time_out_part.astype(jnp.bfloat16),
+            time_in_part.astype(jnp.bfloat16),
+            table_part.astype(jnp.bfloat16),
+            patch_part.astype(jnp.bfloat16),
+            marks,
+            bias_blocks(biases[None])[0].astype(jnp.bfloat16),
+        ],
+        axis=1,
+    )
+    used = small_pack.shape[1]
+    small_pack = jnp.pad(small_pack, ((0, 0), (0, -used % 128)))
+    stem_low = lax.all_gather(small_pack, "fsdp", axis=0, tiled=True)
+    time_out, time_in, table_t, patch_t, mark_cols, bias_low, _ = cut_parts(
+        stem_low, [D, TF, NCLS, PD, 4, bias_cols, 0]
+    )
+    mark_all = mark_cols.reshape(count, width_rows, 4)[:, 0].astype(jnp.int32)
+    times_all = mark_all[:, 0] * 32 + mark_all[:, 1]
+    classes_all = mark_all[:, 2] * 32 + mark_all[:, 3]
+    bias_full = (
+        bias_low.reshape(count, width_rows * bias_cols)[:, :bias_part]
+        .reshape(-1)
+        .astype(jnp.float32)
+    )
     block_bias = bias_full[: L * VB].reshape(L, VB)
     stem_bias = bias_full[L * VB :]
-    time_out, final_ada, table_t, patch_t, proj_one, time_in = cut_parts(
-        stem_low, [D, 2 * D, NCLS, PD, P_SIZE, TF]
-    )
-    proj_two, proj_three = cut_parts(proj_low, [P_SIZE, Z])
     bias_tin, bias_tout, bias_final, bias_patch, bias_one, bias_two, bias_three = cut_parts(
         stem_bias, [D, D, 2 * D, D, P_SIZE, P_SIZE, Z]
     )
-    freq_low = time_freq(timesteps).astype(jnp.bfloat16)
+
+    freq_low = time_freq(times_all).astype(jnp.bfloat16)
     embed_hidden = (
         lax.dot_general(
             freq_low, time_in, (((1,), (1,)), ((), ())), preferred_element_type=jnp.float32
@@ -321,7 +441,7 @@
         + bias_tin
     )
     embed_act = jax.nn.silu(embed_hidden).astype(jnp.bfloat16)
-    one_hot = classes[:, None] == jnp.arange(NCLS)[None, :]
+    one_hot = classes_all[:, None] == jnp.arange(NCLS)[None, :]
     class_embed = lax.dot_general(
         one_hot.astype(jnp.bfloat16),
         table_t,
@@ -330,6 +450,22 @@
     )
     condition = linear(embed_act, time_out) + bias_tout + class_embed
     cond_low = jax.nn.silu(condition).astype(jnp.bfloat16)
+
+    def my_columns(values):
+        return lax.dynamic_slice_in_dim(values, position * width_rows, width_rows, axis=1)
+
+    cond_mine = my_columns(cond_low)
+    ada_mine = jnp.concatenate(
+        [block_in[level, :, 3 * D + D + F :] for level in range(L)] + [final_ada_part], axis=1
+    ).astype(jnp.bfloat16)
+    mod_part = linear(cond_mine, ada_mine)[:, None, :]
+    mods = scatter_sum([mod_part], order_a, position, count, jnp.float32)
+    bias_ada = jnp.concatenate(
+        [block_bias[level, 3 * D + D + F : 3 * D + D + F + 6 * D] for level in range(L)]
+        + [bias_final]
+    )
+    mods = mods + bias_ada[None, :]
+
     latent_low = latents.astype(jnp.bfloat16)
     hidden = (
         lax.dot_general(
@@ -338,22 +474,30 @@
         + bias_patch
         + positions()
     )
-    kept_layers = []
+    main_width = 3 * D + D + F
+    layers_low = [
+        (
+            lax.all_gather(
+                block_in[level, :, :main_width].astype(jnp.bfloat16), "fsdp", axis=0, tiled=True
+            ),
+            lax.all_gather(block_down[level].astype(jnp.bfloat16), "fsdp", axis=0, tiled=True),
+        )
+        for level in range(L)
+    ]
+    proj_one = lax.all_gather(proj_one_part.astype(jnp.bfloat16), "fsdp", axis=0, tiled=True)
+    proj_low = lax.all_gather(stem_proj.astype(jnp.bfloat16), "fsdp", axis=0, tiled=True)
+    proj_two, proj_three = cut_parts(proj_low, [P_SIZE, Z])
     inputs_seen = []
     saved_caches = []
     first_out = hidden
-    for level_index in range(L):
-        layer_low = (
-            lax.all_gather(block_in[level_index].astype(jnp.bfloat16), "fsdp", axis=0, tiled=True),
-            lax.all_gather(
-                block_down[level_index].astype(jnp.bfloat16), "fsdp", axis=0, tiled=True
-            ),
+    for level in range(L):
+        inputs_seen.append(hidden)
+        modulation = mods[:, level * 6 * D : (level + 1) * 6 * D]
+        hidden, layer_cache = layer_forward(
+            hidden, modulation, layers_low[level], block_bias[level]
         )
-        kept_layers.append(layer_low)
-        inputs_seen.append(hidden)
-        hidden, layer_cache = layer_forward(hidden, cond_low, layer_low, block_bias[level_index])
         saved_caches.append(layer_cache)
-        if level_index == 0:
+        if level == 0:
             first_out = hidden
     first_low = first_out.astype(jnp.bfloat16)
     proj_pre_one = linear(first_low, proj_one) + bias_one
@@ -362,8 +506,7 @@
     proj_act_two = jax.nn.silu(proj_pre_two).astype(jnp.bfloat16)
     projected = linear(proj_act_two, proj_three) + bias_three
     cosine_part, cosine_pull = jax.vjp(lambda values: cosine_loss(values, features), projected)
-    final_mods = linear(cond_low, final_ada) + bias_final
-    shift_final, scale_final = jnp.split(final_mods, 2, axis=-1)
+    shift_final, scale_final = jnp.split(mods[:, L * 6 * D :], 2, axis=-1)
     final_normed, final_pull = jax.vjp(modulate, hidden, shift_final, scale_final)
     final_low = final_normed.astype(jnp.bfloat16)
     head_low = head_weight[:D].astype(jnp.bfloat16)
@@ -371,71 +514,56 @@
     residual = output - targets
     local_loss = jnp.sum(time_weights * jnp.mean(residual * residual, axis=(1, 2))) + cosine_part
     grad_output = 2.0 / (TOK * PD) * time_weights[:, None, None] * residual
-    grad_final, grad_head = linear_back(grad_output, final_low, head_low)
+    grad_output_low = grad_output.astype(jnp.bfloat16)
+    grad_final = lax.dot_general(
+        grad_output_low, head_low, (((2,), (1,)), ((), ())), preferred_element_type=jnp.float32
+    )
+    grad_head = lax.dot_general(
+        final_low,
+        grad_output_low,
+        (((0, 1), (0, 1)), ((), ())),
+        preferred_element_type=jnp.float32,
+    )
     grad_head_full = jnp.concatenate([grad_head, total_rows(grad_output)[None, :]], axis=0)
-    head_sum, loss_total = lax.psum((grad_head_full, local_loss), "fsdp")
     grad_hidden, grad_shift_final, grad_scale_final = final_pull(grad_final)
     grad_final_mods = jnp.concatenate([grad_shift_final, grad_scale_final], axis=-1)
-    grad_cond, grad_final_ada = linear_back(grad_final_mods, cond_low, final_ada)
+
     grad_projected = cosine_pull(jnp.float32(1.0))[0]
     grad_act_two, grad_proj_three = linear_back(grad_projected, proj_act_two, proj_three)
     grad_pre_two = silu_back(proj_pre_two, grad_act_two)
     grad_act_one, grad_proj_two = linear_back(grad_pre_two, proj_act_one, proj_two)
     grad_pre_one = silu_back(proj_pre_one, grad_act_one)
     grad_first, grad_proj_one = linear_back(grad_pre_one, first_low, proj_one)
-    block_grads = [None] * L
+
+    def by_owner(values):
+        return values.reshape(count, -1, values.shape[-1])
+
+    def summed(parts, order):
+        return scatter_sum([by_owner(part) for part in parts], order, position, count, jnp.bfloat16)
+
     bias_grads = [None] * L
-    for level_index in reversed(range(L)):
-        layer_low = (
-            lax.all_gather(block_in[level_index].astype(jnp.bfloat16), "fsdp", axis=0, tiled=True),
-            lax.all_gather(
-                block_down[level_index].astype(jnp.bfloat16), "fsdp", axis=0, tiled=True
-            ),
-        )
-        if level_index == 0:
-            grad_hidden = grad_hidden + grad_first
-        grad_hidden, grad_cond_part, grad_in, grad_down, grad_bias, grad_modulation = (
-            layer_backward(
-                grad_hidden,
-                inputs_seen[level_index],
-                cond_low,
-                layer_low,
-                saved_caches[level_index],
-            )
-        )
-        grad_cond = grad_cond + grad_cond_part
-        block_grads[level_index] = (
-            lax.psum_scatter(grad_in, "fsdp", scatter_dimension=0, tiled=True),
-            lax.psum_scatter(grad_down, "fsdp", scatter_dimension=0, tiled=True),
-        )
-        bias_grads[level_index] = grad_bias
+    mod_grads = [None] * L
+    grad_hidden, weight_grads, bias_grads[1], mod_grads[1] = layer_backward(
+        grad_hidden, inputs_seen[1], layers_low[1], saved_caches[1]
+    )
+    down_one = summed(weight_grads[3:], order_a)
+    in_one = summed(list(weight_grads[:3]) + [grad_proj_one], order_b)
+    proj_shard = summed([grad_proj_two, grad_proj_three], order_a)
+    grad_hidden, weight_grads, bias_grads[0], mod_grads[0] = layer_backward(
+        grad_hidden + grad_first, inputs_seen[0], layers_low[0], saved_caches[0]
+    )
+    down_zero = summed(weight_grads[3:], order_b)
+    late_zero = summed(weight_grads[1:3], order_a)
     grad_patch = lax.dot_general(
         grad_hidden.astype(jnp.bfloat16),
         latent_low,
         (((0, 1), (0, 1)), ((), ())),
         preferred_element_type=jnp.float32,
     )
-    grad_condition = silu_back(condition, grad_cond)
-    grad_table = lax.dot_general(
-        grad_condition,
-        one_hot.astype(jnp.float32),
-        (((0,), (0,)), ((), ())),
-        precision=lax.Precision.HIGHEST,
-    )
-    grad_embed_act, grad_time_out = linear_back(grad_condition, embed_act, time_out)
-    grad_embed = silu_back(embed_hidden, grad_embed_act)
-    grad_time_in = lax.dot_general(
-        grad_embed.astype(jnp.bfloat16),
-        freq_low,
-        (((0,), (0,)), ((), ())),
-        preferred_element_type=jnp.float32,
-    )
-    grad_proj = jnp.concatenate([grad_proj_two, grad_proj_three], axis=1)
     grad_bias_all = jnp.concatenate(
         bias_grads
         + [
-            total_rows(grad_embed),
-            total_rows(grad_condition),
+            jnp.zeros((2 * D,), jnp.float32),
             total_rows(grad_final_mods),
             total_rows(grad_hidden),
             total_rows(grad_pre_one),
@@ -443,68 +571,168 @@
             total_rows(grad_projected),
         ]
     )
-    grad_stem = jnp.concatenate(
-        [grad_time_out, grad_final_ada, grad_table, grad_patch, grad_proj_one, grad_time_in], axis=1
-    )
-    stem_shard, proj_shard, bias_shard = (
-        lax.psum_scatter(grad_stem, "fsdp", scatter_dimension=0, tiled=True),
-        lax.psum_scatter(grad_proj, "fsdp", scatter_dimension=0, tiled=True),
-        lax.psum_scatter(grad_bias_all, "fsdp", scatter_dimension=0, tiled=True),
-    )
-    raw_list = [
-        jnp.stack([shard_pair[0] for shard_pair in block_grads]),
-        jnp.stack([shard_pair[1] for shard_pair in block_grads]),
-        stem_shard[None],
-        proj_shard[None],
+    bias_piece = bias_blocks(grad_bias_all.reshape(count, bias_part))
+    extra = PD + bias_cols
+    last_piece = jnp.concatenate(
+        [
+            by_owner(grad_patch.astype(jnp.bfloat16)),
+            bias_piece.astype(jnp.bfloat16),
+            jnp.zeros((count, width_rows, -extra % 128), jnp.bfloat16),
+        ],
+        axis=-1,
+    )
+    last_zero = scatter_sum(
+        [by_owner(weight_grads[0]), last_piece], order_b, position, count, jnp.bfloat16
+    )
+    patch_shard = last_zero[:, 3 * D : 3 * D + PD]
+    bias_shard = last_zero[:, 3 * D + PD : 3 * D + extra].reshape(-1)[:bias_part]
+
+    grad_mods = jnp.concatenate(mod_grads + [grad_final_mods], axis=-1).astype(jnp.bfloat16)
+    grad_mods_all = gather_ordered(grad_mods[0])
+    grad_ada_mine = lax.dot_general(
+        cond_mine, grad_mods_all, (((0,), (0,)), ((), ())), preferred_element_type=jnp.float32
+    )
+    grad_cond_mine = lax.dot_general(
+        grad_mods_all, ada_mine, (((1,), (1,)), ((), ())), preferred_element_type=jnp.float32
+    )
+    grad_condition = silu_back(my_columns(condition), grad_cond_mine)
+    grad_table = lax.dot_general(
+        grad_condition,
+        one_hot.astype(jnp.float32),
+        (((0,), (0,)), ((), ())),
+        precision=lax.Precision.HIGHEST,
+    )
+    grad_condition_low = gather_ordered(grad_condition.astype(jnp.bfloat16))
+    grad_condition_low = jnp.transpose(grad_condition_low, (1, 0, 2)).reshape(images, D)
+    grad_time_out = lax.dot_general(
+        my_columns(embed_act),
+        grad_condition_low,
+        (((0,), (0,)), ((), ())),
+        preferred_element_type=jnp.float32,
+    )
+    grad_embed_act = lax.dot_general(
+        grad_condition_low,
+        time_out_part.astype(jnp.bfloat16),
+        (((1,), (1,)), ((), ())),
+        preferred_element_type=jnp.float32,
+    )
+    grad_embed = silu_back(my_columns(embed_hidden), grad_embed_act)
+    grad_time_in = lax.dot_general(
+        grad_embed.astype(jnp.bfloat16),
+        freq_low,
+        (((0,), (0,)), ((), ())),
+        preferred_element_type=jnp.float32,
+    )
+    late_bias = jnp.zeros((2, D), jnp.float32)
+    late_bias = lax.dynamic_update_slice(
+        late_bias,
+        jnp.stack([jnp.sum(grad_embed, axis=0), jnp.sum(grad_condition, axis=0)]),
+        (0, position * width_rows),
+    )
+
+    ada_zero, ada_one, grad_final_ada = cut_parts(grad_ada_mine, [6 * D, 6 * D, 2 * D])
+    raw_in = jnp.stack(
+        [
+            jnp.concatenate([last_zero[:, : 3 * D], late_zero, ada_zero], axis=1),
+            jnp.concatenate([in_one[:, :main_width], ada_one], axis=1),
+        ]
+    )
+    raw_down = jnp.stack([down_zero, down_one])
+    raw_main = jnp.concatenate(
+        [
+            grad_time_out,
+            grad_final_ada,
+            grad_table,
+            patch_shard,
+            in_one[:, main_width:],
+            grad_time_in,
+        ],
+        axis=1,
+    )
+    raw_proj = proj_shard
+    raws = [raw_in[0], raw_in[1], raw_down[0], raw_down[1], raw_main, raw_proj]
+    row_olds = [
+        block_in_rows[0],
+        block_in_rows[1],
+        block_down_rows[0],
+        block_down_rows[1],
+        stem_main_rows,
+        stem_proj_rows,
     ]
-    weight_list = [block_in, block_down, stem_main[None], stem_proj[None]]
-    row_list = [block_in_rows, block_down_rows, stem_main_rows[None], stem_proj_rows[None]]
-    col_list = [block_in_cols, block_down_cols, stem_main_cols[None], stem_proj_cols[None]]
-    count_list = [D, F, D, P_SIZE]
-    local_square = jnp.sum(bias_shard * bias_shard)
-    for raw_grad in raw_list:
-        local_square = local_square + jnp.sum(raw_grad * raw_grad)
-    head_square = jnp.sum(head_sum * head_sum)
-    total_square = lax.psum(local_square, "fsdp") + head_square
+    squares = [raw * raw for raw in raws]
+    row_squares = [jnp.sum(square, axis=1) for square in squares]
+    late_list = [jnp.sum(square, axis=0) for square in squares] + [
+        jnp.stack([jnp.sum(row_old) for row_old in row_olds]),
+        jnp.stack([jnp.sum(bias_shard * bias_shard), local_loss]),
+        late_bias.reshape(-1),
+        grad_head_full.reshape(-1),
+    ]
+    late_sizes = [values.shape[0] for values in late_list]
+    late_all = jnp.concatenate(late_list)
+    late_all = jnp.pad(late_all, (0, -late_all.shape[0] % 1024)).reshape(-1, 128)
+    late_all = sum_all(late_all, count).reshape(-1)
+    late_sums = []
+    running = 0
+    for size in late_sizes:
+        late_sums.append(late_all[running : running + size])
+        running += size
+    col_squares = late_sums[:6]
+    row_old_sums, bias_loss, late_bias, head_sum = late_sums[6:]
+    head_sum = head_sum.reshape(D + 1, PD)
+    loss_total = bias_loss[1]
+    total_square = bias_loss[0] + jnp.sum(late_bias * late_bias) + jnp.sum(head_sum * head_sum)
+    for col_square in col_squares:
+        total_square = total_square + jnp.sum(col_square)
     grad_norm = jnp.sqrt(total_square)
-    clip_scale = jnp.minimum(1.0, CLIP_LIMIT / grad_norm)
-    clipped = [clip_scale * raw_grad for raw_grad in raw_list]
-    local_cols = tuple((jnp.sum(clip_grad * clip_grad, axis=1) for clip_grad in clipped))
-    local_rows = tuple(
-        (new_row_sum(clip_grad, row_old) for clip_grad, row_old in zip(clipped, row_list))
-    )
-    summed = lax.psum(local_cols + local_rows, "fsdp")
-    col_sums = summed[:4]
-    row_sums = summed[4:]
-    results = []
-    for slot in range(4):
-        new_weight, row_new, col_new = adafactor(
-            weight_list[slot],
-            clipped[slot],
-            row_list[slot],
-            col_list[slot],
-            col_sums[slot],
-            row_sums[slot],
-            count_list[slot],
+    clip = jnp.minimum(1.0, CLIP_LIMIT / grad_norm)
+
+    weights = [block_in[0], block_in[1], block_down[0], block_down[1], stem_main, stem_proj]
+    col_olds = [
+        block_in_cols[0],
+        block_in_cols[1],
+        block_down_cols[0],
+        block_down_cols[1],
+        stem_main_cols,
+        stem_proj_cols,
+    ]
+    results = [
+        factored(
+            weights[slot],
+            raws[slot],
+            row_olds[slot],
+            col_olds[slot],
+            row_squares[slot],
+            col_squares[slot],
+            row_old_sums[slot],
+            count * weights[slot].shape[0],
+            clip,
         )
-        results.append((new_weight, clipped[slot], row_new, col_new))
-    new_in, clip_in, rows_in, cols_in = results[0]
-    new_down, clip_down, rows_down, cols_down = results[1]
-    new_main, clip_main, rows_main, cols_main = results[2]
-    new_proj, clip_proj, rows_proj, cols_proj = results[3]
-    head_clip = (clip_scale * head_sum)[None]
-    head_col_sum = jnp.sum(head_clip * head_clip, axis=1)
-    head_row_sum = new_row_sum(head_clip, head_rows[None])
-    new_head, rows_head_new, cols_head_new = adafactor(
-        head_weight[None],
-        head_clip,
-        head_rows[None],
-        head_cols[None],
-        head_col_sum,
-        head_row_sum,
+        for slot in range(6)
+    ]
+    new_in, clip_in, rows_in, cols_in = [
+        jnp.stack([results[0][part], results[1][part]]) for part in range(4)
+    ]
+    new_down, clip_down, rows_down, cols_down = [
+        jnp.stack([results[2][part], results[3][part]]) for part in range(4)
+    ]
+    new_main, clip_main, rows_main, cols_main = results[4]
+    new_proj, clip_proj, rows_proj, cols_proj = results[5]
+    head_square = head_sum * head_sum
+    new_head, head_clip, rows_head, cols_head = factored(
+        head_weight,
+        head_sum,
+        head_rows,
+        head_cols,
+        jnp.sum(head_square, axis=1),
+        jnp.sum(head_square, axis=0),
+        jnp.sum(head_rows),
         D + 1,
-    )
-    clip_bias = clip_scale * bias_shard
+        clip,
+    )
+    late_flat = jnp.zeros((count * bias_part,), jnp.float32)
+    late_flat = lax.dynamic_update_slice(late_flat, late_bias, (L * VB,))
+    bias_raw = bias_shard + lax.dynamic_slice(late_flat, (position * bias_part,), (bias_part,))
+    clip_bias = clip * bias_raw
     second_new = DECAY_RATE * bias_second + (1.0 - DECAY_RATE) * (
         clip_bias * clip_bias + FACTOR_EPS
     )
@@ -522,20 +750,20 @@
         rows_down,
         cols_down,
         new_down.astype(jnp.bfloat16),
-        new_main[0],
-        clip_main[0],
-        rows_main[0],
-        cols_main[0],
-        new_main[0].astype(jnp.bfloat16),
-        new_proj[0],
-        clip_proj[0],
-        rows_proj[0],
-        cols_proj[0],
-        new_proj[0].astype(jnp.bfloat16),
-        new_head[0],
-        head_clip[0],
-        rows_head_new[0],
-        cols_head_new[0],
+        new_main,
+        clip_main,
+        rows_main,
+        cols_main,
+        new_main.astype(jnp.bfloat16),
+        new_proj,
+        clip_proj,
+        rows_proj,
+        cols_proj,
+        new_proj.astype(jnp.bfloat16),
+        new_head,
+        head_clip,
+        rows_head,
+        cols_head,
         new_bias,
         clip_bias,
         second_new,
@@ -544,7 +772,7 @@
 
 def solution(mesh):
     return jax.shard_map(
-        body,
+        functools.partial(body, mesh.shape["fsdp"]),
         mesh=mesh,
         in_specs=(
             P("fsdp", None, None),

time: 2380 us -> 1170 us (0.49)
  waiting for transfers between devices: 1770 us -> 594 us
  blocking collectives: 130 us -> 0 us
  local copies, waits for them, and re-layouts: 79.8 us -> 153 us
  starting transfers between devices: 1.19 us -> 32.2 us
  matrix products: 215 us -> 186 us
    reduce_scatter x5 -> x0, waiting for transfers between devices: 1070 us -> none  [the longest x2 646 us: body(): lax.psum_scatter(grad_in, 'fsdp', scatter_dimension=0, tiled=True)]
    ppermute x0 -> x50, waiting for transfers between devices: none -> 328 us  [swap(): lax.ppermute(array, 'fsdp', [(place, place ^ mask) for place in range(cou...]
    unnamed x16 -> x7, waiting for transfers between devices: 244 us -> 1.3 us
    psum x1 -> x0, waiting for transfers between devices: 100 us -> none  [body(): summed = lax.psum(local_cols + local_rows, 'fsdp')]
    psum x2 -> x0, blocking collectives: 87.3 us -> none  [the longest x1 45.4 us: body(): total_square = lax.psum(local_square, 'fsdp') + head_square]
    all_gather x5 -> x6, waiting for transfers between devices: 322 us -> 247 us  [the longest x2 109 us: body(): lax.all_gather(block_in[level, :, :main_width].astype(jnp.bfloat16), 'fsd...]
    convert_element_type x5 -> x31, other arithmetic: 5.88 us -> 50.5 us  [the longest x24 46.9 us: scatter_sum(): sent = total({**fixed, bit: 1 - mine}).astype(kind)]
    unnamed x1 -> x0, blocking collectives: 43 us -> none
  transfers between devices with their start and end apart: 14 -> 57, of which waited for: 13 -> 37; matrix products, arithmetic and copies ran while one was open for 14% -> 38% of each run, Pallas kernels for 0% -> 0%
where the time goes in v1:
time: 1170 us; the launch traced here: 1160 us
  waiting for transfers between devices  594 us (51%)
  matrix products  186 us (16%)
  local copies, waits for them, and re-layouts  153 us (13%)
  other arithmetic  153 us (13%)
  between operations  38.1 us (3%)
  starting transfers between devices  32.2 us (3%)
    ppermute x50, waiting for transfers between devices, swap(): lax.ppermute(array, 'fsdp', [(place, place ^ mask) for place in range(cou...  328 us
    all_gather x2, waiting for transfers between devices, body(): lax.all_gather(block_in[level, :, :main_width].astype(jnp.bfloat16), 'fsd...  109 us
    all_gather x2, waiting for transfers between devices, body(): lax.all_gather(block_down[level].astype(jnp.bfloat16), 'fsdp', axis=0, ti...  89.4 us
    dot_general x14, matrix products, linear(): return jnp.dot(left_side, weight_side, preferred_element_type=jnp.float32)  52.6 us
    all_gather x1, waiting for transfers between devices, body(): stem_low = lax.all_gather(small_pack, 'fsdp', axis=0, tiled=True)  48.4 us
    convert_element_type x24, other arithmetic, scatter_sum(): sent = total({**fixed, bit: 1 - mine}).astype(kind)  46.9 us
    dot_general x11, matrix products, linear_back(): lax.dot_general(grad_low, weight_side, (((grad_low.ndim - 1,), (1,)), (()...  38.9 us
    dot_general x11, matrix products, linear_back(): lax.dot_general(flat_left, flat_grad, (((0,), (0,)), ((), ())), preferred...  33.3 us
  transfers between devices with their start and end apart: 57, of which 37 were waited for; matrix products, arithmetic and copies ran while one was open for 38% of the time, Pallas kernels for 0%

profile of v1, /device:TPU:0, one launch (start us, length us, event | category | flops | bytes accessed | tf_op | source)
XLA Modules:
  0.0 1156.0 jit_solution(10967046720136874194)
XLA Ops:
  25.7 48.4 %all-gather.12.cloned.1.call-done = bf16[768,2176]{1,0:T(8,128)(2,1)} async-done(((bf16[24,2176]{1,0:T(8,128)(2,1)}), bf16[768,2176]{1,0:T(8,128)(2,1)}) %all-gather.12.cloned.1.call-update) | async-done | bytes 3342352 | tf_op jit(solution)/shard_map/all_gather | solution.py:418
  104.8 8.5 collective-permute-done.2
  114.1 10.2 collective-permute-done.3
  129.3 31.8 %all-gather.18.cloned.1.call-done = bf16[1,768,6144]{2,1,0:T(8,128)(2,1)} async-done(((bf16[1,24,6144]{2,1,0:T(8,128)(2,1)}), bf16[1,768,6144]{2,1,0:T(8,128)(2,1)}) %all-gather.18.cloned.1.call-update) | async-done | bytes 9437200 | tf_op jit(solution)/shard_map/all_gather | solution.py:480
  167.8 77.5 %all-gather.22.cloned.1.call-done = bf16[1,768,6144]{2,1,0:T(8,128)(2,1)} async-done(((bf16[1,24,6144]{2,1,0:T(8,128)(2,1)}), bf16[1,768,6144]{2,1,0:T(8,128)(2,1)}) %all-gather.22.cloned.1.call-update) | async-done | bytes 9437200 | tf_op jit(solution)/shard_map/all_gather | solution.py:480
  257.8 53.0 %all-gather.20.cloned.1.call-done = bf16[1,3072,768]{2,1,0:T(8,128)(2,1)} async-done(((bf16[1,96,768]{2,1,0:T(8,128)(2,1)}), bf16[1,3072,768]{2,1,0:T(8,128)(2,1)}) %all-gather.20.cloned.1.call-update) | async-done | bytes 4718608 | tf_op jit(solution)/shard_map/all_gather | solution.py:483
  310.8 6.8 fusion.307
  339.7 36.3 %all-gather.24.cloned.1.call-done = bf16[1,3072,768]{2,1,0:T(8,128)(2,1)} async-done(((bf16[1,96,768]{2,1,0:T(8,128)(2,1)}), bf16[1,3072,768]{2,1,0:T(8,128)(2,1)}) %all-gather.24.cloned.1.call-update) | async-done | bytes 4718608 | tf_op jit(solution)/shard_map/all_gather | solution.py:483
  418.9 7.6 fusion.113
  426.6 7.3 fusion.116
  500.0 22.9 %collective-permute-done.31 = bf16[8,96,768]{2,1,0:T(8,128)(2,1)} collective-permute-done((bf16[8,96,768]{2,1,0:T(8,128)(2,1)}, bf16[8,96,768]{2,1,0:T(8,128)(2,1)}, u32[]{:S(2)}, u32[]{:S(2)}) %collective-permute-start.31) | collective-permute-done | bytes 1179680 | tf_op jit(solution)/shard_map/ppermute | solution.py:256
  526.8 17.7 %all-gather.16.cloned.1.call-done = bf16[2048,2816]{1,0:T(8,128)(2,1)} async-done(((bf16[64,2816]{1,0:T(8,128)(2,1)}), bf16[2048,2816]{1,0:T(8,128)(2,1)}) %all-gather.16.cloned.1.call-update) | async-done | bytes 11534352 | tf_op jit(solution)/shard_map/all_gather | solution.py:488
  637.6 6.9 convolution_convert_fusion.3
  716.0 10.4 collective-permute-done.33
  739.7 11.8 %collective-permute-done.19 = bf16[16,10752]{1,0:T(8,128)(2,1)} collective-permute-done((bf16[16,10752]{1,0:T(8,128)(2,1)}, bf16[16,10752]{1,0:T(8,128)(2,1)}, u32[]{:S(2)}, u32[]{:S(2)}) %collective-permute-start.19) | collective-permute-done | bytes 344096 | tf_op jit(solution)/shard_map/ppermute | solution.py:256
  797.1 15.8 %collective-permute-done.6 = bf16[8,24,2432]{2,1,0:T(8,128)(2,1)} collective-permute-done((bf16[8,24,2432]{2,1,0:T(8,128)(2,1)}, bf16[8,24,2432]{2,1,0:T(8,128)(2,1)}, u32[]{:S(2)}, u32[]{:S(2)}) %collective-permute-start.6) | collective-permute-done | bytes 933920 | tf_op jit(solution)/shard_map/ppermute | solution.py:256
  829.2 8.9 collective-permute-done.26
  846.0 56.4 %collective-permute-done.27 = bf16[4,96,768]{2,1,0:T(8,128)(2,1)S(1)} collective-permute-done((bf16[4,96,768]{2,1,0:T(8,128)(2,1)S(1)}, bf16[4,96,768]{2,1,0:T(8,128)(2,1)S(1)}, u32[]{:S(2)}, u32[]{:S(2)}) %collective-permute-start.27) | collective-permute-done | bytes 589856 | tf_op jit(solution)/shard_map/ppermute | solution.py:256
  905.0 11.1 collective-permute-done.28
  918.0 14.3 %collective-permute-done.11 = bf16[8,24,3840]{2,1,0:T(8,128)(2,1)S(1)} collective-permute-done((bf16[8,24,3840]{2,1,0:T(8,128)(2,1)S(1)}, bf16[8,24,3840]{2,1,0:T(8,128)(2,1)S(1)}, u32[]{:S(2)}, u32[]{:S(2)}) %collective-permute-start.11) | collective-permute-done | bytes 1474592 | tf_op jit(solution)/shard_map/ppermute | solution.py:256
  956.6 26.6 %collective-permute-done.42 = bf16[4,64,2816]{2,1,0:T(8,128)(2,1)S(1)} collective-permute-done((bf16[4,64,2816]{2,1,0:T(8,128)(2,1)}, bf16[4,64,2816]{2,1,0:T(8,128)(2,1)S(1)}, u32[]{:S(2)}, u32[]{:S(2)}) %collective-permute-start.42) | collective-permute-done | bytes 1441824 | tf_op jit(solution)/shard_map/ppermute | solution.py:256
  992.1 41.6 %collective-permute-done.43 = bf16[2,64,2816]{2,1,0:T(8,128)(2,1)S(1)} collective-permute-done((bf16[2,64,2816]{2,1,0:T(8,128)(2,1)S(1)}, bf16[2,64,2816]{2,1,0:T(8,128)(2,1)S(1)}, u32[]{:S(2)}, u32[]{:S(2)}) %collective-permute-start.43) | collective-permute-done | bytes 720928 | tf_op jit(solution)/shard_map/ppermute | solution.py:256
  1035.2 15.4 %collective-permute-done.23 = bf16[2,24,8192]{2,1,0:T(8,128)(2,1)S(1)} collective-permute-done((bf16[2,24,8192]{2,1,0:T(8,128)(2,1)S(1)}, bf16[2,24,8192]{2,1,0:T(8,128)(2,1)S(1)}, u32[]{:S(2)}, u32[]{:S(2)}) %collective-permute-start.23) | collective-permute-done | bytes 786464 | tf_op jit(solution)/shard_map/ppermute | solution.py:256
  1095.2 7.8 collective-permute-done.49
  (1188 shorter events, 562.8 us)
Async XLA Ops:
  7.2 66.8 %all-gather.12.cloned.1.call-start = ((), (), s32[]{:S(2)}) async-start(), calls=%async_computation | async-start | bytes 3446784 | tf_op jit(solution)/shard_map/all_gather | solution.py:418
  11.6 149.5 %all-gather.18.cloned.1.call-start = ((), (), s32[]{:S(2)}) async-start(), calls=%async_computation.3 | async-start | bytes 9732096 | tf_op jit(solution)/shard_map/all_gather | solution.py:480
  14.2 231.0 %all-gather.22.cloned.1.call-start = ((), (), s32[]{:S(2)}) async-start(), calls=%async_computation.5 | async-start | bytes 9732096 | tf_op jit(solution)/shard_map/all_gather | solution.py:480
  15.0 295.8 %all-gather.20.cloned.1.call-start = ((), (), s32[]{:S(2)}) async-start(), calls=%async_computation.4 | async-start | bytes 4866048 | tf_op jit(solution)/shard_map/all_gather | solution.py:483
  15.8 360.3 %all-gather.24.cloned.1.call-start = ((), (), s32[]{:S(2)}) async-start(), calls=%async_computation.6 | async-start | bytes 4866048 | tf_op jit(solution)/shard_map/all_gather | solution.py:483
  16.4 473.6 %all-gather.14.cloned.1.call-start = ((), (), s32[]{:S(2)}) async-start(), calls=%async_computation.1 | async-start | bytes 3244032 | tf_op jit(solution)/shard_map/all_gather | solution.py:487
  17.2 527.3 %all-gather.16.cloned.1.call-start = ((), (), s32[]{:S(2)}) async-start(), calls=%async_computation.2 | async-start | bytes 11894784 | tf_op jit(solution)/shard_map/all_gather | solution.py:488
  479.5 43.4 %collective-permute-start.31 = (bf16[8,96,768]{2,1,0:T(8,128)(2,1)}, bf16[8,96,768]{2,1,0:T(8,128)(2,1)}, u32[]{:S(2)}, u32[]{:S(2)}) collective-permute-start(bf16[8,96,768]{2,1,0:T(8,128)(2,1)} %fusion.130), channel_id=1, source_target_pairs={{0,2},{1,3},{2,0},{3,1},{4,6},{5,7},{6,4},{7,5},{8,10},{9,11},{10,... | collective-permute-start | bytes 3538952 | tf_op jit(solution)/shard_map/ppermute | solution.py:256
  525.3 185.1 %collective-permute-start.32 = (bf16[4,96,768]{2,1,0:T(8,128)(2,1)}, bf16[4,96,768]{2,1,0:T(8,128)(2,1)}, u32[]{:S(2)}, u32[]{:S(2)}) collective-permute-start(bf16[4,96,768]{2,1,0:T(8,128)(2,1)} %fusion.153), channel_id=1, source_target_pairs={{0,4},{1,5},{2,6},{3,7},{4,0},{5,1},{6,2},{7,3},{8,12},{9,13},{10,... | collective-permute-start | bytes 1769480 | tf_op jit(solution)/shard_map/ppermute | solution.py:256
  650.2 52.8 %collective-permute-start.15 = (bf16[1,10752]{1,0:T(2,128)(2,1)S(1)}, bf16[1,10752]{1,0:T(2,128)(2,1)}, u32[]{:S(2)}, u32[]{:S(2)}) collective-permute-start(bf16[1,10752]{1,0:T(2,128)(2,1)S(1)} %constant_dynamic-update-slice_fusion.13), channel_id=1, source_target_pairs={{0,1},{1,0},{2,3},{3,2},{4,5},{5,4},{6,7},{7,6},{8,9},{9,8},{10,11... | collective-permute-start | bytes 64520 | tf_op jit(solution)/shard_map/ppermute | solution.py:256
  656.8 157.9 %collective-permute-start.40 = (bf16[16,64,2816]{2,1,0:T(8,128)(2,1)}, bf16[16,64,2816]{2,1,0:T(8,128)(2,1)}, u32[]{:S(2)}, u32[]{:S(2)}) collective-permute-start(bf16[16,64,2816]{2,1,0:T(8,128)(2,1)} %pad_maximum_fusion.1), channel_id=1, source_target_pairs={{0,1},{1,0},{2,3},{3,2},{4,5},{5,4},{6,7},{7,6},{8,9},{9,8},{10,11... | collective-permute-start | bytes 17301512 | tf_op jit(solution)/shard_map/ppermute | solution.py:256
  672.8 146.3 %collective-permute-start.20 = (bf16[16,24,8192]{2,1,0:T(8,128)(2,1)}, bf16[16,24,8192]{2,1,0:T(8,128)(2,1)}, u32[]{:S(2)}, u32[]{:S(2)}) collective-permute-start(bf16[16,24,8192]{2,1,0:T(8,128)(2,1)} %pad_maximum_fusion), channel_id=1, source_target_pairs={{0,1},{1,0},{2,3},{3,2},{4,5},{5,4},{6,7},{7,6},{8,9},{9,8},{10,11... | collective-permute-start | bytes 18874376 | tf_op jit(solution)/shard_map/ppermute | solution.py:256
  680.4 105.1 %collective-permute-start.5 = (bf16[16,24,2432]{2,1,0:T(8,128)(2,1)}, bf16[16,24,2432]{2,1,0:T(8,128)(2,1)}, u32[]{:S(2)}, u32[]{:S(2)}) collective-permute-start(bf16[16,24,2432]{2,1,0:T(8,128)(2,1)} %pad_maximum_fusion.7), channel_id=1, source_target_pairs={{0,1},{1,0},{2,3},{3,2},{4,5},{5,4},{6,7},{7,6},{8,9},{9,8},{10,11... | collective-permute-start | bytes 5603336 | tf_op jit(solution)/shard_map/ppermute | solution.py:256
  736.9 56.8 %collective-permute-start.25 = (bf16[16,96,768]{2,1,0:T(8,128)(2,1)}, bf16[16,96,768]{2,1,0:T(8,128)(2,1)}, u32[]{:S(2)}, u32[]{:S(2)}) collective-permute-start(bf16[16,96,768]{2,1,0:T(8,128)(2,1)} %dynamic-slice_bitcast_fusion.2), channel_id=1, source_target_pairs={{0,1},{1,0},{2,3},{3,2},{4,5},{5,4},{6,7},{7,6},{8,9},{9,8},{10,11... | collective-permute-start | bytes 7077896 | tf_op jit(solution)/shard_map/ppermute | solution.py:256
  784.3 56.3 %collective-permute-start.10 = (bf16[16,24,3840]{2,1,0:T(8,128)(2,1)}, bf16[16,24,3840]{2,1,0:T(8,128)(2,1)}, u32[]{:S(2)}, u32[]{:S(2)}) collective-permute-start(bf16[16,24,3840]{2,1,0:T(8,128)(2,1)} %pad_maximum_fusion.2), channel_id=1, source_target_pairs={{0,1},{1,0},{2,3},{3,2},{4,5},{5,4},{6,7},{7,6},{8,9},{9,8},{10,11... | collective-permute-start | bytes 8847368 | tf_op jit(solution)/shard_map/ppermute | solution.py:256
  817.4 118.4 %collective-permute-start.41 = (bf16[8,64,2816]{2,1,0:T(8,128)(2,1)S(1)}, bf16[8,64,2816]{2,1,0:T(8,128)(2,1)S(1)}, u32[]{:S(2)}, u32[]{:S(2)}) collective-permute-start(bf16[8,64,2816]{2,1,0:T(8,128)(2,1)S(1)} %fusion.7), channel_id=1, source_target_pairs={{0,2},{1,3},{2,0},{3,1},{4,6},{5,7},{6,4},{7,5},{8,10},{9,11},{10,... | collective-permute-start | bytes 8650760 | tf_op jit(solution)/shard_map/ppermute | solution.py:256
  823.0 118.3 %collective-permute-start.21 = (bf16[8,24,8192]{2,1,0:T(8,128)(2,1)S(1)}, bf16[8,24,8192]{2,1,0:T(8,128)(2,1)S(1)}, u32[]{:S(2)}, u32[]{:S(2)}) collective-permute-start(bf16[8,24,8192]{2,1,0:T(8,128)(2,1)S(1)} %fusion.6), channel_id=1, source_target_pairs={{0,4},{1,5},{2,6},{3,7},{4,0},{5,1},{6,2},{7,3},{8,12},{9,13},{10,... | collective-permute-start | bytes 9437192 | tf_op jit(solution)/shard_map/ppermute | solution.py:256
  840.1 62.3 %collective-permute-start.27 = (bf16[4,96,768]{2,1,0:T(8,128)(2,1)S(1)}, bf16[4,96,768]{2,1,0:T(8,128)(2,1)S(1)}, u32[]{:S(2)}, u32[]{:S(2)}) collective-permute-start(bf16[4,96,768]{2,1,0:T(8,128)(2,1)S(1)} %fusion.152), channel_id=1, source_target_pairs={{0,2},{1,3},{2,0},{3,1},{4,6},{5,7},{6,4},{7,5},{8,10},{9,11},{10,... | collective-permute-start | bytes 1769480 | tf_op jit(solution)/shard_map/ppermute | solution.py:256
  842.4 89.9 %collective-permute-start.11 = (bf16[8,24,3840]{2,1,0:T(8,128)(2,1)S(1)}, bf16[8,24,3840]{2,1,0:T(8,128)(2,1)S(1)}, u32[]{:S(2)}, u32[]{:S(2)}) collective-permute-start(bf16[8,24,3840]{2,1,0:T(8,128)(2,1)S(1)} %fusion.53), channel_id=1, source_target_pairs={{0,2},{1,3},{2,0},{3,1},{4,6},{5,7},{6,4},{7,5},{8,10},{9,11},{10,... | collective-permute-start | bytes 4423688 | tf_op jit(solution)/shard_map/ppermute | solution.py:256
  845.9 58.0 %collective-permute-start.9 = (bf16[1,24,2432]{2,1,0:T(8,128)(2,1)S(1)}, bf16[1,24,2432]{2,1,0:T(8,128)(2,1)S(1)}, u32[]{:S(2)}, u32[]{:S(2)}) collective-permute-start(bf16[1,24,2432]{2,1,0:T(8,128)(2,1)S(1)} %add_convert_fusion.13), channel_id=1, source_target_pairs={{0,8},{1,9},{2,10},{3,11},{4,12},{5,13},{6,14},{7,15},{8,0},{9,1},... | collective-permute-start | bytes 350216 | tf_op jit(solution)/shard_map/ppermute | solution.py:256
  939.9 43.2 %collective-permute-start.42 = (bf16[4,64,2816]{2,1,0:T(8,128)(2,1)}, bf16[4,64,2816]{2,1,0:T(8,128)(2,1)S(1)}, u32[]{:S(2)}, u32[]{:S(2)}) collective-permute-start(bf16[4,64,2816]{2,1,0:T(8,128)(2,1)} %fusion.54), channel_id=1, source_target_pairs={{0,4},{1,5},{2,6},{3,7},{4,0},{5,1},{6,2},{7,3},{8,12},{9,13},{10,... | collective-permute-start | bytes 4325384 | tf_op jit(solution)/shard_map/ppermute | solution.py:256
  985.4 48.3 %collective-permute-start.43 = (bf16[2,64,2816]{2,1,0:T(8,128)(2,1)S(1)}, bf16[2,64,2816]{2,1,0:T(8,128)(2,1)S(1)}, u32[]{:S(2)}, u32[]{:S(2)}) collective-permute-start(bf16[2,64,2816]{2,1,0:T(8,128)(2,1)S(1)} %fusion.106), channel_id=1, source_target_pairs={{0,16},{1,17},{2,18},{3,19},{4,20},{5,21},{6,22},{7,23},{8,24},{9,... | collective-permute-start | bytes 2162696 | tf_op jit(solution)/shard_map/ppermute | solution.py:256
  987.8 62.8 %collective-permute-start.23 = (bf16[2,24,8192]{2,1,0:T(8,128)(2,1)S(1)}, bf16[2,24,8192]{2,1,0:T(8,128)(2,1)S(1)}, u32[]{:S(2)}, u32[]{:S(2)}) collective-permute-start(bf16[2,24,8192]{2,1,0:T(8,128)(2,1)S(1)} %fusion.98), channel_id=1, source_target_pairs={{0,16},{1,17},{2,18},{3,19},{4,20},{5,21},{6,22},{7,23},{8,24},{9,... | collective-permute-start | bytes 2359304 | tf_op jit(solution)/shard_map/ppermute | solution.py:256
  992.0 60.0 %collective-permute-start.14 = (bf16[1,24,3840]{2,1,0:T(8,128)(2,1)S(1)}, bf16[1,24,3840]{2,1,0:T(8,128)(2,1)S(1)}, u32[]{:S(2)}, u32[]{:S(2)}) collective-permute-start(bf16[1,24,3840]{2,1,0:T(8,128)(2,1)S(1)} %add_convert_fusion.10), channel_id=1, source_target_pairs={{0,8},{1,9},{2,10},{3,11},{4,12},{5,13},{6,14},{7,15},{8,0},{9,1},... | collective-permute-start | bytes 552968 | tf_op jit(solution)/shard_map/ppermute | solution.py:256
  (364 other events, 5836.5 us)
Sparse Core Ops, SparseCore 0:
  11.7 62.3 all-gather.11
  77.5 83.5 all-gather.17
  164.5 80.6 all-gather.21
  248.5 62.2 all-gather.19
  313.6 62.4 all-gather.23
  378.8 57.7 all-gather.13
  440.0 104.4 all-gather.15

commit v2 on v1

v2 whole, which is shorter than its diff:
```python
import functools
import math

import jax
import jax.numpy as jnp
from jax import lax
from jax.experimental import pallas as pl
from jax.experimental.pallas import tpu as pltpu
from jax.sharding import PartitionSpec as P

D = 768
HD = 64
F = 3072
P_SIZE = 2048
Z = 768
NCLS = 1001
PD = 16
TF = 256
L = 2
GRID = 16
TOK = 256
VB = 11520


NORM_EPS = 1e-06
SCORE_SCALE = 0.125
LEARN_RATE = 0.03
DECAY_RATE = 0.5
CLIP_LIMIT = 0.05
FACTOR_EPS = 1e-30


def cut_parts(array, part_widths):
    borders = []
    running = 0
    for part_width in part_widths[:-1]:
        running += part_width
        borders.append(running)
    return jnp.split(array, borders, axis=-1)


def positions():
    quarter = D // 4
    omega_rate = jnp.exp(-math.log(10000.0) * jnp.arange(quarter, dtype=jnp.float32) / quarter)
    token_place = jnp.arange(TOK)
    column = (token_place % GRID).astype(jnp.float32)
    row_place = (token_place // GRID).astype(jnp.float32)

    def encode(coords):
        angles = coords[:, None] * omega_rate[None, :]
        return jnp.concatenate([jnp.sin(angles), jnp.cos(angles)], axis=1)

    return jnp.concatenate([encode(column), encode(row_place)], axis=1)


def time_freq(timesteps):
    half_width = TF // 2
    freq_rate = jnp.exp(-math.log(10000.0) * jnp.arange(half_width, dtype=jnp.float32) / half_width)
    angles = timesteps.astype(jnp.float32)[:, None] * freq_rate[None, :]
    return jnp.concatenate([jnp.cos(angles), jnp.sin(angles)], axis=1)


def silu_back(before, grad_after):
    return jax.vjp(jax.nn.silu, before)[1](grad_after)[0]


def total_rows(values):
    return jnp.sum(values.reshape(-1, values.shape[-1]), axis=0)


def linear(left_side, weight_side):
    return jnp.dot(left_side, weight_side, preferred_element_type=jnp.float32)


LOW = jnp.bfloat16
FULL = jnp.float32


def dot(left, right):
    return jnp.dot(left, right, preferred_element_type=jnp.float32)


def dot_rows(left, right):
    return lax.dot_general(
        left, right, (((1,), (1,)), ((), ())), preferred_element_type=jnp.float32
    )


def dot_tokens(left, right):
    return lax.dot_general(
        left, right, (((0,), (0,)), ((), ())), preferred_element_type=jnp.float32
    )


def bf16(values):
    return values.astype(jnp.bfloat16)


def moved(values, order):
    return bf16(dot(values, order))


def moved_back(values, order):
    return bf16(dot_rows(values, order))


def moved_back_wide(values, order):
    high = bf16(values)
    return dot_rows(high, order) + dot_rows(bf16(values - high.astype(FULL)), order)


def row_sum(values):
    return jnp.sum(values, axis=0, keepdims=True)


def norm_parts(values):
    centred = values - jnp.mean(values, axis=-1, keepdims=True)
    scale = lax.rsqrt(jnp.mean(centred * centred, axis=-1, keepdims=True) + NORM_EPS)
    return centred * scale, scale


def norm_back(unit, scale, grad_unit):
    mean_grad = jnp.mean(grad_unit, axis=-1, keepdims=True)
    mean_both = jnp.mean(grad_unit * unit, axis=-1, keepdims=True)
    return scale * (grad_unit - mean_grad - unit * mean_both)


GELU_ROOT = math.sqrt(2.0 / math.pi)
GELU_CUBE = 0.044715


def gelu_parts(values):
    square = values * values
    bent = jnp.tanh(GELU_ROOT * values * (1.0 + GELU_CUBE * square))
    half = 0.5 * (1.0 + bent)
    slope = half + 0.5 * values * (1.0 - bent * bent) * GELU_ROOT * (
        1.0 + 3.0 * GELU_CUBE * square
    )
    return values * half, slope


def silu_parts(values):
    gate = jax.nn.sigmoid(values)
    return values * gate, gate * (1.0 + values * (1.0 - gate))


def half_lanes(shape, which):
    lane = lax.broadcasted_iota(jnp.int32, shape, 1)
    return (lane < HD) if which == 0 else (lane >= HD)


def fetch(source, target, semaphore):
    return pltpu.make_async_copy(source, target, semaphore)


def group_of(groups, place, block, half):
    base = 5 * (place // 4)
    if place % 4 < 3:
        return groups[base + place % 4].at[block]
    if block < half:
        return groups[base + 3].at[block]
    return groups[base + 4].at[block - half]


def load_blocks(groups, half, first, size, held, semaphores, rows):
    copies = []
    for block in range(size):
        copies.append(
            [
                fetch(
                    group_of(groups, place, first + block, half),
                    held.at[block, pl.ds(place * rows, rows)],
                    semaphores.at[block, place],
                )
                for place in range(8)
            ]
        )
    return copies


def start_all(copies):
    for copy in copies:
        copy.start()


def wait_all(copies):
    for copy in copies:
        copy.wait()


def depth_of(relative, index):
    if not relative:
        return index
    return index ^ (lax.axis_index("fsdp") // 8)


def attn_forward_kernel(
    half,
    hidden,
    mods,
    bias,
    order,
    *refs,
):
    groups = refs[:10]
    normed_out, packed_out, log_out, attended_out, branch_out, middle_out = refs[10:16]
    held, attended, semaphores = refs[16:]
    copies = load_blocks(groups, half, 0, 4, held, semaphores, 96)
    for block in range(4):
        start_all(copies[block])
    unit, _ = norm_parts(hidden[...])
    normed_out[...] = moved(bf16(unit * (1.0 + mods[1:2]) + mods[0:1]), order[...])
    for block in range(3):
        wait_all(copies[block])
        packed_out[block] = bf16(dot(normed_out[...], held[block]) + bias[block : block + 1])
    lanes = lax.broadcasted_iota(jnp.int32, (TOK, 128), 1)

    def pair(index, logs):
        columns = pl.ds(pl.multiple_of(index * 128, 128), 128)
        queries, keys, values = (packed_out[part, :, columns] for part in range(3))
        halves = []
        for which in range(2):
            mask = half_lanes((TOK, 128), which)
            scores = dot_rows(jnp.where(mask, queries, 0), keys) * SCORE_SCALE
            top = jnp.max(scores, axis=-1, keepdims=True)
            raised = jnp.exp(scores - top)
            total = jnp.sum(raised, axis=-1, keepdims=True)
            halves.append(dot(bf16(raised * (1.0 / total)), values))
            logs = jnp.where(lanes == 2 * index + which, top + jnp.log(total), logs)
        attended[:, columns] = bf16(jnp.where(half_lanes((TOK, 128), 0), *halves))
        return logs

    log_out[...] = lax.fori_loop(0, D // 128, pair, jnp.zeros((TOK, 128), jnp.float32))
    attended_out[...] = moved(attended[...], order[...])
    wait_all(copies[3])
    branch = dot(attended_out[...], held[3]) + bias[3:4]
    branch_out[...] = branch
    middle_out[...] = hidden[...] + mods[2:3] * branch


def mlp_forward_kernel(half, first_down, relative, middle, mods, bias, order, down_order, *refs):
    groups = refs[:10]
    normed_out, slope_out, active_out, branch_out, hidden_out = refs[10:15]
    held_up, held_down, total, before, semaphores_up, semaphores_down = refs[15:]
    ups = load_blocks(groups, half, 4, 4, held_up, semaphores_up, 96)
    downs = load_blocks(groups, half, first_down, 4, held_down, semaphores_down, 96)
    for block in range(4):
        start_all(ups[block])
    for block in range(4):
        start_all(downs[block])
    unit, _ = norm_parts(middle[...])
    normed_out[...] = moved(bf16(unit * (1.0 + mods[4:5]) + mods[3:4]), order[...])
    for block in range(4):
        wait_all(ups[block])
        before[block] = dot(normed_out[...], held_up[block]) + bias[block + 4 : block + 5]
    for depth in range(4):
        active, slope = gelu_parts(before[depth_of(relative, depth)])
        active_out[depth] = moved(bf16(active), down_order[...])
        slope_out[depth] = moved(bf16(slope), down_order[...])
        wait_all(downs[depth])
        part = dot(active_out[depth], held_down[depth])
        total[...] = part if depth == 0 else total[...] + part
    branch = total[...] + bias[14:15]
    branch_out[...] = branch
    hidden_out[...] = middle[...] + mods[5:6] * branch


def mlp_backward_kernel(
    half,
    first_down,
    relative,
    grad_out,
    mods,
    middle,
    normed,
    slope,
    active,
    branch,
    order,
    down_order,
    *refs,
):
    groups = refs[:10]
    grad_middle_out, grad_mods_out, grad_bias_out, mine_out = refs[10:14]
    theirs_out = refs[14:18]
    held_up, held_down, made, low, grad_normed, semaphores_up, semaphores_down, sent = refs[18:]
    ups = load_blocks(groups, half, 4, 4, held_up, semaphores_up, 96)
    downs = load_blocks(groups, half, first_down, 4, held_down, semaphores_down, 96)
    for block in range(4):
        start_all(downs[block])
    for block in range(4):
        start_all(ups[block])
    grad_hidden = grad_out[...]
    grad_branch = grad_hidden * mods[5:6]
    grad_mods_out[2:3] = row_sum(grad_hidden * branch[...])
    grad_bias_out[4:5] = row_sum(grad_branch)
    grad_low = bf16(grad_branch)
    given = []
    for depth in range(4):
        wait_all(downs[depth])
        grad_active = dot_rows(grad_low, held_down[depth])
        made[4 + depth] = bf16(dot_tokens(active[depth], grad_low))
        given += give(made, 4 + depth, mine_out, theirs_out, sent)
        before_low = moved_back(
            bf16(grad_active * slope[depth].astype(FULL)), down_order[...]
        )
        low[depth_of(relative, depth)] = before_low
    for block in range(4):
        before_low = low[block]
        grad_bias_out[block : block + 1] = row_sum(before_low.astype(FULL))
        made[block] = bf16(dot_tokens(normed[...], before_low))
        given += give(made, block, mine_out, theirs_out, sent)
        wait_all(ups[block])
        part = dot_rows(before_low, held_up[block])
        grad_normed[...] = part if block == 0 else grad_normed[...] + part
    unit, scale = norm_parts(middle[...])
    grad_unit = moved_back_wide(grad_normed[...], order[...])
    grad_mods_out[0:1] = row_sum(grad_unit)
    grad_mods_out[1:2] = row_sum(grad_unit * unit)
    grad_middle_out[...] = grad_hidden + norm_back(unit, scale, grad_unit * (1.0 + mods[4:5]))
    wait_all(given)


def give(made, block, mine_out, theirs_outs, sent):
    length = made.shape[1] // 2
    step = theirs_outs[0].shape[0]
    theirs_out = theirs_outs[block // step].at[block % step]
    copies = [
        fetch(made.at[block, pl.ds(0, length)], mine_out.at[block], sent.at[0, block]),
        fetch(made.at[block, pl.ds(length, length)], theirs_out, sent.at[1, block]),
    ]
    start_all(copies)
    return copies


def attn_backward_kernel(
    half,
    grad_middle,
    mods,
    hidden,
    normed,
    packed,
    logs,
    attended,
    branch,
    order,
    *refs,
):
    groups = refs[:10]
    grad_hidden_out, grad_mods_out, grad_bias_out, mine_out = refs[10:14]
    theirs_out = refs[14:16]
    held, made, grad_packed, grad_attended, grad_normed, semaphores, sent = refs[16:]
    copies = load_blocks(groups, half, 0, 4, held, semaphores, 96)
    for block in (3, 0, 1, 2):
        start_all(copies[block])
    grad_mid = grad_middle[...]
    grad_branch = grad_mid * mods[2:3]
    grad_mods_out[2:3] = row_sum(grad_mid * branch[...])
    grad_bias_out[3:4] = row_sum(grad_branch)
    grad_low = bf16(grad_branch)
    made[3] = bf16(dot_tokens(attended[...], grad_low))
    given = give(made, 3, mine_out, theirs_out, sent)
    wait_all(copies[3])
    grad_attended[...] = moved_back(bf16(dot_rows(grad_low, held[3])), order[...])
    lanes = lax.broadcasted_iota(jnp.int32, (TOK, 128), 1)
    first = half_lanes((TOK, 128), 0)

    def pair(index, carry):
        columns = pl.ds(pl.multiple_of(index * 128, 128), 128)
        queries, keys, values = (packed[part, :, columns] for part in range(3))
        grad_pair = grad_attended[:, columns]
        grads = []
        for which in range(2):
            mask = half_lanes((TOK, 128), which)
            log_total = jnp.sum(
                jnp.where(lanes == 2 * index + which, logs[...], 0.0), axis=-1, keepdims=True
            )
            scores = dot_rows(jnp.where(mask, queries, 0), keys) * SCORE_SCALE
            attention = jnp.exp(scores - log_total)
            grad_attention = dot_rows(jnp.where(mask, grad_pair, 0), values)
            grad_values = dot_tokens(bf16(attention), grad_pair)
            weighted = attention * grad_attention
            grad_scores = weighted - attention * jnp.sum(weighted, axis=-1, keepdims=True)
            score_low = bf16(grad_scores * SCORE_SCALE)
            grads.append((dot(score_low, keys), dot_tokens(score_low, queries), grad_values))
        for part in range(3):
            both = jnp.where(first, grads[0][part], grads[1][part])
            grad_bias_out[part : part + 1, columns] = row_sum(both)
            grad_packed[part, :, columns] = bf16(both)
        return carry

    lax.fori_loop(0, D // 128, pair, 0)
    for block in range(3):
        grad_part = grad_packed[block]
        made[block] = bf16(dot_tokens(normed[...], grad_part))
        given += give(made, block, mine_out, theirs_out, sent)
        wait_all(copies[block])
        part = dot_rows(grad_part, held[block])
        grad_normed[...] = part if block == 0 else grad_normed[...] + part
    unit, scale = norm_parts(hidden[...])
    grad_unit = moved_back_wide(grad_normed[...], order[...])
    grad_mods_out[0:1] = row_sum(grad_unit)
    grad_mods_out[1:2] = row_sum(grad_unit * unit)
    grad_hidden_out[...] = grad_mid + norm_back(unit, scale, grad_unit * (1.0 + mods[1:2]))
    wait_all(given)


ONE_WIDTHS = (D, D, P_SIZE - 2 * D)
REST = P_SIZE + Z
CHUNK = P_SIZE // 4


def projector_kernel(
    half,
    first_one,
    relative,
    first,
    features,
    bias_one,
    bias_two,
    bias_three,
    order,
    chunk_order,
    *refs,
):
    groups, rest_groups = refs[:10], refs[10:20]
    outs = refs[20:32]
    grad_first_out, loss_out, grad_bias_one, grad_bias_two, grad_bias_three = outs[:5]
    one_mine, one_theirs, rest_mine, rest_theirs = outs[5], outs[6:7], outs[7], outs[8:]
    (
        held_one,
        held_rest,
        made_one,
        made_rest,
        slope_one,
        slope_two,
        active_one,
        active_two,
        wide,
        low,
        one_semaphores,
        rest_semaphores,
        one_sent,
        rest_sent,
    ) = refs[32:]
    ones = load_blocks(groups, half, first_one, 3, held_one, one_semaphores, 96)
    rests = load_blocks(rest_groups, 2, 0, 4, held_rest, rest_semaphores, 64)
    for copies in ones + rests:
        start_all(copies)
    chunks = [pl.ds(CHUNK * index, CHUNK) for index in range(4)]

    def source(depth):
        return pl.ds(pl.multiple_of(depth_of(relative, depth) * CHUNK, CHUNK), CHUNK)

    def bend(active, slope):
        for depth in range(4):
            values, slopes = silu_parts(wide[:, source(depth)])
            active[:, chunks[depth]] = moved(bf16(values), chunk_order[...])
            slope[:, chunks[depth]] = moved(bf16(slopes), chunk_order[...])

    first_low = moved(bf16(first[...]), order[...])
    running = 0
    for block, width in enumerate(ONE_WIDTHS):
        columns = slice(running, running + width)
        wait_all(ones[block])
        wide[:, columns] = dot(first_low, held_one[block, :, :width]) + bias_one[:, columns]
        running += width
    bend(active_one, slope_one)
    for copies in rests:
        wait_all(copies)

    def product(left, columns):
        total = dot(left[:, chunks[0]], held_rest[0, :, columns])
        for depth in range(1, 4):
            total = total + dot(left[:, chunks[depth]], held_rest[depth, :, columns])
        return total

    for index in range(4):
        wide[:, chunks[index]] = product(active_one, chunks[index]) + bias_two[:, chunks[index]]
    bend(active_two, slope_two)
    tail = pl.ds(P_SIZE, Z)
    result = product(active_two, tail) + bias_three[...]
    wanted = features[...]
    inner = jnp.sum(result * wanted, axis=-1, keepdims=True)
    own = jnp.sum(result * result, axis=-1, keepdims=True) + NORM_EPS
    length = jnp.sqrt(own) * jnp.sqrt(jnp.sum(wanted * wanted, axis=-1, keepdims=True) + NORM_EPS)
    cosine = inner / length
    loss_out[...] = jnp.broadcast_to(-0.5 / TOK * row_sum(cosine), (8, 128))
    grad_result = (-0.5 / TOK) * (wanted / length - result * (cosine / own))
    grad_bias_three[...] = row_sum(grad_result)
    grad_three = bf16(grad_result)
    for depth in range(4):
        made_rest[depth, :, tail] = bf16(dot_tokens(active_two[:, chunks[depth]], grad_three))

    def bend_back(grad, slope, depth, grad_bias):
        columns = source(depth)
        low[:, columns] = moved_back(
            bf16(grad * slope[:, chunks[depth]].astype(FULL)), chunk_order[...]
        )
        grad_bias[:, columns] = row_sum(low[:, columns].astype(FULL))

    for depth in range(4):
        bend_back(dot_rows(grad_three, held_rest[depth, :, tail]), slope_two, depth, grad_bias_two)
    given = []
    main = pl.ds(0, P_SIZE)
    for depth in range(4):
        made_rest[depth, :, main] = bf16(dot_tokens(active_one[:, chunks[depth]], low[...]))
        given += give(made_rest, depth, rest_mine, rest_theirs, rest_sent)
    for depth in range(4):
        wide[:, chunks[depth]] = dot_rows(low[...], held_rest[depth, :, main])
    for depth in range(4):
        bend_back(wide[:, chunks[depth]], slope_one, depth, grad_bias_one)
    running = 0
    grad_first = None
    for block, width in enumerate(ONE_WIDTHS):
        grad_part = low[:, running : running + width]
        made_one[block, :, :width] = bf16(dot_tokens(first_low, grad_part))
        if width < D:
            made_one[block, :, width:] = jnp.zeros((D, D - width), LOW)
        given += give(made_one, block, one_mine, one_theirs, one_sent)
        part = dot_rows(grad_part, held_one[block, :, :width])
        grad_first = part if grad_first is None else grad_first + part
        running += width
    grad_first_out[...] = moved_back_wide(grad_first, order[...])
    wait_all(given)


def head_kernel(
    hidden,
    mods,
    head,
    head_bias,
    targets,
    time_weight,
    grad_hidden_out,
    grad_mods_out,
    grad_head_out,
    grad_head_bias_out,
    loss_out,
):
    unit, scale = norm_parts(hidden[...])
    final_low = bf16(unit * (1.0 + mods[1:2]) + mods[0:1])
    residual = dot(final_low, head[...]) + head_bias[...] - targets[...]
    weight = time_weight[...]
    square = jnp.sum(row_sum(residual * residual), axis=1, keepdims=True)
    loss_out[...] = jnp.broadcast_to(square * weight / (TOK * PD), (8, 128))
    grad_output = (2.0 / (TOK * PD)) * weight * residual
    grad_head_bias_out[...] = row_sum(grad_output)
    grad_low = bf16(grad_output)
    grad_head_out[...] = dot_tokens(final_low, grad_low)
    grad_unit = dot_rows(grad_low, head[...])
    grad_mods_out[0:1] = row_sum(grad_unit)
    grad_mods_out[1:2] = row_sum(grad_unit * unit)
    grad_hidden_out[...] = norm_back(unit, scale, grad_unit * (1.0 + mods[1:2]))


def cost(microseconds):
    return pl.CostEstimate(flops=microseconds, bytes_accessed=0, transcendentals=0)


VMEM_WHOLE = pl.BlockSpec(memory_space=pltpu.VMEM)
IN_PLACE = pl.BlockSpec(memory_space=pl.ANY)


def shaped(kind, *shape):
    return jax.ShapeDtypeStruct(shape, kind)


def call(kernel, inputs, far_inputs, outputs, far_outputs, scratch, microseconds, limit):
    return pl.pallas_call(
        kernel,
        in_specs=[VMEM_WHOLE] * len(inputs) + [IN_PLACE] * len(far_inputs),
        out_specs=[VMEM_WHOLE] * len(outputs) + [IN_PLACE] * len(far_outputs),
        out_shape=[*outputs, *far_outputs],
        scratch_shapes=scratch,
        cost_estimate=cost(microseconds),
        compiler_params=pltpu.CompilerParams(vmem_limit_bytes=limit * 2**20),
    )(*inputs, *far_inputs)


BLOCK_SEMAPHORES = pltpu.SemaphoreType.DMA((4, 8))


def orders_kernel(narrow_source, down_source, chunk_source, narrow, down, chunk):
    for source, order in [(narrow_source, narrow), (down_source, down), (chunk_source, chunk)]:
        rows = lax.broadcasted_iota(jnp.int32, order.shape, 0)
        order[...] = jnp.where(rows == source[...], 1.0, 0.0).astype(LOW)


class Orders:
    def __init__(self, position, relative):
        self.relative = relative
        near, depth = (position & 7, position >> 3) if relative else (0, 0)

        def places(index):
            if not relative:
                return index
            return near ^ (((index & 3) << 1) | (index >> 2))

        column = jnp.arange(D)
        narrow = column
        if relative:
            group, deep, inner = column // 96, (column // 24) % 4, column % 24
            narrow = ((deep ^ depth) * 8 + places(group)) * 24 + inner
        down = places(column // 96) * 96 + column % 96
        column = jnp.arange(CHUNK)
        chunk = places(column // 64) * 64 + column % 64
        sources = [source[None].astype(jnp.int32) for source in (narrow, down, chunk)]
        self.narrow, self.down, self.chunk = pl.pallas_call(
            orders_kernel,
            in_specs=[VMEM_WHOLE] * 3,
            out_specs=[VMEM_WHOLE] * 3,
            out_shape=[shaped(LOW, D, D), shaped(LOW, D, D), shaped(LOW, CHUNK, CHUNK)],
            cost_estimate=cost(3),
            compiler_params=pltpu.CompilerParams(vmem_limit_bytes=16 * 2**20),
        )(*sources)


def attn_forward(hidden, mods, bias, orders, gathered):
    return call(
        functools.partial(attn_forward_kernel, gathered.half),
        [hidden, mods, bias, orders.narrow],
        gathered.groups,
        [
            shaped(LOW, TOK, D),
            shaped(LOW, 3, TOK, D),
            shaped(FULL, TOK, 128),
            shaped(LOW, TOK, D),
            shaped(FULL, TOK, D),
            shaped(FULL, TOK, D),
        ],
        [],
        [pltpu.VMEM((4, D, D), LOW), pltpu.VMEM((TOK, D), LOW), BLOCK_SEMAPHORES],
        11,
        32,
    )


def mlp_forward(middle, mods, bias, orders, gathered):
    return call(
        functools.partial(
            mlp_forward_kernel, gathered.half, gathered.first_down, orders.relative
        ),
        [middle, mods, bias, orders.narrow, orders.down],
        gathered.groups,
        [
            shaped(LOW, TOK, D),
            shaped(LOW, 4, TOK, D),
            shaped(LOW, 4, TOK, D),
            shaped(FULL, TOK, D),
            shaped(FULL, TOK, D),
        ],
        [],
        [
            pltpu.VMEM((4, D, D), LOW),
            pltpu.VMEM((4, D, D), LOW),
            pltpu.VMEM((TOK, D), FULL),
            pltpu.VMEM((4, TOK, D), FULL),
            BLOCK_SEMAPHORES,
            BLOCK_SEMAPHORES,
        ],
        11,
        40,
    )


def mlp_backward(grad_out, mods, kept, orders, gathered):
    return call(
        functools.partial(
            mlp_backward_kernel, gathered.half, gathered.first_down, orders.relative
        ),
        [grad_out, mods, *kept, orders.narrow, orders.down],
        gathered.groups,
        [shaped(FULL, TOK, D), shaped(FULL, 3, D), shaped(FULL, 5, D)],
        [shaped(LOW, 8, D // 2, D)] + [shaped(LOW, 2, D // 2, D)] * 4,
        [
            pltpu.VMEM((4, D, D), LOW),
            pltpu.VMEM((4, D, D), LOW),
            pltpu.VMEM((8, D, D), LOW),
            pltpu.VMEM((4, TOK, D), LOW),
            pltpu.VMEM((TOK, D), FULL),
            BLOCK_SEMAPHORES,
            BLOCK_SEMAPHORES,
            pltpu.SemaphoreType.DMA((2, 8)),
        ],
        16,
        48,
    )


def attn_backward(grad_middle, mods, kept, orders, gathered):
    return call(
        functools.partial(attn_backward_kernel, gathered.half),
        [grad_middle, mods, *kept, orders.narrow],
        gathered.groups,
        [shaped(FULL, TOK, D), shaped(FULL, 3, D), shaped(FULL, 4, D)],
        [shaped(LOW, 4, D // 2, D)] + [shaped(LOW, 2, D // 2, D)] * 2,
        [
            pltpu.VMEM((4, D, D), LOW),
            pltpu.VMEM((4, D, D), LOW),
            pltpu.VMEM((3, TOK, D), LOW),
            pltpu.VMEM((TOK, D), LOW),
            pltpu.VMEM((TOK, D), FULL),
            BLOCK_SEMAPHORES,
            pltpu.SemaphoreType.DMA((2, 4)),
        ],
        13,
        40,
    )


def projector(first, features, bias_one, bias_two, bias_three, orders, gathered, rest_gathered):
    return call(
        functools.partial(
            projector_kernel, gathered.half, gathered.first_one, orders.relative
        ),
        [first, features, bias_one, bias_two, bias_three, orders.narrow, orders.chunk],
        [*gathered.groups, *rest_gathered.groups],
        [
            shaped(FULL, TOK, D),
            shaped(FULL, 8, 128),
            shaped(FULL, 1, P_SIZE),
            shaped(FULL, 1, P_SIZE),
            shaped(FULL, 1, Z),
        ],
        [
            shaped(LOW, 3, D // 2, D),
            shaped(LOW, 3, D // 2, D),
            shaped(LOW, 4, CHUNK // 2, REST),
        ]
        + [shaped(LOW, 1, CHUNK // 2, REST)] * 4,
        [
            pltpu.VMEM((3, D, D), LOW),
            pltpu.VMEM((4, CHUNK, REST), LOW),
            pltpu.VMEM((3, D, D), LOW),
            pltpu.VMEM((4, CHUNK, REST), LOW),
            pltpu.VMEM((TOK, P_SIZE), LOW),
            pltpu.VMEM((TOK, P_SIZE), LOW),
            pltpu.VMEM((TOK, P_SIZE), LOW),
            pltpu.VMEM((TOK, P_SIZE), LOW),
            pltpu.VMEM((TOK, P_SIZE), FULL),
            pltpu.VMEM((TOK, P_SIZE), LOW),
            pltpu.SemaphoreType.DMA((3, 8)),
            BLOCK_SEMAPHORES,
            pltpu.SemaphoreType.DMA((2, 3)),
            pltpu.SemaphoreType.DMA((2, 4)),
        ],
        27,
        56,
    )


def head(hidden, mods, head_low, head_bias, targets, time_weight):
    return call(
        head_kernel,
        [hidden, mods, head_low, head_bias, targets, time_weight],
        [],
        [
            shaped(FULL, TOK, D),
            shaped(FULL, 2, D),
            shaped(FULL, D, PD),
            shaped(FULL, 1, PD),
            shaped(FULL, 8, 128),
        ],
        [],
        [],
        5,
        24,
    )


def swap(array, mask, count):
    return lax.ppermute(array, "fsdp", [(place, place ^ mask) for place in range(count)])


def bit_of(position, bit):
    return (position >> bit) & 1


def pick(array, bits, chosen):
    sizes, starts, lengths = [], [], []
    previous = None
    for bit in bits:
        fixed = bit in chosen
        if fixed != previous:
            sizes.append(1)
            starts.append(0)
            lengths.append(1)
        sizes[-1] *= 2
        if fixed:
            starts[-1] = starts[-1] * 2 + chosen[bit]
        else:
            lengths[-1] *= 2
        previous = fixed
    ahead, tail = array.shape[:1], array.shape[2:]
    view = array.reshape(ahead + tuple(sizes) + tail)
    starts = [jnp.int32(0)] + [jnp.asarray(start, jnp.int32) for start in starts]
    starts += [jnp.int32(0)] * len(tail)
    taken = lax.dynamic_slice(view, starts, ahead + tuple(lengths) + tail)
    return taken.reshape(ahead + (-1,) + tail)


def scatter_sum(parts, bit_order, position, count, kind, before=()):
    before = dict(before)
    all_bits = list(reversed(range(count.bit_length() - 1)))
    held = [(parts, all_bits)]
    fixed = {}

    def totals(chosen):
        summed = [None] * len(parts)
        for arrays, bits in held:
            wanted = {bit: value for bit, value in chosen.items() if bit in bits}
            for slot, array in enumerate(arrays):
                piece = pick(array, bits, wanted).astype(jnp.float32)
                summed[slot] = piece if summed[slot] is None else summed[slot] + piece
        return summed

    for bit in bit_order:
        mine = bit_of(position, bit)
        pieces = [piece.astype(kind) for piece in totals({**fixed, bit: 1 - mine})]
        if bit in before:
            pieces = before[bit](pieces)
        shapes = [piece.shape for piece in pieces]
        if len(pieces) == 1:
            received = [swap(pieces[0], 1 << bit, count)]
        else:
            width = pieces[0].shape[-1]
            flat = [piece.reshape(-1, width) for piece in pieces]
            moved = swap(jnp.concatenate(flat), 1 << bit, count)
            received, running = [], 0
            for piece, shape in zip(flat, shapes):
                received.append(moved[running : running + piece.shape[0]].reshape(shape))
                running += piece.shape[0]
        fixed[bit] = mine
        held.append((received, [other for other in all_bits if other not in fixed]))
    return [piece[:, 0] for piece in totals(fixed)]


def meet(*values):
    return lax.optimization_barrier(values)


class Gather:
    def __init__(self, pack, wide, count):
        self.pack, self.wide, self.count = pack, wide, count

    def move(self, array, mask):
        return swap(array, mask, self.count)

    def merged(self, packs):
        width = self.pack.shape[-1]
        long = [pack[self.wide :].reshape(1, -1, width) for pack in packs]
        if not self.wide:
            return jnp.concatenate(long)
        short = jnp.stack([pack[: self.wide] for pack in packs], axis=1)
        return jnp.concatenate([short.reshape(self.wide, -1, width)] + long)

    def along_z(self):
        own = self.pack
        self.quad = self.merged([own] + [self.move(own, mask) for mask in (8, 16, 24)])
        self.half = self.quad.shape[0] // 2

    def along_xy(self):
        self.by_y = self.move(self.quad, 4)
        self.by_x = self.move(self.quad, 2)

    def across(self):
        self.far = [
            self.move(self.by_y[: self.half], 2),
            self.move(self.by_x[self.half :], 4),
        ]

    def finish(self):
        own = [self.quad, self.by_x, self.by_y, *self.far]
        self.groups = own + [self.move(group, 1) for group in own]


class PlainGather(Gather):
    def along_z(self):
        pass

    along_xy = across = along_z

    def finish(self):
        full = lax.all_gather(self.pack, "fsdp")
        _, _, rows, width = full.shape
        long = full[:, self.wide :].reshape(4, 8, -1, width)
        blocks = long
        if self.wide:
            short = jnp.swapaxes(full[:, : self.wide], 0, 1).reshape(self.wide, 8, -1, width)
            blocks = jnp.concatenate([short, long])
        self.half = blocks.shape[0] // 2
        self.groups = []
        for core in range(2):
            group = [blocks[:, 4 * core + place] for place in range(4)]
            self.groups += group[:3] + [group[3][: self.half], group[3][self.half :]]


def across_kernel(counts, rows, half, *refs):
    arrays, (far_y, far_x, own, other, semaphores) = refs[:-5], refs[-5:]
    copies = load_sums(arrays, counts, 3 * rows, rows, own, other, semaphores)
    start_all(copies)
    wait_all(copies)
    for block in range(sum(map(sum, counts))):
        total = bf16(own[block].astype(FULL) + other[block].astype(FULL))
        if block < half:
            far_y[block] = total
        else:
            far_x[block - half] = total


def load_sums(arrays, counts, first, rows, own, other, semaphores):
    copies, running, index = [], 0, 0

    def load(target, start, size):
        source = arrays[index].at[:, pl.ds(first, rows)]
        copies.append(fetch(source, target.at[pl.ds(start, size)], semaphores.at[index]))

    for sizes in counts:
        load(own, running, sum(sizes))
        index += 1
        for size in sizes:
            load(other, running, size)
            index += 1
            running += size
    return copies


def along_xy_kernel(counts, rows, half, far_y, far_x, *refs):
    arrays, (to_x, to_y, own, other, semaphores) = refs[:-5], refs[-5:]
    copies = load_sums(arrays, counts, rows, 2 * rows, own, other, semaphores)
    start_all(copies)
    wait_all(copies)
    for block in range(sum(map(sum, counts))):
        total = own[block, :rows].astype(FULL) + other[block, :rows].astype(FULL)
        if block < half:
            total = total + far_y[block].astype(FULL)
        to_x[block] = bf16(total)
        total = own[block, rows:].astype(FULL) + other[block, rows:].astype(FULL)
        if block >= half:
            total = total + far_x[block - half].astype(FULL)
        to_y[block] = bf16(total)


def along_z_kernel(counts, rows, kinds, by_x, by_y, *refs):
    arrays, outs, (own, other, semaphores) = refs[:-7], refs[-7:-3], refs[-3:]
    copies = load_sums(arrays, counts, 0, rows, own, other, semaphores)
    start_all(copies)
    wait_all(copies)
    made = 0
    for block, (kind, depth) in enumerate(kinds):
        total = own[block].astype(FULL) + other[block].astype(FULL)
        total = total + by_x[block].astype(FULL) + by_y[block].astype(FULL)
        if kind == "long":
            step = outs[0].shape[1]
            for index in range(rows // step):
                part = total[index * step : (index + 1) * step]
                outs[depth][made + index] = part.astype(outs[depth].dtype)
            made += rows // step if depth == 3 else 0
        else:
            step = rows // 4
            for deep in range(4):
                part = total[deep * step : (deep + 1) * step]
                outs[deep][made] = part.astype(outs[deep].dtype)
            made += 1


class Scatter:
    def __init__(self, parts, count):
        self.parts, self.count = parts, count
        self.sizes = [[piece.shape[0] for piece in theirs] for _, theirs, _, _ in parts]
        self.blocks = sum(map(sum, self.sizes))
        self.half = self.blocks // 2
        self.rows, self.width = parts[0][0].shape[1] // 4, parts[0][0].shape[2]

    def move(self, array, mask):
        return swap(array, mask, self.count)

    def cores(self):
        self.held = []
        for mine, theirs, _, _ in self.parts:
            self.held += [mine] + [self.move(piece, 1) for piece in theirs]

    def call(self, kernel, extra, near, outs, length):
        return pl.pallas_call(
            kernel,
            in_specs=[VMEM_WHOLE] * len(near) + [IN_PLACE] * len(self.held),
            out_specs=[VMEM_WHOLE] * len(outs),
            out_shape=outs,
            scratch_shapes=[
                pltpu.VMEM((self.blocks, length, self.width), LOW),
                pltpu.VMEM((self.blocks, length, self.width), LOW),
                pltpu.SemaphoreType.DMA((len(self.held),)),
            ],
            cost_estimate=cost(4),
            compiler_params=pltpu.CompilerParams(vmem_limit_bytes=48 * 2**20),
        )(*near, *self.held)

    def make_far(self):
        self.to_far = self.call(
            functools.partial(across_kernel, self.sizes, self.rows, self.half),
            (),
            [],
            [
                shaped(LOW, self.half, self.rows, self.width),
                shaped(LOW, self.blocks - self.half, self.rows, self.width),
            ],
            self.rows,
        )

    def across(self):
        self.far = [self.move(self.to_far[0], 4), self.move(self.to_far[1], 2)]

    def make_near(self):
        self.to_near = self.call(
            functools.partial(along_xy_kernel, self.sizes, self.rows, self.half),
            (),
            self.far,
            [shaped(LOW, self.blocks, self.rows, self.width)] * 2,
            2 * self.rows,
        )

    def along_xy(self):
        self.near = [self.move(self.to_near[0], 2), self.move(self.to_near[1], 4)]

    def make_deep(self):
        kinds = []
        for _, _, short, long in self.parts:
            kinds += [("short", 0)] * short + [("long", depth) for depth in range(long)]
        shorts = sum(short for _, _, short, _ in self.parts)
        step, made = (self.rows // 4, self.blocks) if shorts else (self.rows, 1)
        outs = [shaped(FULL, made, step, self.width)]
        outs += [shaped(LOW, made, step, self.width)] * 3
        self.own, *self.to_deep = self.call(
            functools.partial(along_z_kernel, self.sizes, self.rows, kinds),
            (),
            self.near,
            outs,
            self.rows,
        )

    def along_z(self):
        self.deep = [self.move(part, mask) for part, mask in zip(self.to_deep, (8, 16, 24))]

    def result(self):
        total = self.own
        for part in self.deep:
            total = total + part.astype(FULL)
        return total


class PlainScatter(Scatter):
    def cores(self):
        pass

    make_far = across = make_near = along_xy = make_deep = along_z = cores

    def result(self):
        whole = []
        for mine, theirs, short, long in self.parts:
            full = jnp.concatenate([mine, jnp.concatenate(theirs)], axis=1)
            if short:
                whole.append(full[:short].reshape(short, self.count, -1, self.width))
            if long:
                whole.append(full[short:].reshape(1, self.count, -1, self.width))
        position = lax.axis_index("fsdp")
        order = range(self.count.bit_length() - 1)
        sums = scatter_sum(whole, order, position, self.count, LOW)
        rows = min(part.shape[1] for part in sums)
        return jnp.concatenate([part.reshape(-1, rows, self.width) for part in sums])


def order_of(places, position):
    device = jnp.arange(len(places))[:, None]
    return (device == (jnp.array(places)[None, :] ^ position)).astype(LOW)


def ordered(blocks, places, position):
    flat = dot(order_of(places, position), blocks.reshape(len(places), -1))
    return flat.astype(LOW).reshape(blocks.shape)


def gather_all(array, position, count, masks, between=None):
    blocks = array[None]
    places = [0]
    for step, mask in enumerate(masks):
        if step == 2 and between is not None:
            blocks = between(blocks)
        blocks = jnp.concatenate([blocks, swap(blocks, mask, count)], axis=0)
        places = places + [place ^ mask for place in places]
    return ordered(blocks, places, position)


def gather_and_turn(array, parts, position, count, between):
    blocks = array[None]
    places = [0]
    turned = ordered(parts, list(range(count)), position)
    rows = parts.shape[1]
    for bit in reversed(range(count.bit_length() - 1)):
        if bit == 2:
            blocks = between(blocks)
        halves = turned.reshape(-1, 2, 1 << bit, rows, 128)
        kept, sent = halves[:, 0], halves[:, 1]
        sent = jnp.concatenate([blocks.reshape(-1, 128), sent.reshape(-1, 128)])
        received = swap(sent, 1 << bit, count)
        size = blocks.shape[0] * blocks.shape[1]
        blocks = jnp.concatenate([blocks, received[:size].reshape(blocks.shape)])
        places = places + [place ^ (1 << bit) for place in places]
        turned = jnp.stack([kept, received[size:].reshape(kept.shape)], axis=1)
    turned = turned.reshape(parts.shape)
    return ordered(blocks, places, position), ordered(turned, list(range(count)), position)


def gather_and_sum(array, parts, position, count, between):
    blocks = array[None]
    all_bits = list(reversed(range(count.bit_length() - 1)))
    held = [(parts[None], all_bits)]
    fixed = {}

    def total(chosen):
        summed = None
        for part, bits in held:
            wanted = {bit: value for bit, value in chosen.items() if bit in bits}
            piece = pick(part, bits, wanted).astype(FULL)
            summed = piece if summed is None else summed + piece
        return summed

    for bit in range(count.bit_length() - 1):
        mine = bit_of(position, bit)
        piece = total({**fixed, bit: 1 - mine}).astype(LOW)
        sent = jnp.concatenate([blocks.reshape(-1, 128), piece.reshape(-1, 128)])
        if bit == 3:
            sent = between(sent)
        received = swap(sent, 1 << bit, count)
        size = blocks.shape[0] * blocks.shape[1]
        blocks = jnp.concatenate([blocks, received[:size].reshape(blocks.shape)])
        fixed[bit] = mine
        left = [other for other in all_bits if other not in fixed]
        held.append((received[size:].reshape(piece.shape), left))
    return blocks, total(fixed)[0, 0]


def sum_all(array, count):
    mask = 1
    while mask < count:
        array = array + swap(array, mask, count)
        mask *= 2
    return array


def split_high(values):
    return (values // 32).astype(jnp.bfloat16), (values % 32).astype(jnp.bfloat16)


def factored(weight, raw, row_old, col_old, row_square, col_square, row_old_sum, rows_all, clip):
    columns = weight.shape[-1]
    row_new = DECAY_RATE * row_old + (1.0 - DECAY_RATE) * (
        clip * (clip * (row_square / columns)) + FACTOR_EPS
    )
    col_new = DECAY_RATE * col_old + (1.0 - DECAY_RATE) * (
        clip * (clip * (col_square / rows_all)) + FACTOR_EPS
    )
    row_mean = (
        DECAY_RATE * row_old_sum
        + (1.0 - DECAY_RATE) * (clip * (clip * (jnp.sum(col_square) / columns)))
    ) / rows_all + (1.0 - DECAY_RATE) * FACTOR_EPS
    clipped = clip * raw
    estimate = row_new[:, None] * col_new[None, :] / row_mean
    return (weight - LEARN_RATE * clipped * lax.rsqrt(estimate), clipped, row_new, col_new)


def body(
    count,
    latents,
    targets,
    features,
    time_weights,
    timesteps,
    classes,
    block_in,
    block_in_rows,
    block_in_cols,
    block_down,
    block_down_rows,
    block_down_cols,
    stem_main,
    stem_main_rows,
    stem_main_cols,
    stem_proj,
    stem_proj_rows,
    stem_proj_cols,
    head_weight,
    head_rows,
    head_cols,
    biases,
    bias_second,
):
    position = lax.axis_index("fsdp")
    images = count * latents.shape[0]
    width_rows = block_in.shape[1]
    bias_part = biases.shape[0]
    bias_cols = -(-bias_part // width_rows)
    bits = count.bit_length() - 1
    gather = Gather if count == 32 else PlainGather
    scatter = Scatter if count == 32 else PlainScatter
    time_out_part, final_ada_part, table_part, patch_part, proj_one_part, time_in_part = cut_parts(
        stem_main, [D, 2 * D, NCLS, PD, P_SIZE, TF]
    )
    main_width = 3 * D + D + F
    main_blocks = main_width // D
    def blocks_of(part, width):
        return jnp.swapaxes(part.astype(LOW).reshape(part.shape[0], -1, width), 0, 1)

    one_part = jnp.pad(proj_one_part, ((0, 0), (0, 3 * D - P_SIZE)))
    layers = []
    for level in range(L):
        main = [blocks_of(block_in[level, :, :main_width], D)]
        if level == 0:
            main.append(blocks_of(one_part, D))
        down = block_down[level].astype(LOW).reshape(4, width_rows, D)
        wide = sum(part.shape[0] for part in main)
        layers.append(gather(jnp.concatenate(main + [down]), wide, count))
        layers[level].first_one = main_blocks
        layers[level].first_down = wide
    rest = gather(stem_proj.astype(LOW)[None], 0, count)

    time_high, time_low = split_high(timesteps)
    class_high, class_low = split_high(classes)
    small = jnp.concatenate(
        [
            biases.astype(LOW),
            patch_part.astype(LOW).reshape(-1),
            time_high,
            time_low,
            class_high,
            class_low,
        ]
    )
    used = small.shape[0]
    small = jnp.pad(small, (0, -used % 2048))
    head_size = small.shape[0]
    small = jnp.concatenate([small, time_in_part.astype(LOW).reshape(-1)])
    small = jnp.pad(small, (0, -small.shape[0] % 2048)).reshape(-1, 128)
    turned = jnp.swapaxes(time_out_part.astype(LOW).reshape(width_rows, count, width_rows), 0, 1)
    turned = turned.reshape(count, -1)
    turned_used = turned.shape[1]
    turned = jnp.pad(turned, ((0, 0), (0, -turned_used % 2048))).reshape(count, -1, 128)

    def start_gathers(blocks):
        blocks, layers[0].pack = meet(blocks, layers[0].pack)
        layers[0].along_z()
        return blocks

    small_all, time_out_mine = gather_and_turn(small, turned, position, count, start_gathers)
    small_all = small_all.reshape(count, -1)
    orders = Orders(position, count == 32)
    bias_full = small_all[:, :bias_part].reshape(-1).astype(FULL)
    patch_t = small_all[:, bias_part : used - 4].reshape(D, PD)
    marks = small_all[:, used - 4 : used].astype(jnp.int32)
    time_in = small_all[:, head_size : head_size + width_rows * TF].reshape(D, TF)
    time_out_mine = time_out_mine.reshape(count, -1)[:, :turned_used].reshape(D, width_rows)
    times_all = marks[:, 0] * 32 + marks[:, 1]
    classes_all = marks[:, 2] * 32 + marks[:, 3]
    block_bias = bias_full[: L * VB].reshape(L, VB // D, D)
    stem_bias = bias_full[L * VB :]
    bias_tin, bias_tout, bias_final, bias_patch, bias_one, bias_two, bias_three = cut_parts(
        stem_bias, [D, D, 2 * D, D, P_SIZE, P_SIZE, Z]
    )

    def mine(values):
        return lax.dynamic_slice_in_dim(values, position * width_rows, width_rows)

    freq_low = time_freq(times_all).astype(LOW)
    embed_hidden = dot_rows(time_in, freq_low) + bias_tin[:, None]
    embed_act = jax.nn.silu(embed_hidden).astype(LOW)
    one_hot = classes_all[:, None] == jnp.arange(NCLS)[None, :]
    class_embed = dot_rows(table_part.astype(LOW), one_hot.astype(LOW))
    condition = dot_tokens(time_out_mine, embed_act) + mine(bias_tout)[:, None] + class_embed
    cond_low = jax.nn.silu(condition).astype(LOW)

    ada_mine = jnp.concatenate(
        [block_in[level, :, 3 * D + D + F :] for level in range(L)] + [final_ada_part], axis=1
    ).astype(LOW)
    mod_part = dot_tokens(cond_low, ada_mine).reshape(1, images, -1, 128)
    before = {}
    if count == 32:

        def start_near(pieces):
            pieces, layers[0].quad = meet(pieces, layers[0].quad)
            layers[0].along_xy()
            return pieces

        before = {3: start_near}
    (mods,) = scatter_sum([mod_part], range(bits), position, count, FULL, before)
    mods, rest.pack = meet(mods, rest.pack)
    rest.along_z()
    mods = mods.reshape(-1)
    bias_ada = jnp.concatenate(
        [block_bias[level, 8:14].reshape(-1) for level in range(L)] + [bias_final]
    )
    mods = (mods + bias_ada).reshape(-1, D)

    latent_low = latents.reshape(TOK, PD).astype(jnp.bfloat16)
    hidden = (
        lax.dot_general(
            latent_low, patch_t, (((1,), (1,)), ((), ())), preferred_element_type=jnp.float32
        )
        + bias_patch
        + positions()
    )
    layers[0].across()
    if count == 32:
        rest.quad, layers[1].pack = meet(rest.quad, layers[1].pack)
        layers[0].far, rest.quad = meet(layers[0].far, rest.quad)
    rest.along_xy()
    layers[1].along_z()
    layers[0].finish()

    def forward(level, hidden):
        level_mods = mods[6 * level : 6 * level + 6]
        normed, packed, logs, attended, branch, middle = attn_forward(
            hidden, level_mods, block_bias[level], orders, layers[level]
        )
        kept_attn = [hidden, normed, packed, logs, attended, branch]
        if count == 32 and level == 1:
            middle, rest_sum.to_far = meet(middle, rest_sum.to_far)
            rest_sum.across()
        normed, slope, active, branch, hidden = mlp_forward(
            middle, level_mods, block_bias[level], orders, layers[level]
        )
        return hidden, kept_attn, [middle, normed, slope, active, branch]

    kept = [None] * L
    hidden, *kept[0] = forward(0, hidden)
    first_out = hidden
    if count == 32:
        hidden, rest.by_x, rest.by_y = meet(hidden, rest.by_x, rest.by_y)
        rest.across()
        rest.far, layers[1].quad = meet(rest.far, layers[1].quad)
    first_out = hidden
    layers[1].along_xy()
    rest.finish()
    (
        grad_first,
        cosine_part,
        grad_one,
        grad_two,
        grad_three,
        one_mine,
        one_theirs,
        rest_mine,
        *rest_theirs,
    ) = projector(
        first_out,
        features.reshape(TOK, Z),
        bias_one[None],
        bias_two[None],
        bias_three[None],
        orders,
        layers[0],
        rest,
    )
    layers[1].across()
    layers[1].finish()
    rest_sum = scatter([(rest_mine, rest_theirs, 0, 4)], count)
    rest_sum.cores()
    rest_sum.make_far()
    hidden, *kept[1] = forward(1, hidden)
    grad_hidden, grad_final_mods, grad_head, grad_head_bias, head_loss = head(
        hidden,
        mods[6 * L :],
        head_weight[:D].astype(LOW),
        head_weight[D:],
        targets.reshape(TOK, PD),
        time_weights.reshape(1, 1),
    )
    local_loss = head_loss[0, 0] + cosine_part[0, 0]
    grad_head_full = jnp.concatenate([grad_head, grad_head_bias], axis=0)

    bias_grads, mod_grads = [None] * L, [None] * L

    def backward(level, grad_hidden):
        level_mods = mods[6 * level : 6 * level + 6]
        grad_middle, mlp_mods, mlp_bias, mlp_mine, *mlp_theirs = mlp_backward(
            grad_hidden, level_mods, kept[level][1], orders, layers[level]
        )
        grad_hidden, attn_mods, attn_bias, attn_mine, *attn_theirs = attn_backward(
            grad_middle, level_mods, kept[level][0], orders, layers[level]
        )
        mod_grads[level] = jnp.concatenate([attn_mods, mlp_mods])
        bias_grads[level] = jnp.concatenate(
            [attn_bias, mlp_bias[:4], mod_grads[level], mlp_bias[4:]]
        ).reshape(-1)
        parts = [(attn_mine, attn_theirs, 4, 0), (mlp_mine, mlp_theirs, 4, 4)]
        return grad_hidden, parts

    rest_sum.make_near()
    rest_sum.along_xy()
    grad_hidden, parts = backward(1, grad_hidden)
    one_sum = scatter(parts + [(one_mine, [one_theirs], 3, 0)], count)
    one_sum.cores()
    one_sum.make_far()
    grad_hidden = grad_hidden + grad_first
    if count == 32:
        grad_hidden, one_sum.to_far, rest_sum.near = meet(
            grad_hidden, one_sum.to_far, rest_sum.near
        )
    one_sum.across()
    rest_sum.make_deep()
    rest_sum.along_z()
    grad_hidden, parts = backward(0, grad_hidden)
    zero_sum = scatter(parts, count)
    zero_sum.cores()
    zero_sum.make_far()
    one_sum.make_near()
    grad_patch = lax.dot_general(
        grad_hidden.astype(jnp.bfloat16),
        latent_low,
        (((0,), (0,)), ((), ())),
        preferred_element_type=jnp.float32,
    )
    grad_bias_all = jnp.concatenate(
        bias_grads
        + [
            jnp.zeros((2 * D,), jnp.float32),
            grad_final_mods.reshape(-1),
            total_rows(grad_hidden),
            grad_one.reshape(-1),
            grad_two.reshape(-1),
            grad_three.reshape(-1),
        ]
    )
    extra = jnp.concatenate(
        [grad_patch.reshape(count, -1), grad_bias_all.reshape(count, bias_part)], axis=1
    )
    grad_mods = jnp.concatenate(mod_grads + [grad_final_mods]).astype(LOW).reshape(-1, 128)
    mod_rows = grad_mods.shape[0]
    grad_mods = jnp.pad(grad_mods, ((0, -mod_rows % 16), (0, 0)))
    extra = jnp.pad(extra, ((0, 0), (0, -extra.shape[1] % 2048))).reshape(count, -1, 128)
    if count == 32:
        grad_mods, one_sum.to_near = meet(grad_mods, one_sum.to_near)
    one_sum.along_xy()

    def start_far(sent):
        if count == 32:
            sent, one_sum.near, zero_sum.to_far = meet(sent, one_sum.near, zero_sum.to_far)
        zero_sum.across()
        return sent

    grad_mods_all, extra = gather_and_sum(grad_mods, extra, position, count, start_far)
    grad_mods_all = grad_mods_all[:, :mod_rows].reshape(images, -1)
    turned = order_of(list(range(count)), position)
    cond_turned = dot(cond_low, turned).astype(LOW)
    extra = extra.reshape(-1)
    patch_shard = extra[: width_rows * PD].reshape(width_rows, PD)
    bias_shard = extra[width_rows * PD : width_rows * PD + bias_part]

    grad_ada_mine = dot(cond_turned, grad_mods_all)
    grad_cond_mine = jnp.dot(
        dot_rows(ada_mine, grad_mods_all),
        turned.astype(FULL),
        precision=lax.Precision.HIGHEST,
    )
    grad_condition = silu_back(condition, grad_cond_mine)
    grad_table = jnp.dot(
        grad_condition, one_hot.astype(jnp.float32), precision=lax.Precision.HIGHEST
    )
    grad_condition_low = grad_condition.astype(LOW)

    one_sum.make_deep()
    zero_sum.make_near()

    def between(blocks):
        if count == 32:
            blocks, one_sum.to_deep, zero_sum.to_near = meet(
                blocks, one_sum.to_deep, zero_sum.to_near
            )
        one_sum.along_z()
        zero_sum.along_xy()
        return blocks

    masks = [1 << bit for bit in range(3, bits)] + [4, 2, 1]
    grad_condition_low = gather_all(grad_condition_low, position, count, masks, between)
    grad_condition_low = grad_condition_low.reshape(D, images)
    grad_time_out = dot_rows(mine(embed_act), grad_condition_low)
    grad_embed_act = dot(time_out_part.astype(LOW), grad_condition_low)
    grad_embed = silu_back(mine(embed_hidden), grad_embed_act)
    grad_time_in = dot(grad_embed.astype(LOW), freq_low)
    zero_sum.make_deep()
    zero_sum.along_z()
    late_bias = jnp.zeros((2, D), jnp.float32)
    late_bias = lax.dynamic_update_slice(
        late_bias,
        jnp.stack([jnp.sum(grad_embed, axis=1), jnp.sum(grad_condition, axis=1)]),
        (0, position * width_rows),
    )

    def side_by_side(blocks):
        return jnp.swapaxes(blocks, 0, 1).reshape(blocks.shape[1], -1)

    shards = [zero_sum.result(), one_sum.result()]
    ada_zero, ada_one, grad_final_ada = cut_parts(grad_ada_mine, [6 * D, 6 * D, 2 * D])
    raw_in = jnp.stack(
        [
            jnp.concatenate(
                [side_by_side(shards[level][:8]), ada], axis=1
            )
            for level, ada in enumerate([ada_zero, ada_one])
        ]
    )
    raw_down = jnp.stack([shards[0][8:].reshape(-1, D), shards[1][8:12].reshape(-1, D)])
    raw_main = jnp.concatenate(
        [
            grad_time_out,
            grad_final_ada,
            grad_table,
            patch_shard,
            side_by_side(shards[1][12:])[:, :P_SIZE],
            grad_time_in,
        ],
        axis=1,
    )
    raw_proj = rest_sum.result()[0]
    raws = [raw_in[0], raw_in[1], raw_down[0], raw_down[1], raw_main, raw_proj]
    row_olds = [
        block_in_rows[0],
        block_in_rows[1],
        block_down_rows[0],
        block_down_rows[1],
        stem_main_rows,
        stem_proj_rows,
    ]
    squares = [raw * raw for raw in raws]
    row_squares = [jnp.sum(square, axis=1) for square in squares]
    late_list = [jnp.sum(square, axis=0) for square in squares] + [
        jnp.stack([jnp.sum(row_old) for row_old in row_olds]),
        jnp.stack([jnp.sum(bias_shard * bias_shard), local_loss]),
        late_bias.reshape(-1),
        grad_head_full.reshape(-1),
    ]
    late_sizes = [values.shape[0] for values in late_list]
    late_all = jnp.concatenate(late_list)
    late_all = jnp.pad(late_all, (0, -late_all.shape[0] % 1024)).reshape(-1, 128)
    late_all = sum_all(late_all, count).reshape(-1)
    late_sums = []
    running = 0
    for size in late_sizes:
        late_sums.append(late_all[running : running + size])
        running += size
    col_squares = late_sums[:6]
    row_old_sums, bias_loss, late_bias, head_sum = late_sums[6:]
    head_sum = head_sum.reshape(D + 1, PD)
    loss_total = bias_loss[1]
    total_square = bias_loss[0] + jnp.sum(late_bias * late_bias) + jnp.sum(head_sum * head_sum)
    for col_square in col_squares:
        total_square = total_square + jnp.sum(col_square)
    grad_norm = jnp.sqrt(total_square)
    clip = jnp.minimum(1.0, CLIP_LIMIT / grad_norm)

    olds = [block_in[0], block_in[1], block_down[0], block_down[1], stem_main, stem_proj]
    col_olds = [
        block_in_cols[0],
        block_in_cols[1],
        block_down_cols[0],
        block_down_cols[1],
        stem_main_cols,
        stem_proj_cols,
    ]
    results = [
        factored(
            olds[slot],
            raws[slot],
            row_olds[slot],
            col_olds[slot],
            row_squares[slot],
            col_squares[slot],
            row_old_sums[slot],
            count * olds[slot].shape[0],
            clip,
        )
        for slot in range(6)
    ]
    new_in, clip_in, rows_in, cols_in = [
        jnp.stack([results[0][part], results[1][part]]) for part in range(4)
    ]
    new_down, clip_down, rows_down, cols_down = [
        jnp.stack([results[2][part], results[3][part]]) for part in range(4)
    ]
    new_main, clip_main, rows_main, cols_main = results[4]
    new_proj, clip_proj, rows_proj, cols_proj = results[5]
    head_square = head_sum * head_sum
    new_head, head_clip, rows_head, cols_head = factored(
        head_weight,
        head_sum,
        head_rows,
        head_cols,
        jnp.sum(head_square, axis=1),
        jnp.sum(head_square, axis=0),
        jnp.sum(head_rows),
        D + 1,
        clip,
    )
    late_flat = jnp.zeros((count * bias_part,), jnp.float32)
    late_flat = lax.dynamic_update_slice(late_flat, late_bias, (L * VB,))
    bias_raw = bias_shard + lax.dynamic_slice(late_flat, (position * bias_part,), (bias_part,))
    clip_bias = clip * bias_raw
    second_new = DECAY_RATE * bias_second + (1.0 - DECAY_RATE) * (
        clip_bias * clip_bias + FACTOR_EPS
    )
    new_bias = biases - LEARN_RATE * clip_bias * lax.rsqrt(second_new)
    return (
        loss_total,
        grad_norm,
        new_in,
        clip_in,
        rows_in,
        cols_in,
        new_in.astype(jnp.bfloat16),
        new_down,
        clip_down,
        rows_down,
        cols_down,
        new_down.astype(jnp.bfloat16),
        new_main,
        clip_main,
        rows_main,
        cols_main,
        new_main.astype(jnp.bfloat16),
        new_proj,
        clip_proj,
        rows_proj,
        cols_proj,
        new_proj.astype(jnp.bfloat16),
        new_head,
        head_clip,
        rows_head,
        cols_head,
        new_bias,
        clip_bias,
        second_new,
    )


def solution(mesh):
    return jax.shard_map(
        functools.partial(body, mesh.shape["fsdp"]),
        mesh=mesh,
        in_specs=(
            P("fsdp", None, None),
            P("fsdp", None, None),
            P("fsdp", None, None),
            P("fsdp"),
            P("fsdp"),
            P("fsdp"),
            P(None, "fsdp", None),
            P(None, "fsdp"),
            P(),
            P(None, "fsdp", None),
            P(None, "fsdp"),
            P(),
            P("fsdp", None),
            P("fsdp"),
            P(),
            P("fsdp", None),
            P("fsdp"),
            P(),
            P(),
            P(),
            P(),
            P("fsdp"),
            P("fsdp"),
        ),
        out_specs=(
            P(),
            P(),
            P(None, "fsdp", None),
            P(None, "fsdp", None),
            P(None, "fsdp"),
            P(),
            P(None, "fsdp", None),
            P(None, "fsdp", None),
            P(None, "fsdp", None),
            P(None, "fsdp"),
            P(),
            P(None, "fsdp", None),
            P("fsdp", None),
            P("fsdp", None),
            P("fsdp"),
            P(),
            P("fsdp", None),
            P("fsdp", None),
            P("fsdp", None),
            P("fsdp"),
            P(),
            P("fsdp", None),
            P(),
            P(),
            P(),
            P(),
            P("fsdp"),
            P("fsdp"),
            P("fsdp"),
        ),
        check_vma=False,
    )
```

time: 1170 us -> 860 us (0.74)
  waiting for transfers between devices: 594 us -> 330 us
  Pallas kernels: 0 us -> 174 us
  matrix products: 186 us -> 13.8 us
  other arithmetic: 153 us -> 65.7 us
  starting transfers between devices: 32.2 us -> 84.8 us
  between operations: 38.1 us -> 23.5 us
    all_gather x7 -> x0, waiting for transfers between devices: 265 us -> none  [the longest x2 109 us: body(): lax.all_gather(block_in[level, :, :main_width].astype(jnp.bfloat16), 'fsd...]
    pallas_call x0 -> x20, Pallas kernels: none -> 174 us  [the longest x10 128 us: call(): pl.pallas_call(kernel, in_specs=[VMEM_WHOLE] * len(inputs) + [IN_PLACE] *...]
    dot_general x62 -> x17, matrix products: 186 us -> 13.8 us  [the longest x7 5.38 us: dot(): return jnp.dot(left, right, preferred_element_type=jnp.float32)]
    ppermute x50 -> x99, starting transfers between devices: 32 us -> 84.8 us  [swap(): lax.ppermute(array, 'fsdp', [(place, place ^ mask) for place in range(cou...]
    convert_element_type x33 -> x6, other arithmetic: 49.4 us -> 0.32 us  [the longest x1 0.18 us: time_freq(): angles = timesteps.astype(jnp.float32)[:, None] * freq_rate[None, :]]
    unnamed x700 -> x438, local copies, waits for them, and re-layouts: 21.3 us -> 63.5 us
    convert_element_type x41 -> x5, local copies, waits for them, and re-layouts: 41.3 us -> 0.3 us  [the longest x1 0.15 us: body(): bias_full = small_all[:, :bias_part].reshape(-1).astype(FULL)]
    slice x10 -> x59, local copies, waits for them, and re-layouts: 3.06 us -> 27 us  [the longest x10 5.29 us: merged(): long = [pack[self.wide:].reshape(1, -1, width) for pack in packs]]
  transfers between devices with their start and end apart: 57 -> 99, of which waited for: 37 -> 42; matrix products, arithmetic and copies ran while one was open for 38% -> 17% of each run, Pallas kernels for 0% -> 17%
where the time goes in v2:
time: 860 us; the launch traced here: 851 us
  waiting for transfers between devices  330 us (38%)
  Pallas kernels  174 us (20%)
  local copies, waits for them, and re-layouts  159 us (18%)
  starting transfers between devices  84.8 us (10%)
  other arithmetic  65.7 us (8%)
  between operations  23.5 us (3%)
  matrix products  13.8 us (2%)
    ppermute x99, waiting for transfers between devices, swap(): lax.ppermute(array, 'fsdp', [(place, place ^ mask) for place in range(cou...  330 us
    pallas_call x10, Pallas kernels, call(): pl.pallas_call(kernel, in_specs=[VMEM_WHOLE] * len(inputs) + [IN_PLACE] *...  128 us
    ppermute x99, starting transfers between devices, swap(): lax.ppermute(array, 'fsdp', [(place, place ^ mask) for place in range(cou...  84.8 us
    unnamed x438, local copies, waits for them, and re-layouts  63.5 us
    pallas_call x9, Pallas kernels, call(): pl.pallas_call(kernel, in_specs=[VMEM_WHOLE] * len(near) + [IN_PLACE] * l...  45.2 us
  transfers between devices with their start and end apart: 99, of which 42 were waited for; matrix products, arithmetic and copies ran while one was open for 17% of the time, Pallas kernels for 17%

profile of v2, /device:TPU:0, one launch (start us, length us, event | category | flops | bytes accessed | tf_op | source)
XLA Modules:
  0.0 850.9 jit_solution(10141183229178482371)
XLA Ops:
  38.2 31.2 %collective-permute-done.9 = bf16[15,24,768]{2,1,0:T(8,128)(2,1)S(1)} collective-permute-done((bf16[15,24,768]{2,1,0:T(8,128)(2,1)S(1)}, bf16[15,24,768]{2,1,0:T(8,128)(2,1)S(1)}, u32[]{:S(2)}, u32[]{:S(2)}) %collective-permute-start.9) | collective-permute-done | bytes 552992 | tf_op jit(solution)/shard_map/ppermute | solution.py:773
  91.9 6.6 collective-permute-done.6
  129.2 8.9 %collective-permute-done.19 = bf16[1,64,2816]{2,1,0:T(8,128)(2,1)S(1)} collective-permute-done((bf16[1,64,2816]{2,1,0:T(8,128)(2,1)}, bf16[1,64,2816]{2,1,0:T(8,128)(2,1)S(1)}, u32[]{:S(2)}, u32[]{:S(2)}) %collective-permute-start.19) | collective-permute-done | bytes 360480 | tf_op jit(solution)/shard_map/ppermute | solution.py:773
  138.1 18.0 %collective-permute-done.13.refs_1_ = bf16[15,96,768]{2,1,0:T(8,128)(2,1)} collective-permute-done((bf16[15,96,768]{2,1,0:T(8,128)(2,1)S(1)}, bf16[15,96,768]{2,1,0:T(8,128)(2,1)}, u32[]{:S(2)}, u32[]{:S(2)}) %collective-permute-start.13) | collective-permute-done | bytes 2211872 | tf_op jit(solution)/shard_map/ppermute | solution.py:773
  195.5 19.6 %collective-permute-done.30 = bf16[12,24,768]{2,1,0:T(8,128)(2,1)} collective-permute-done((bf16[12,24,768]{2,1,0:T(8,128)(2,1)}, bf16[12,24,768]{2,1,0:T(8,128)(2,1)}, u32[]{:S(2)}, u32[]{:S(2)}) %collective-permute-start.30) | collective-permute-done | bytes 442400 | tf_op jit(solution)/shard_map/ppermute | solution.py:773
  229.8 11.1 %shard_map.492 = (bf16[256,768]{1,0:T(8,128)(2,1)S(1)}, bf16[3,256,768]{2,1,0:T(8,128)(2,1)S(1)}, f32[256,128]{1,0:T(8,128)S(1)}, bf16[256,768]{1,0:T(8,128)(2,1...) custom-call(f32[256,768]{1,0:T(8,128)S(1)} %copy-done.33, f32[6,768]{1,0:T(8,128)S(1)} %get-tuple-element.528.mods, ...), custom_call_target="tpu_custom_call" | custom-call | flops 11 | tf_op jit(solution)/shard_map/pallas_call | solution.py:570
  245.1 10.9 %shard_map.493 = (bf16[256,768]{1,0:T(8,128)(2,1)S(1)}, bf16[4,256,768]{2,1,0:T(8,128)(2,1)S(1)}, bf16[4,256,768]{2,1,0:T(8,128)(2,1)S(1)}, f32[256,768]{1,0:T(8,128)S(1)}, f32[256,768]{1,0:T(8,128)S(1)}) custom-call(f32[256,768]{1,0:T(8,128)S(1)} %get-tuple-element.172.middle, f32[6,768]{1,0:T(8,128)S(1)} %get-tuple-element.528.mods, ...), custom_call_target="tpu_custom_call" | custom-call | flops 11 | tf_op jit(solution)/shard_map/pallas_call | solution.py:570
  268.5 9.5 %collective-permute-done.27.refs_13_ = bf16[2,64,2816]{2,1,0:T(8,128)(2,1)S(1)} collective-permute-done((bf16[2,64,2816]{2,1,0:T(8,128)(2,1)S(1)}, bf16[2,64,2816]{2,1,0:T(8,128)(2,1)S(1)}, u32[]{:S(2)}, u32[]{:S(2)}) %collective-permute-start.27) | collective-permute-done | bytes 720928 | tf_op jit(solution)/shard_map/ppermute | solution.py:773
  286.0 27.0 %shard_map.495 = (f32[256,768]{1,0:T(8,128)}, f32[8,128]{1,0:T(8,128)}, f32[1,2048]{1,0:T(1,128)}, f32[1,2048]{1,0:T(1,128)}, f32[1,768]{1,0:T(1,128)}, /*index=...) custom-call(f32[256,768]{1,0:T(8,128)} %copy-done.35, ...), custom_call_target="tpu_custom_call" | custom-call | flops 27 | tf_op jit(solution)/shard_map/pallas_call | solution.py:570
  330.6 12.9 %collective-permute-done.34.refs_3_ = bf16[6,96,768]{2,1,0:T(8,128)(2,1)} collective-permute-done((bf16[6,96,768]{2,1,0:T(8,128)(2,1)S(1)}, bf16[6,96,768]{2,1,0:T(8,128)(2,1)}, u32[]{:S(2)}, u32[]{:S(2)}) %collective-permute-start.34) | collective-permute-done | bytes 884768 | tf_op jit(solution)/shard_map/ppermute | solution.py:773
  358.8 11.1 %shard_map.494 = (bf16[256,768]{1,0:T(8,128)(2,1)S(1)}, bf16[3,256,768]{2,1,0:T(8,128)(2,1)S(1)}, f32[256,128]{1,0:T(8,128)S(1)}, bf16[256,768]{1,0:T(8,128)(2,1...) custom-call(f32[256,768]{1,0:T(8,128)S(1)} %copy-done.36, f32[6,768]{1,0:T(8,128)S(1)} %get-tuple-element.527.mods, ...), custom_call_target="tpu_custom_call" | custom-call | flops 11 | tf_op jit(solution)/shard_map/pallas_call | solution.py:570
  381.1 10.5 %shard_map.497 = (bf16[256,768]{1,0:T(8,128)(2,1)S(1)}, bf16[4,256,768]{2,1,0:T(8,128)(2,1)S(1)}, bf16[4,256,768]{2,1,0:T(8,128)(2,1)S(1)}, f32[256,768]{1,0:T(8,128)S(1)}, f32[256,768]{1,0:T(8,128)S(1)}) custom-call(f32[256,768]{1,0:T(8,128)S(1)} %copy-done.41, f32[6,768]{1,0:T(8,128)S(1)} %get-tuple-element.527.mods, f32[15,768]{1,0:T(8,128)S(1)} %slice.459.bias, ...), custom_call_target="tpu_custom_call" | custom-call | flops 11 | tf_op jit(solution)/shard_map/pallas_call | solution.py:570
  396.7 15.4 %shard_map.499 = (f32[256,768]{1,0:T(8,128)S(1)}, f32[3,768]{1,0:T(4,128)S(1)}, f32[5,768]{1,0:T(8,128)S(1)}, bf16[8,384,768]{2,1,0:T(8,128)(2,1)}, bf16[2,384,7...) custom-call(f32[256,768]{1,0:T(8,128)S(1)} %get-tuple-element.194.gr, ...), custom_call_target="tpu_custom_call" | custom-call | flops 16 | tf_op jit(solution)/shard_map/pallas_call | solution.py:570
  414.2 13.2 %shard_map.500 = (f32[256,768]{1,0:T(8,128)S(1)}, f32[3,768]{1,0:T(4,128)S(1)}, f32[4,768]{1,0:T(4,128)S(1)}, bf16[4,384,768]{2,1,0:T(8,128)(2,1)}, bf16[2,384,7...) custom-call(f32[256,768]{1,0:T(8,128)S(1)} %get-tuple-element.199.grad_middle, ...), custom_call_target="tpu_custom_call" | custom-call | flops 13 | tf_op jit(solution)/shard_map/pallas_call | solution.py:570
  429.7 16.8 %collective-permute-done.58.far_x = bf16[2,64,2816]{2,1,0:T(8,128)(2,1)S(1)} collective-permute-done((bf16[2,64,2816]{2,1,0:T(8,128)(2,1)S(1)}, bf16[2,64,2816]{2,1,0:T(8,128)(2,1)S(1)}, u32[]{:S(2)}, u32[]{:S(2)}) %collective-permute-start.58) | collective-permute-done | bytes 720928 | tf_op jit(solution)/shard_map/ppermute | solution.py:773
  466.5 19.3 %collective-permute-done.59.by_x = bf16[4,64,2816]{2,1,0:T(8,128)(2,1)} collective-permute-done((bf16[4,64,2816]{2,1,0:T(8,128)(2,1)}, bf16[4,64,2816]{2,1,0:T(8,128)(2,1)}, u32[]{:S(2)}, u32[]{:S(2)}) %collective-permute-start.59) | collective-permute-done | bytes 1441824 | tf_op jit(solution)/shard_map/ppermute | solution.py:773
  487.1 15.0 %shard_map.503 = (f32[256,768]{1,0:T(8,128)S(1)}, f32[3,768]{1,0:T(4,128)S(1)}, f32[5,768]{1,0:T(8,128)S(1)}, bf16[8,384,768]{2,1,0:T(8,128)(2,1)}, bf16[2,384,7...) custom-call(f32[256,768]{1,0:T(8,128)S(1)} %add.1020.grad_out, ...), custom_call_target="tpu_custom_call" | custom-call | flops 16 | tf_op jit(solution)/shard_map/pallas_call | solution.py:570
  503.6 13.2 %shard_map.504 = (f32[256,768]{1,0:T(8,128)S(1)}, f32[3,768]{1,0:T(4,128)S(1)}, f32[4,768]{1,0:T(4,128)S(1)}, bf16[4,384,768]{2,1,0:T(8,128)(2,1)}, bf16[2,384,7...) custom-call(f32[256,768]{1,0:T(8,128)S(1)} %get-tuple-element.228.grad_middle, ...), custom_call_target="tpu_custom_call" | custom-call | flops 13 | tf_op jit(solution)/shard_map/pallas_call | solution.py:570
  541.2 8.2 shard_map.505
  569.6 32.3 %collective-permute-done.64 = bf16[320,128]{1,0:T(8,128)(2,1)S(1)} collective-permute-done((bf16[320,128]{1,0:T(8,128)(2,1)S(1)}, bf16[320,128]{1,0:T(8,128)(2,1)S(1)}, u32[]{:S(2)}, u32[]{:S(2)}) %collective-permute-start.64) | collective-permute-done | bytes 81952 | tf_op jit(solution)/shard_map/ppermute | solution.py:773
  609.2 11.2 %collective-permute-done.74 = bf16[800,128]{1,0:T(8,128)(2,1)S(1)} collective-permute-done((bf16[800,128]{1,0:T(8,128)(2,1)S(1)}, bf16[800,128]{1,0:T(8,128)(2,1)S(1)}, u32[]{:S(2)}, u32[]{:S(2)}) %collective-permute-start.74) | collective-permute-done | bytes 204832 | tf_op jit(solution)/shard_map/ppermute | solution.py:773
  651.5 7.2 shard_map.508
  686.7 33.7 %collective-permute-done.86 = bf16[15,24,768]{2,1,0:T(8,128)(2,1)} collective-permute-done((bf16[15,24,768]{2,1,0:T(8,128)(2,1)S(1)}, bf16[15,24,768]{2,1,0:T(8,128)(2,1)}, u32[]{:S(2)}, u32[]{:S(2)}) %collective-permute-start.86) | collective-permute-done | bytes 552992 | tf_op jit(solution)/shard_map/ppermute | solution.py:773
  743.9 23.2 %collective-permute-done.83 = bf16[12,24,768]{2,1,0:T(8,128)(2,1)} collective-permute-done((bf16[12,24,768]{2,1,0:T(8,128)(2,1)S(1)}, bf16[12,24,768]{2,1,0:T(8,128)(2,1)}, u32[]{:S(2)}, u32[]{:S(2)}) %collective-permute-start.83) | collective-permute-done | bytes 442400 | tf_op jit(solution)/shard_map/ppermute | solution.py:773
  (946 shorter events, 441.3 us)
Async XLA Ops:
  23.4 46.0 %collective-permute-start.9 = (bf16[15,24,768]{2,1,0:T(8,128)(2,1)S(1)}, bf16[15,24,768]{2,1,0:T(8,128)(2,1)S(1)}, u32[]{:S(2)}, u32[]{:S(2)}) collective-permute-start(bf16[15,24,768]{2,1,0:T(8,128)(2,1)S(1)} %pad_maximum_fusion.7), channel_id=1, source_target_pairs={{0,16},{1,17},{2,18},{3,19},{4,20},{5,21},{6,22},{7,23},{8,24},{9,... | collective-permute-start | bytes 1658888 | tf_op jit(solution)/shard_map/ppermute | solution.py:773
  23.4 55.6 %collective-permute-start.8 = (bf16[15,24,768]{2,1,0:T(8,128)(2,1)S(1)}, bf16[15,24,768]{2,1,0:T(8,128)(2,1)}, u32[]{:S(2)}, u32[]{:S(2)}) collective-permute-start(bf16[15,24,768]{2,1,0:T(8,128)(2,1)S(1)} %pad_maximum_fusion.7), channel_id=1, source_target_pairs={{0,8},{1,9},{2,10},{3,11},{4,12},{5,13},{6,14},{7,15},{8,0},{9,1},... | collective-permute-start | bytes 1658888 | tf_op jit(solution)/shard_map/ppermute | solution.py:773
  107.2 48.9 %collective-permute-start.13 = (bf16[15,96,768]{2,1,0:T(8,128)(2,1)S(1)}, bf16[15,96,768]{2,1,0:T(8,128)(2,1)}, u32[]{:S(2)}, u32[]{:S(2)}) collective-permute-start(bf16[15,96,768]{2,1,0:T(8,128)(2,1)S(1)} %bitcast_dynamic-update-slice_fusion.4.refs_0_), channel_id=1, source_target_pairs={{0,2},{1,3},{2,0},{3,1},{4,6},{5,7},{6,4},{7,5},{8,10},{9,11},{10,... | collective-permute-start | bytes 6635528 | tf_op jit(solution)/shard_map/ppermute | solution.py:773
  108.7 52.7 %collective-permute-start.14 = (bf16[15,96,768]{2,1,0:T(8,128)(2,1)S(1)}, bf16[15,96,768]{2,1,0:T(8,128)(2,1)}, u32[]{:S(2)}, u32[]{:S(2)}) collective-permute-start(bf16[15,96,768]{2,1,0:T(8,128)(2,1)S(1)} %bitcast_dynamic-update-slice_fusion.4.refs_0_), channel_id=1, source_target_pairs={{0,4},{1,5},{2,6},{3,7},{4,0},{5,1},{6,2},{7,3},{8,12},{9,13},{10,... | collective-permute-start | bytes 6635528 | tf_op jit(solution)/shard_map/ppermute | solution.py:773
  127.2 39.5 %collective-permute-start.17 = (bf16[1,64,2816]{2,1,0:T(8,128)(2,1)}, bf16[1,64,2816]{2,1,0:T(8,128)(2,1)}, u32[]{:S(2)}, u32[]{:S(2)}) collective-permute-start(bf16[1,64,2816]{2,1,0:T(8,128)(2,1)} %convert_bitcast_fusion), channel_id=1, source_target_pairs={{0,8},{1,9},{2,10},{3,11},{4,12},{5,13},{6,14},{7,15},{8,0},{9,1},... | collective-permute-start | bytes 1081352 | tf_op jit(solution)/shard_map/ppermute | solution.py:773
  138.1 86.2 %collective-permute-start.20 = (bf16[15,96,768]{2,1,0:T(8,128)(2,1)S(1)}, bf16[15,96,768]{2,1,0:T(8,128)(2,1)}, u32[]{:S(2)}, u32[]{:S(2)}) collective-permute-start(bf16[15,96,768]{2,1,0:T(8,128)(2,1)S(1)} %bitcast_dynamic-update-slice_fusion.4.refs_0_), channel_id=1, source_target_pairs={{0,1},{1,0},{2,3},{3,2},{4,5},{5,4},{6,7},{7,6},{8,9},{9,8},{10,11... | collective-permute-start | bytes 6635528 | tf_op jit(solution)/shard_map/ppermute | solution.py:773
  156.1 68.2 %collective-permute-start.21 = (bf16[15,96,768]{2,1,0:T(8,128)(2,1)}, bf16[15,96,768]{2,1,0:T(8,128)(2,1)}, u32[]{:S(2)}, u32[]{:S(2)}) collective-permute-start(bf16[15,96,768]{2,1,0:T(8,128)(2,1)} %collective-permute-done.13.refs_1_), channel_id=1, source_target_pairs={{0,1},{1,0},{2,3},{3,2},{4,5},{5,4},{6,7},{7,6},{8,9},{9,8},{10,11... | collective-permute-start | bytes 6635528 | tf_op jit(solution)/shard_map/ppermute | solution.py:773
  183.4 46.3 %collective-permute-start.22 = (bf16[15,96,768]{2,1,0:T(8,128)(2,1)}, bf16[15,96,768]{2,1,0:T(8,128)(2,1)}, u32[]{:S(2)}, u32[]{:S(2)}) collective-permute-start(bf16[15,96,768]{2,1,0:T(8,128)(2,1)} %collective-permute-done.14.refs_2_), channel_id=1, source_target_pairs={{0,1},{1,0},{2,3},{3,2},{4,5},{5,4},{6,7},{7,6},{8,9},{9,8},{10,11... | collective-permute-start | bytes 6635528 | tf_op jit(solution)/shard_map/ppermute | solution.py:773
  215.1 43.0 %collective-permute-start.25 = (bf16[4,64,2816]{2,1,0:T(8,128)(2,1)}, bf16[4,64,2816]{2,1,0:T(8,128)(2,1)}, u32[]{:S(2)}, u32[]{:S(2)}) collective-permute-start(bf16[4,64,2816]{2,1,0:T(8,128)(2,1)} %pad_maximum_fusion.3.refs_10_), channel_id=1, source_target_pairs={{0,2},{1,3},{2,0},{3,1},{4,6},{5,7},{6,4},{7,5},{8,10},{9,11},{10,... | collective-permute-start | bytes 4325384 | tf_op jit(solution)/shard_map/ppermute | solution.py:773
  215.6 42.5 %collective-permute-start.26 = (bf16[4,64,2816]{2,1,0:T(8,128)(2,1)}, bf16[4,64,2816]{2,1,0:T(8,128)(2,1)}, u32[]{:S(2)}, u32[]{:S(2)}) collective-permute-start(bf16[4,64,2816]{2,1,0:T(8,128)(2,1)} %pad_maximum_fusion.3.refs_10_), channel_id=1, source_target_pairs={{0,4},{1,5},{2,6},{3,7},{4,0},{5,1},{6,2},{7,3},{8,12},{9,13},{10,... | collective-permute-start | bytes 4325384 | tf_op jit(solution)/shard_map/ppermute | solution.py:773
  280.5 39.5 %collective-permute-start.33 = (bf16[12,96,768]{2,1,0:T(8,128)(2,1)S(1)}, bf16[12,96,768]{2,1,0:T(8,128)(2,1)}, u32[]{:S(2)}, u32[]{:S(2)}) collective-permute-start(bf16[12,96,768]{2,1,0:T(8,128)(2,1)S(1)} %bitcast_dynamic-update-slice_fusion.refs_0_), channel_id=1, source_target_pairs={{0,4},{1,5},{2,6},{3,7},{4,0},{5,1},{6,2},{7,3},{8,12},{9,13},{10,... | collective-permute-start | bytes 5308424 | tf_op jit(solution)/shard_map/ppermute | solution.py:773
  281.7 40.7 %collective-permute-start.32 = (bf16[12,96,768]{2,1,0:T(8,128)(2,1)S(1)}, bf16[12,96,768]{2,1,0:T(8,128)(2,1)}, u32[]{:S(2)}, u32[]{:S(2)}) collective-permute-start(bf16[12,96,768]{2,1,0:T(8,128)(2,1)S(1)} %bitcast_dynamic-update-slice_fusion.refs_0_), channel_id=1, source_target_pairs={{0,2},{1,3},{2,0},{3,1},{4,6},{5,7},{6,4},{7,5},{8,10},{9,11},{10,... | collective-permute-start | bytes 5308424 | tf_op jit(solution)/shard_map/ppermute | solution.py:773
  282.3 41.9 %collective-permute-start.36 = (bf16[12,96,768]{2,1,0:T(8,128)(2,1)S(1)}, bf16[12,96,768]{2,1,0:T(8,128)(2,1)S(1)}, u32[]{:S(2)}, u32[]{:S(2)}) collective-permute-start(bf16[12,96,768]{2,1,0:T(8,128)(2,1)S(1)} %bitcast_dynamic-update-slice_fusion.refs_0_), channel_id=1, source_target_pairs={{0,1},{1,0},{2,3},{3,2},{4,5},{5,4},{6,7},{7,6},{8,9},{9,8},{10,11... | collective-permute-start | bytes 5308424 | tf_op jit(solution)/shard_map/ppermute | solution.py:773
  349.9 104.2 %collective-permute-start.56 = (bf16[3,384,768]{2,1,0:T(8,128)(2,1)}, bf16[3,384,768]{2,1,0:T(8,128)(2,1)}, u32[]{:S(2)}, u32[]{:S(2)}) collective-permute-start(bf16[3,384,768]{2,1,0:T(8,128)(2,1)} %get-tuple-element.216), channel_id=1, source_target_pairs={{0,1},{1,0},{2,3},{3,2},{4,5},{5,4},{6,7},{7,6},{8,9},{9,8},{10,11... | collective-permute-start | bytes 5308424 | tf_op jit(solution)/shard_map/ppermute | solution.py:773
  374.9 53.4 %collective-permute-start.57 = (bf16[2,64,2816]{2,1,0:T(8,128)(2,1)}, bf16[2,64,2816]{2,1,0:T(8,128)(2,1)}, u32[]{:S(2)}, u32[]{:S(2)}) collective-permute-start(bf16[2,64,2816]{2,1,0:T(8,128)(2,1)} %get-tuple-element.219), channel_id=1, source_target_pairs={{0,4},{1,5},{2,6},{3,7},{4,0},{5,1},{6,2},{7,3},{8,12},{9,13},{10,... | collective-permute-start | bytes 2162696 | tf_op jit(solution)/shard_map/ppermute | solution.py:773
  549.5 58.7 %collective-permute-start.66 = (bf16[15,96,768]{2,1,0:T(8,128)(2,1)}, bf16[15,96,768]{2,1,0:T(8,128)(2,1)}, u32[]{:S(2)}, u32[]{:S(2)}) collective-permute-start(bf16[15,96,768]{2,1,0:T(8,128)(2,1)} %get-tuple-element.252), channel_id=1, source_target_pairs={{0,2},{1,3},{2,0},{3,1},{4,6},{5,7},{6,4},{7,5},{8,10},{9,11},{10,... | collective-permute-start | bytes 6635528 | tf_op jit(solution)/shard_map/ppermute | solution.py:773
  551.0 57.2 %collective-permute-start.67 = (bf16[15,96,768]{2,1,0:T(8,128)(2,1)}, bf16[15,96,768]{2,1,0:T(8,128)(2,1)}, u32[]{:S(2)}, u32[]{:S(2)}) collective-permute-start(bf16[15,96,768]{2,1,0:T(8,128)(2,1)} %get-tuple-element.253), channel_id=1, source_target_pairs={{0,4},{1,5},{2,6},{3,7},{4,0},{5,1},{6,2},{7,3},{8,12},{9,13},{10,... | collective-permute-start | bytes 6635528 | tf_op jit(solution)/shard_map/ppermute | solution.py:773
  563.9 38.1 %collective-permute-start.64 = (bf16[320,128]{1,0:T(8,128)(2,1)S(1)}, bf16[320,128]{1,0:T(8,128)(2,1)S(1)}, u32[]{:S(2)}, u32[]{:S(2)}) collective-permute-start(bf16[320,128]{1,0:T(8,128)(2,1)S(1)} %pad_maximum_fusion.31), channel_id=1, source_target_pairs={{0,2},{1,3},{2,0},{3,1},{4,6},{5,7},{6,4},{7,5},{8,10},{9,11},{10,... | collective-permute-start | bytes 245768 | tf_op jit(solution)/shard_map/ppermute | solution.py:773
  564.5 63.5 %collective-permute-start.93 = (bf16[1,64,2816]{2,1,0:T(8,128)(2,1)}, bf16[1,64,2816]{2,1,0:T(8,128)(2,1)}, u32[]{:S(2)}, u32[]{:S(2)}) collective-permute-start(bf16[1,64,2816]{2,1,0:T(8,128)(2,1)} %get-tuple-element.290), channel_id=1, source_target_pairs={{0,24},{1,25},{2,26},{3,27},{4,28},{5,29},{6,30},{7,31},{8,16},{9,... | collective-permute-start | bytes 1081352 | tf_op jit(solution)/shard_map/ppermute | solution.py:773
  567.3 60.7 %collective-permute-start.92 = (bf16[1,64,2816]{2,1,0:T(8,128)(2,1)}, bf16[1,64,2816]{2,1,0:T(8,128)(2,1)}, u32[]{:S(2)}, u32[]{:S(2)}) collective-permute-start(bf16[1,64,2816]{2,1,0:T(8,128)(2,1)} %get-tuple-element.289), channel_id=1, source_target_pairs={{0,16},{1,17},{2,18},{3,19},{4,20},{5,21},{6,22},{7,23},{8,24},{9,... | collective-permute-start | bytes 1081352 | tf_op jit(solution)/shard_map/ppermute | solution.py:773
  664.6 59.3 %collective-permute-start.80 = (bf16[12,96,768]{2,1,0:T(8,128)(2,1)}, bf16[12,96,768]{2,1,0:T(8,128)(2,1)}, u32[]{:S(2)}, u32[]{:S(2)}) collective-permute-start(bf16[12,96,768]{2,1,0:T(8,128)(2,1)} %get-tuple-element.274), channel_id=1, source_target_pairs={{0,2},{1,3},{2,0},{3,1},{4,6},{5,7},{6,4},{7,5},{8,10},{9,11},{10,... | collective-permute-start | bytes 5308424 | tf_op jit(solution)/shard_map/ppermute | solution.py:773
  665.6 58.3 %collective-permute-start.81 = (bf16[12,96,768]{2,1,0:T(8,128)(2,1)}, bf16[12,96,768]{2,1,0:T(8,128)(2,1)}, u32[]{:S(2)}, u32[]{:S(2)}) collective-permute-start(bf16[12,96,768]{2,1,0:T(8,128)(2,1)} %get-tuple-element.275), channel_id=1, source_target_pairs={{0,4},{1,5},{2,6},{3,7},{4,0},{5,1},{6,2},{7,3},{8,12},{9,13},{10,... | collective-permute-start | bytes 5308424 | tf_op jit(solution)/shard_map/ppermute | solution.py:773
  671.6 48.8 %collective-permute-start.86 = (bf16[15,24,768]{2,1,0:T(8,128)(2,1)S(1)}, bf16[15,24,768]{2,1,0:T(8,128)(2,1)}, u32[]{:S(2)}, u32[]{:S(2)}) collective-permute-start(bf16[15,24,768]{2,1,0:T(8,128)(2,1)S(1)} %copy-done.88), channel_id=1, source_target_pairs={{0,16},{1,17},{2,18},{3,19},{4,20},{5,21},{6,22},{7,23},{8,24},{9,... | collective-permute-start | bytes 1658888 | tf_op jit(solution)/shard_map/ppermute | solution.py:773
  671.6 48.8 %collective-permute-start.85 = (bf16[15,24,768]{2,1,0:T(8,128)(2,1)S(1)}, bf16[15,24,768]{2,1,0:T(8,128)(2,1)}, u32[]{:S(2)}, u32[]{:S(2)}) collective-permute-start(bf16[15,24,768]{2,1,0:T(8,128)(2,1)S(1)} %copy-done.86), channel_id=1, source_target_pairs={{0,8},{1,9},{2,10},{3,11},{4,12},{5,13},{6,14},{7,15},{8,0},{9,1},... | collective-permute-start | bytes 1658888 | tf_op jit(solution)/shard_map/ppermute | solution.py:773
  (281 other events, 3706.3 us)

commit v3 on v2

--- a/solution.py
+++ b/solution.py
@@ -554,10 +554,137 @@
     grad_hidden_out[...] = norm_back(unit, scale, grad_unit * (1.0 + mods[1:2]))
 
 
+def full_sum(values):
+    return row_sum(jnp.sum(values, axis=1, keepdims=True))
+
+
+def update_kernel(
+    count,
+    raw_in,
+    raw_down,
+    raw_main,
+    raw_rest,
+    old_in,
+    old_down,
+    old_main,
+    old_rest,
+    rows_in,
+    rows_down,
+    rows_main,
+    rows_rest,
+    cols_in,
+    cols_down,
+    cols_main,
+    cols_rest,
+    squares_in,
+    squares_down,
+    squares_main,
+    squares_rest,
+    row_sums,
+    late_bias,
+    head_sum,
+    scales_out,
+    new_in,
+    clip_in,
+    copy_in,
+    new_cols_in,
+    new_down,
+    clip_down,
+    copy_down,
+    new_cols_down,
+    new_main,
+    clip_main,
+    copy_main,
+    new_cols_main,
+    new_rest,
+    clip_rest,
+    copy_rest,
+    new_cols_rest,
+):
+    total = row_sums[0:1, 6:7] + full_sum(late_bias[...] * late_bias[...])
+    total = total + full_sum(head_sum[...] * head_sum[...])
+    for squares in (squares_in, squares_down, squares_main, squares_rest):
+        total = total + full_sum(squares[...])
+    norm = jnp.sqrt(total)
+    clip = jnp.minimum(1.0, CLIP_LIMIT / norm)
+    scales_out[0:1] = jnp.broadcast_to(norm, (1, 128))
+    scales_out[1:2] = jnp.broadcast_to(clip, (1, 128))
+
+    def step(place, old, raw, pair, col_old, squares):
+        rows, columns = raw.shape
+        rows_all = count * rows
+        row_new = DECAY_RATE * pair[:, 0:1] + (1.0 - DECAY_RATE) * (
+            clip * (clip * (pair[:, 1:2] / columns)) + FACTOR_EPS
+        )
+        col_new = DECAY_RATE * col_old + (1.0 - DECAY_RATE) * (
+            clip * (clip * (squares / rows_all)) + FACTOR_EPS
+        )
+        row_mean = (
+            DECAY_RATE * row_sums[0:1, place : place + 1]
+            + (1.0 - DECAY_RATE) * (clip * (clip * (full_sum(squares) / columns)))
+        ) / rows_all + (1.0 - DECAY_RATE) * FACTOR_EPS
+        clipped = clip * raw
+        estimate = row_new * col_new / row_mean
+        return old - LEARN_RATE * clipped * lax.rsqrt(estimate), clipped, col_new
+
+    for level in range(L):
+        one = slice(level, level + 1)
+        for place, old, raw, pair, col_old, squares, new, clipped, copy, cols in (
+            (level, old_in, raw_in, rows_in, cols_in, squares_in, new_in, clip_in, copy_in, new_cols_in),
+            (
+                L + level,
+                old_down,
+                raw_down,
+                rows_down,
+                cols_down,
+                squares_down,
+                new_down,
+                clip_down,
+                copy_down,
+                new_cols_down,
+            ),
+        ):
+            made = step(
+                place, old[level], raw[level], pair[level], col_old[one], squares[one]
+            )
+            new[level], clipped[level], cols[one] = made
+            copy[level] = bf16(made[0])
+    for place, old, raw, pair, col_old, squares, new, clipped, copy, cols in (
+        (
+            2 * L,
+            old_main,
+            raw_main,
+            rows_main,
+            cols_main,
+            squares_main,
+            new_main,
+            clip_main,
+            copy_main,
+            new_cols_main,
+        ),
+        (
+            2 * L + 1,
+            old_rest,
+            raw_rest,
+            rows_rest,
+            cols_rest,
+            squares_rest,
+            new_rest,
+            clip_rest,
+            copy_rest,
+            new_cols_rest,
+        ),
+    ):
+        made = step(place, old[...], raw[...], pair[...], col_old[...], squares[...])
+        new[...], clipped[...], cols[...] = made
+        copy[...] = bf16(made[0])
+
+
 def cost(microseconds):
     return pl.CostEstimate(flops=microseconds, bytes_accessed=0, transcendentals=0)
 
 
+VMEM_GRANT = 60 * 2**20
 VMEM_WHOLE = pl.BlockSpec(memory_space=pltpu.VMEM)
 IN_PLACE = pl.BlockSpec(memory_space=pl.ANY)
 
@@ -574,7 +701,7 @@
         out_shape=[*outputs, *far_outputs],
         scratch_shapes=scratch,
         cost_estimate=cost(microseconds),
-        compiler_params=pltpu.CompilerParams(vmem_limit_bytes=limit * 2**20),
+        compiler_params=pltpu.CompilerParams(vmem_limit_bytes=VMEM_GRANT),
     )(*inputs, *far_inputs)
 
 
@@ -612,7 +739,7 @@
             out_specs=[VMEM_WHOLE] * 3,
             out_shape=[shaped(LOW, D, D), shaped(LOW, D, D), shaped(LOW, CHUNK, CHUNK)],
             cost_estimate=cost(3),
-            compiler_params=pltpu.CompilerParams(vmem_limit_bytes=16 * 2**20),
+            compiler_params=pltpu.CompilerParams(vmem_limit_bytes=VMEM_GRANT),
         )(*sources)
 
 
@@ -856,11 +983,11 @@
         return jnp.concatenate([short.reshape(self.wide, -1, width)] + long)
 
     def along_z(self):
-        own = self.pack
-        self.quad = self.merged([own] + [self.move(own, mask) for mask in (8, 16, 24)])
+        self.deep = [self.pack] + [self.move(self.pack, mask) for mask in (8, 16, 24)]
+
+    def along_xy(self):
+        self.quad = self.merged(self.deep)
         self.half = self.quad.shape[0] // 2
-
-    def along_xy(self):
         self.by_y = self.move(self.quad, 4)
         self.by_x = self.move(self.quad, 2)
 
@@ -993,7 +1120,7 @@
                 pltpu.SemaphoreType.DMA((len(self.held),)),
             ],
             cost_estimate=cost(4),
-            compiler_params=pltpu.CompilerParams(vmem_limit_bytes=48 * 2**20),
+            compiler_params=pltpu.CompilerParams(vmem_limit_bytes=VMEM_GRANT),
         )(*near, *self.held)
 
     def make_far(self):
@@ -1097,8 +1224,8 @@
     turned = ordered(parts, list(range(count)), position)
     rows = parts.shape[1]
     for bit in reversed(range(count.bit_length() - 1)):
-        if bit == 2:
-            blocks = between(blocks)
+        if bit == 2 or bit == 0:
+            blocks = between[bit](blocks)
         halves = turned.reshape(-1, 2, 1 << bit, rows, 128)
         kept, sent = halves[:, 0], halves[:, 1]
         sent = jnp.concatenate([blocks.reshape(-1, 128), sent.reshape(-1, 128)])
@@ -1129,8 +1256,8 @@
         mine = bit_of(position, bit)
         piece = total({**fixed, bit: 1 - mine}).astype(LOW)
         sent = jnp.concatenate([blocks.reshape(-1, 128), piece.reshape(-1, 128)])
-        if bit == 3:
-            sent = between(sent)
+        if bit in between:
+            sent = between[bit](sent)
         received = swap(sent, 1 << bit, count)
         size = blocks.shape[0] * blocks.shape[1]
         blocks = jnp.concatenate([blocks, received[:size].reshape(blocks.shape)])
@@ -1251,7 +1378,16 @@
         layers[0].along_z()
         return blocks
 
-    small_all, time_out_mine = gather_and_turn(small, turned, position, count, start_gathers)
+    def see_one(blocks):
+        if count == 32:
+            blocks, layers[0].deep[1], layers[0].deep[3] = meet(
+                blocks, layers[0].deep[1], layers[0].deep[3]
+            )
+        return blocks
+
+    small_all, time_out_mine = gather_and_turn(
+        small, turned, position, count, {2: start_gathers, 0: see_one}
+    )
     small_all = small_all.reshape(count, -1)
     orders = Orders(position, count == 32)
     bias_full = small_all[:, :bias_part].reshape(-1).astype(FULL)
@@ -1270,6 +1406,14 @@
     def mine(values):
         return lax.dynamic_slice_in_dim(values, position * width_rows, width_rows)
 
+    latent_low = latents.reshape(TOK, PD).astype(jnp.bfloat16)
+    hidden = (
+        lax.dot_general(
+            latent_low, patch_t, (((1,), (1,)), ((), ())), preferred_element_type=jnp.float32
+        )
+        + bias_patch
+        + positions()
+    )
     freq_low = time_freq(times_all).astype(LOW)
     embed_hidden = dot_rows(time_in, freq_low) + bias_tin[:, None]
     embed_act = jax.nn.silu(embed_hidden).astype(LOW)
@@ -1286,7 +1430,7 @@
     if count == 32:
 
         def start_near(pieces):
-            pieces, layers[0].quad = meet(pieces, layers[0].quad)
+            pieces, layers[0].deep = meet(pieces, layers[0].deep)
             layers[0].along_xy()
             return pieces
 
@@ -1294,27 +1438,24 @@
     (mods,) = scatter_sum([mod_part], range(bits), position, count, FULL, before)
     mods, rest.pack = meet(mods, rest.pack)
     rest.along_z()
+    if count == 32:
+        mods, layers[0].by_x, layers[0].by_y, rest.deep, hidden, block_bias = meet(
+            mods, layers[0].by_x, layers[0].by_y, rest.deep, hidden, block_bias
+        )
     mods = mods.reshape(-1)
     bias_ada = jnp.concatenate(
         [block_bias[level, 8:14].reshape(-1) for level in range(L)] + [bias_final]
     )
     mods = (mods + bias_ada).reshape(-1, D)
 
-    latent_low = latents.reshape(TOK, PD).astype(jnp.bfloat16)
-    hidden = (
-        lax.dot_general(
-            latent_low, patch_t, (((1,), (1,)), ((), ())), preferred_element_type=jnp.float32
-        )
-        + bias_patch
-        + positions()
-    )
     layers[0].across()
     if count == 32:
-        rest.quad, layers[1].pack = meet(rest.quad, layers[1].pack)
-        layers[0].far, rest.quad = meet(layers[0].far, rest.quad)
+        layers[0].far, rest.deep, layers[1].pack = meet(
+            layers[0].far, rest.deep, layers[1].pack
+        )
+    layers[0].finish()
     rest.along_xy()
     layers[1].along_z()
-    layers[0].finish()
 
     def forward(level, hidden):
         level_mods = mods[6 * level : 6 * level + 6]
@@ -1322,6 +1463,11 @@
             hidden, level_mods, block_bias[level], orders, layers[level]
         )
         kept_attn = [hidden, normed, packed, logs, attended, branch]
+        if count == 32 and level == 0:
+            middle, rest.by_x, rest.by_y, layers[1].deep = meet(
+                middle, rest.by_x, rest.by_y, layers[1].deep
+            )
+            rest.across()
         if count == 32 and level == 1:
             middle, rest_sum.to_far = meet(middle, rest_sum.to_far)
             rest_sum.across()
@@ -1334,9 +1480,7 @@
     hidden, *kept[0] = forward(0, hidden)
     first_out = hidden
     if count == 32:
-        hidden, rest.by_x, rest.by_y = meet(hidden, rest.by_x, rest.by_y)
-        rest.across()
-        rest.far, layers[1].quad = meet(rest.far, layers[1].quad)
+        hidden, rest.far, layers[1].deep = meet(hidden, rest.far, layers[1].deep)
     first_out = hidden
     layers[1].along_xy()
     rest.finish()
@@ -1374,9 +1518,6 @@
         targets.reshape(TOK, PD),
         time_weights.reshape(1, 1),
     )
-    local_loss = head_loss[0, 0] + cosine_part[0, 0]
-    grad_head_full = jnp.concatenate([grad_head, grad_head_bias], axis=0)
-
     bias_grads, mod_grads = [None] * L, [None] * L
 
     def backward(level, grad_hidden):
@@ -1384,17 +1525,24 @@
         grad_middle, mlp_mods, mlp_bias, mlp_mine, *mlp_theirs = mlp_backward(
             grad_hidden, level_mods, kept[level][1], orders, layers[level]
         )
+        if count == 32 and level == 0:
+            one_sum.far, rest_sum.deep = meet(one_sum.far, rest_sum.deep)
+            one_sum.make_near()
+            grad_middle, one_sum.to_near = meet(grad_middle, one_sum.to_near)
+            one_sum.along_xy()
         grad_hidden, attn_mods, attn_bias, attn_mine, *attn_theirs = attn_backward(
             grad_middle, level_mods, kept[level][0], orders, layers[level]
         )
         mod_grads[level] = jnp.concatenate([attn_mods, mlp_mods])
-        bias_grads[level] = jnp.concatenate(
-            [attn_bias, mlp_bias[:4], mod_grads[level], mlp_bias[4:]]
-        ).reshape(-1)
+        bias_grads[level] = (attn_bias, mlp_bias)
+        if count == 32 and level == 1:
+            attn_theirs, rest_sum.near = meet(attn_theirs, rest_sum.near)
         parts = [(attn_mine, attn_theirs, 4, 0), (mlp_mine, mlp_theirs, 4, 4)]
         return grad_hidden, parts
 
     rest_sum.make_near()
+    if count == 32:
+        grad_hidden, rest_sum.to_near = meet(grad_hidden, rest_sum.to_near)
     rest_sum.along_xy()
     grad_hidden, parts = backward(1, grad_hidden)
     one_sum = scatter(parts + [(one_mine, [one_theirs], 3, 0)], count)
@@ -1402,9 +1550,7 @@
     one_sum.make_far()
     grad_hidden = grad_hidden + grad_first
     if count == 32:
-        grad_hidden, one_sum.to_far, rest_sum.near = meet(
-            grad_hidden, one_sum.to_far, rest_sum.near
-        )
+        grad_hidden, one_sum.to_far = meet(grad_hidden, one_sum.to_far)
     one_sum.across()
     rest_sum.make_deep()
     rest_sum.along_z()
@@ -1412,7 +1558,34 @@
     zero_sum = scatter(parts, count)
     zero_sum.cores()
     zero_sum.make_far()
-    one_sum.make_near()
+    grad_mods = jnp.concatenate(mod_grads + [grad_final_mods]).astype(LOW).reshape(-1, 128)
+    mod_rows = grad_mods.shape[0]
+    grad_mods = jnp.pad(grad_mods, ((0, -mod_rows % 16), (0, 0)))
+    left = (
+        (grad_hidden, grad_one, grad_two, grad_three, grad_final_mods, bias_grads, mod_grads),
+        (grad_head, grad_head_bias, head_loss, cosine_part),
+        (block_in, stem_main, stem_main_rows, stem_proj_rows, block_in_rows, block_down_rows),
+    )
+    if count == 32:
+        grad_mods, one_sum.near, zero_sum.to_far, left = meet(
+            grad_mods, one_sum.near, zero_sum.to_far, left
+        )
+    grad_hidden, grad_one, grad_two, grad_three, grad_final_mods, bias_grads, mod_grads = left[0]
+    grad_head, grad_head_bias, head_loss, cosine_part = left[1]
+    block_in, stem_main, stem_main_rows, stem_proj_rows, block_in_rows, block_down_rows = left[2]
+    zero_sum.across()
+    one_sum.make_deep()
+    one_sum.along_z()
+    time_out_part, final_ada_part = stem_main[:, :D], stem_main[:, D : 3 * D]
+    ada_mine = jnp.concatenate(
+        [block_in[level, :, main_width:] for level in range(L)] + [final_ada_part], axis=1
+    ).astype(LOW)
+    local_loss = head_loss[0, 0] + cosine_part[0, 0]
+    grad_head_full = jnp.concatenate([grad_head, grad_head_bias], axis=0)
+    bias_grads = [
+        jnp.concatenate([attn_bias, mlp_bias[:4], grads, mlp_bias[4:]]).reshape(-1)
+        for (attn_bias, mlp_bias), grads in zip(bias_grads, mod_grads)
+    ]
     grad_patch = lax.dot_general(
         grad_hidden.astype(jnp.bfloat16),
         latent_low,
@@ -1433,21 +1606,22 @@
     extra = jnp.concatenate(
         [grad_patch.reshape(count, -1), grad_bias_all.reshape(count, bias_part)], axis=1
     )
-    grad_mods = jnp.concatenate(mod_grads + [grad_final_mods]).astype(LOW).reshape(-1, 128)
-    mod_rows = grad_mods.shape[0]
-    grad_mods = jnp.pad(grad_mods, ((0, -mod_rows % 16), (0, 0)))
     extra = jnp.pad(extra, ((0, 0), (0, -extra.shape[1] % 2048))).reshape(count, -1, 128)
-    if count == 32:
-        grad_mods, one_sum.to_near = meet(grad_mods, one_sum.to_near)
-    one_sum.along_xy()
-
-    def start_far(sent):
+    def start_near(sent):
         if count == 32:
-            sent, one_sum.near, zero_sum.to_far = meet(sent, one_sum.near, zero_sum.to_far)
-        zero_sum.across()
+            sent, zero_sum.far = meet(sent, zero_sum.far)
+        zero_sum.make_near()
+        zero_sum.along_xy()
         return sent
 
-    grad_mods_all, extra = gather_and_sum(grad_mods, extra, position, count, start_far)
+    def see_deep(sent):
+        if count == 32:
+            sent, one_sum.deep = meet(sent, one_sum.deep)
+        return sent
+
+    grad_mods_all, extra = gather_and_sum(
+        grad_mods, extra, position, count, {2: start_near, 3: see_deep}
+    )
     grad_mods_all = grad_mods_all[:, :mod_rows].reshape(images, -1)
     turned = order_of(list(range(count)), position)
     cond_turned = dot(cond_low, turned).astype(LOW)
@@ -1467,16 +1641,11 @@
     )
     grad_condition_low = grad_condition.astype(LOW)
 
-    one_sum.make_deep()
-    zero_sum.make_near()
-
     def between(blocks):
         if count == 32:
-            blocks, one_sum.to_deep, zero_sum.to_near = meet(
-                blocks, one_sum.to_deep, zero_sum.to_near
-            )
-        one_sum.along_z()
-        zero_sum.along_xy()
+            blocks, zero_sum.near = meet(blocks, zero_sum.near)
+        zero_sum.make_deep()
+        zero_sum.along_z()
         return blocks
 
     masks = [1 << bit for bit in range(3, bits)] + [4, 2, 1]
@@ -1486,8 +1655,6 @@
     grad_embed_act = dot(time_out_part.astype(LOW), grad_condition_low)
     grad_embed = silu_back(mine(embed_hidden), grad_embed_act)
     grad_time_in = dot(grad_embed.astype(LOW), freq_low)
-    zero_sum.make_deep()
-    zero_sum.along_z()
     late_bias = jnp.zeros((2, D), jnp.float32)
     late_bias = lax.dynamic_update_slice(
         late_bias,
@@ -1551,43 +1718,59 @@
     row_old_sums, bias_loss, late_bias, head_sum = late_sums[6:]
     head_sum = head_sum.reshape(D + 1, PD)
     loss_total = bias_loss[1]
-    total_square = bias_loss[0] + jnp.sum(late_bias * late_bias) + jnp.sum(head_sum * head_sum)
-    for col_square in col_squares:
-        total_square = total_square + jnp.sum(col_square)
-    grad_norm = jnp.sqrt(total_square)
-    clip = jnp.minimum(1.0, CLIP_LIMIT / grad_norm)
-
-    olds = [block_in[0], block_in[1], block_down[0], block_down[1], stem_main, stem_proj]
-    col_olds = [
-        block_in_cols[0],
-        block_in_cols[1],
-        block_down_cols[0],
-        block_down_cols[1],
-        stem_main_cols,
-        stem_proj_cols,
+    row_sums = jnp.pad(jnp.concatenate([row_old_sums, bias_loss])[None], ((0, 0), (0, 120)))
+    pairs = [
+        jnp.stack([row_old, square], axis=-1) for row_old, square in zip(row_olds, row_squares)
     ]
-    results = [
-        factored(
-            olds[slot],
-            raws[slot],
-            row_olds[slot],
-            col_olds[slot],
-            row_squares[slot],
-            col_squares[slot],
-            row_old_sums[slot],
-            count * olds[slot].shape[0],
-            clip,
+    olds = [block_in, block_down, stem_main, stem_proj]
+    raw_list = [raw_in, raw_down, raw_main, raw_proj]
+    outputs = [shaped(FULL, 8, 128)]
+    col_old_list = [block_in_cols, block_down_cols, stem_main_cols[None], stem_proj_cols[None]]
+    for old, col_old in zip(olds, col_old_list):
+        outputs += [shaped(FULL, *old.shape), shaped(FULL, *old.shape), shaped(LOW, *old.shape)]
+        outputs.append(shaped(FULL, *col_old.shape))
+    made = call(
+        functools.partial(update_kernel, count),
+        [
+            *raw_list,
+            *olds,
+            jnp.stack(pairs[0:2]),
+            jnp.stack(pairs[2:4]),
+            pairs[4],
+            pairs[5],
+            *col_old_list,
+            jnp.stack(col_squares[0:2]),
+            jnp.stack(col_squares[2:4]),
+            col_squares[4][None],
+            col_squares[5][None],
+            row_sums,
+            late_bias.reshape(2, D),
+            head_sum,
+        ],
+        [],
+        outputs,
+        [],
+        [],
+        12,
+        0,
+    )
+    grad_norm, clip = made[0][0, 0], made[0][1, 0]
+    (
+        (new_in, clip_in, copy_in, cols_in),
+        (new_down, clip_down, copy_down, cols_down),
+        (new_main, clip_main, copy_main, cols_main),
+        (new_proj, clip_proj, copy_proj, cols_proj),
+    ) = (made[1 + 4 * slot : 5 + 4 * slot] for slot in range(4))
+
+    def new_rows(row_old, row_square, columns):
+        return DECAY_RATE * row_old + (1.0 - DECAY_RATE) * (
+            clip * (clip * (row_square / columns)) + FACTOR_EPS
         )
-        for slot in range(6)
-    ]
-    new_in, clip_in, rows_in, cols_in = [
-        jnp.stack([results[0][part], results[1][part]]) for part in range(4)
-    ]
-    new_down, clip_down, rows_down, cols_down = [
-        jnp.stack([results[2][part], results[3][part]]) for part in range(4)
-    ]
-    new_main, clip_main, rows_main, cols_main = results[4]
-    new_proj, clip_proj, rows_proj, cols_proj = results[5]
+
+    rows_in = new_rows(block_in_rows, jnp.stack(row_squares[0:2]), block_in.shape[-1])
+    rows_down = new_rows(block_down_rows, jnp.stack(row_squares[2:4]), D)
+    rows_main = new_rows(stem_main_rows, row_squares[4], stem_main.shape[-1])
+    rows_proj = new_rows(stem_proj_rows, row_squares[5], stem_proj.shape[-1])
     head_square = head_sum * head_sum
     new_head, head_clip, rows_head, cols_head = factored(
         head_weight,
@@ -1615,22 +1798,22 @@
         clip_in,
         rows_in,
         cols_in,
-        new_in.astype(jnp.bfloat16),
+        copy_in,
         new_down,
         clip_down,
         rows_down,
         cols_down,
-        new_down.astype(jnp.bfloat16),
+        copy_down,
         new_main,
         clip_main,
         rows_main,
-        cols_main,
-        new_main.astype(jnp.bfloat16),
+        cols_main[0],
+        copy_main,
         new_proj,
         clip_proj,
         rows_proj,
-        cols_proj,
-        new_proj.astype(jnp.bfloat16),
+        cols_proj[0],
+        copy_proj,
         new_head,
         head_clip,
         rows_head,

time: 860 us -> 751 us (0.87)
  waiting for transfers between devices: 330 us -> 255 us
  local copies, waits for them, and re-layouts: 159 us -> 87.3 us
  Pallas kernels: 174 us -> 211 us
  starting transfers between devices: 84.8 us -> 114 us
  other arithmetic: 65.7 us -> 53.8 us
  between operations: 23.5 us -> 13.2 us
    ppermute x99, waiting for transfers between devices: 330 us -> 255 us  [swap(): lax.ppermute(array, 'fsdp', [(place, place ^ mask) for place in range(cou...]
    unnamed x438 -> x325, local copies, waits for them, and re-layouts: 63.5 us -> 24.5 us
    pallas_call x10 -> x11, Pallas kernels: 128 us -> 158 us  [call(): pl.pallas_call(kernel, in_specs=[VMEM_WHOLE] * len(inputs) + [IN_PLACE] *...]
    ppermute x99, starting transfers between devices: 84.8 us -> 114 us  [swap(): lax.ppermute(array, 'fsdp', [(place, place ^ mask) for place in range(cou...]
  transfers between devices with their start and end apart: 99 -> 99, of which waited for: 42 -> 47; matrix products, arithmetic and copies ran while one was open for 17% -> 12% of each run, Pallas kernels for 17% -> 25%
where the time goes in v3:
time: 751 us; the launch traced here: 742 us
  waiting for transfers between devices  255 us (34%)
  Pallas kernels  211 us (28%)
  starting transfers between devices  114 us (15%)
  local copies, waits for them, and re-layouts  87.3 us (12%)
  other arithmetic  53.8 us (7%)
  between operations  13.2 us (2%)
  matrix products  8.23 us (1%)
    ppermute x99, waiting for transfers between devices, swap(): lax.ppermute(array, 'fsdp', [(place, place ^ mask) for place in range(cou...  255 us
    pallas_call x11, Pallas kernels, call(): pl.pallas_call(kernel, in_specs=[VMEM_WHOLE] * len(inputs) + [IN_PLACE] *...  158 us
    ppermute x99, starting transfers between devices, swap(): lax.ppermute(array, 'fsdp', [(place, place ^ mask) for place in range(cou...  114 us
    pallas_call x9, Pallas kernels, call(): pl.pallas_call(kernel, in_specs=[VMEM_WHOLE] * len(near) + [IN_PLACE] * l...  50.4 us
    unnamed x325, local copies, waits for them, and re-layouts  24.5 us
  transfers between devices with their start and end apart: 99, of which 47 were waited for; matrix products, arithmetic and copies ran while one was open for 12% of the time, Pallas kernels for 25%

profile of v3, /device:TPU:0, one launch (start us, length us, event | category | flops | bytes accessed | tf_op | source)
XLA Modules:
  0.0 742.2 jit_solution(17389949300162606612)
XLA Ops:
  34.9 13.3 %collective-permute-done.5 = bf16[15,24,768]{2,1,0:T(8,128)(2,1)} collective-permute-done((bf16[15,24,768]{2,1,0:T(8,128)(2,1)S(1)}, bf16[15,24,768]{2,1,0:T(8,128)(2,1)}, u32[]{:S(2)}, u32[]{:S(2)}) %collective-permute-start.5) | collective-permute-done | bytes 552992 | tf_op jit(solution)/shard_map/ppermute | solution.py:900
  80.6 8.6 %collective-permute-done.10 = bf16[15,24,768]{2,1,0:T(8,128)(2,1)} collective-permute-done((bf16[15,24,768]{2,1,0:T(8,128)(2,1)S(1)}, bf16[15,24,768]{2,1,0:T(8,128)(2,1)}, u32[]{:S(2)}, u32[]{:S(2)}) %collective-permute-start.10) | collective-permute-done | bytes 552992 | tf_op jit(solution)/shard_map/ppermute | solution.py:900
  126.5 12.1 %collective-permute-done.16 = bf16[1,64,2816]{2,1,0:T(8,128)(2,1)} collective-permute-done((bf16[1,64,2816]{2,1,0:T(8,128)(2,1)S(1)}, bf16[1,64,2816]{2,1,0:T(8,128)(2,1)}, u32[]{:S(2)}, u32[]{:S(2)}) %collective-permute-start.16) | collective-permute-done | bytes 360480 | tf_op jit(solution)/shard_map/ppermute | solution.py:900
  151.2 20.4 %collective-permute-done.18.refs_3_ = bf16[7,96,768]{2,1,0:T(8,128)(2,1)S(1)} collective-permute-done((bf16[7,96,768]{2,1,0:T(8,128)(2,1)S(1)}, bf16[7,96,768]{2,1,0:T(8,128)(2,1)S(1)}, u32[]{:S(2)}, u32[]{:S(2)}) %collective-permute-start.18) | collective-permute-done | bytes 1032224 | tf_op jit(solution)/shard_map/ppermute | solution.py:900
  193.6 13.4 %shard_map.492 = (bf16[256,768]{1,0:T(8,128)(2,1)}, bf16[3,256,768]{2,1,0:T(8,128)(2,1)}, f32[256,128]{1,0:T(8,128)}, bf16[256,768]{1,0:T(8,128)(2,1)}, f32[256,768]{1,0:T(8,128)}, /*index=5*/f32[256,768]{1,0:T(8,128)}) custom-call(f32[256,768]{1,0:T(8,128)} %fusion.1.hidden, f32[6,768]{1,0:T(8,128)} %get-tuple-element.673.mods, ...), custom_call_target="tpu_custom_call" | custom-call | flops 11 | tf_op jit(solution)/shard_map/pallas_call | solution.py:697
  207.6 13.6 %collective-permute-done.28 = bf16[12,24,768]{2,1,0:T(8,128)(2,1)S(1)} collective-permute-done((bf16[12,24,768]{2,1,0:T(8,128)(2,1)}, bf16[12,24,768]{2,1,0:T(8,128)(2,1)S(1)}, u32[]{:S(2)}, u32[]{:S(2)}) %collective-permute-start.28) | collective-permute-done | bytes 442400 | tf_op jit(solution)/shard_map/ppermute | solution.py:900
  226.0 13.6 %shard_map.493 = (bf16[256,768]{1,0:T(8,128)(2,1)}, bf16[4,256,768]{2,1,0:T(8,128)(2,1)}, bf16[4,256,768]{2,1,0:T(8,128)(2,1)}, f32[256,768]{1,0:T(8,128)}, f32[256,768]{1,0:T(8,128)}) custom-call(f32[256,768]{1,0:T(8,128)} %get-tuple-element.269.middle, f32[6,768]{1,0:T(8,128)} %get-tuple-element.673.mods, f32[15,768]{1,0:T(8,128)} %get-tuple-element.665.bias, ...), custom_call_target="tpu_custom_call" | custom-call | flops 11 | tf_op jit(solution)/shard_map/pallas_call | solution.py:697
  250.7 27.0 %shard_map.495 = (f32[256,768]{1,0:T(8,128)}, f32[8,128]{1,0:T(8,128)}, f32[1,2048]{1,0:T(1,128)}, f32[1,2048]{1,0:T(1,128)}, f32[1,768]{1,0:T(1,128)}, /*index=...) custom-call(f32[256,768]{1,0:T(8,128)} %get-tuple-element.278.hidden, ...), custom_call_target="tpu_custom_call" | custom-call | flops 27 | tf_op jit(solution)/shard_map/pallas_call | solution.py:697
  289.1 18.6 %collective-permute-done.34.refs_3_ = bf16[6,96,768]{2,1,0:T(8,128)(2,1)} collective-permute-done((bf16[6,96,768]{2,1,0:T(8,128)(2,1)S(1)}, bf16[6,96,768]{2,1,0:T(8,128)(2,1)}, u32[]{:S(2)}, u32[]{:S(2)}) %collective-permute-start.34) | collective-permute-done | bytes 884768 | tf_op jit(solution)/shard_map/ppermute | solution.py:900
  312.0 12.9 %shard_map.494 = (bf16[256,768]{1,0:T(8,128)(2,1)}, bf16[3,256,768]{2,1,0:T(8,128)(2,1)}, f32[256,128]{1,0:T(8,128)}, bf16[256,768]{1,0:T(8,128)(2,1)}, f32[256,768]{1,0:T(8,128)}, /*index=5*/f32[256,768]{1,0:T(8,128)}) custom-call(f32[256,768]{1,0:T(8,128)} %get-tuple-element.278.hidden.first, f32[6,768]{1,0:T(8,128)} %get-tuple-element.672.mods, ...), custom_call_target="tpu_custom_call" | custom-call | flops 11 | tf_op jit(solution)/shard_map/pallas_call | solution.py:697
  331.3 13.7 %shard_map.497 = (bf16[256,768]{1,0:T(8,128)(2,1)}, bf16[4,256,768]{2,1,0:T(8,128)(2,1)}, bf16[4,256,768]{2,1,0:T(8,128)(2,1)}, f32[256,768]{1,0:T(8,128)}, f32[256,768]{1,0:T(8,128)}) custom-call(f32[256,768]{1,0:T(8,128)} %get-tuple-element.294.middle, f32[6,768]{1,0:T(8,128)} %get-tuple-element.672.mods, f32[15,768]{1,0:T(8,128)} %get-tuple-element.664.bias, ...), custom_call_target="tpu_custom_call" | custom-call | flops 11 | tf_op jit(solution)/shard_map/pallas_call | solution.py:697
  356.6 16.4 %shard_map.500 = (f32[256,768]{1,0:T(8,128)}, f32[3,768]{1,0:T(4,128)}, f32[5,768]{1,0:T(8,128)}, bf16[8,384,768]{2,1,0:T(8,128)(2,1)}, bf16[2,384,768]{2,1,0:T(...) custom-call(f32[256,768]{1,0:T(8,128)} %get-tuple-element.301.grad_out, ...), custom_call_target="tpu_custom_call" | custom-call | flops 16 | tf_op jit(solution)/shard_map/pallas_call | solution.py:697
  373.6 16.1 %shard_map.501 = (f32[256,768]{1,0:T(8,128)}, f32[3,768]{1,0:T(4,128)}, f32[4,768]{1,0:T(4,128)}, bf16[4,384,768]{2,1,0:T(8,128)(2,1)}, bf16[2,384,768]{2,1,0:T(8,128)(2,1)}, /*index=5*/bf16[2,384,768]{2,1,0:T(8,128)(2,1)}) custom-call(f32[256,768]{1,0:T(8,128)} %get-tuple-element.306.grad_middle, f32[6,768]{1,0:T(8,128)} %get-tuple-element.672.mods, ...), custom_call_target="tpu_custom_call" | custom-call | flops 13 | tf_op jit(solution)/shard_map/pallas_call | solution.py:697
  420.0 16.6 %shard_map.503 = (f32[256,768]{1,0:T(8,128)}, f32[3,768]{1,0:T(4,128)}, f32[5,768]{1,0:T(8,128)}, bf16[8,384,768]{2,1,0:T(8,128)(2,1)}, bf16[2,384,768]{2,1,0:T(...) custom-call(f32[256,768]{1,0:T(8,128)} %add.778.grad_out, ...), custom_call_target="tpu_custom_call" | custom-call | flops 16 | tf_op jit(solution)/shard_map/pallas_call | solution.py:697
  436.8 8.7 %collective-permute-done.64 = bf16[1,64,2816]{2,1,0:T(8,128)(2,1)S(1)} collective-permute-done((bf16[1,64,2816]{2,1,0:T(8,128)(2,1)}, bf16[1,64,2816]{2,1,0:T(8,128)(2,1)S(1)}, u32[]{:S(2)}, u32[]{:S(2)}) %collective-permute-start.64) | collective-permute-done | bytes 360480 | tf_op jit(solution)/shard_map/ppermute | solution.py:900
  457.5 16.0 %shard_map.506 = (f32[256,768]{1,0:T(8,128)}, f32[3,768]{1,0:T(4,128)}, f32[4,768]{1,0:T(4,128)}, bf16[4,384,768]{2,1,0:T(8,128)(2,1)}, bf16[2,384,768]{2,1,0:T(8,128)(2,1)}, /*index=5*/bf16[2,384,768]{2,1,0:T(8,128)(2,1)}) custom-call(f32[256,768]{1,0:T(8,128)} %get-tuple-element.347.grad_middle, f32[6,768]{1,0:T(8,128)} %get-tuple-element.673.mods, ...), custom_call_target="tpu_custom_call" | custom-call | flops 13 | tf_op jit(solution)/shard_map/pallas_call | solution.py:697
  483.9 21.8 %collective-permute-done.66.by_x = bf16[15,96,768]{2,1,0:T(8,128)(2,1)} collective-permute-done((bf16[15,96,768]{2,1,0:T(8,128)(2,1)}, bf16[15,96,768]{2,1,0:T(8,128)(2,1)}, u32[]{:S(2)}, u32[]{:S(2)}) %collective-permute-start.66) | collective-permute-done | bytes 2211872 | tf_op jit(solution)/shard_map/ppermute | solution.py:900
  553.5 11.9 %collective-permute-done.80 = bf16[15,24,768]{2,1,0:T(8,128)(2,1)} collective-permute-done((bf16[15,24,768]{2,1,0:T(8,128)(2,1)}, bf16[15,24,768]{2,1,0:T(8,128)(2,1)}, u32[]{:S(2)}, u32[]{:S(2)}) %collective-permute-start.80) | collective-permute-done | bytes 552992 | tf_op jit(solution)/shard_map/ppermute | solution.py:900
  565.5 11.2 %collective-permute-start.82 = (bf16[800,128]{1,0:T(8,128)(2,1)S(1)}, bf16[800,128]{1,0:T(8,128)(2,1)S(1)}, u32[]{:S(2)}, u32[]{:S(2)}) collective-permute-start(bf16[800,128]{1,0:T(8,128)(2,1)S(1)} %pad_maximum_fusion.12), channel_id=1, source_target_pairs={{0,8},{1,9},{2,10},{3,11},{4,12},{5,13},{6,14},{7,15},{8,0},{9,1},... | collective-permute-start | bytes 614408 | tf_op jit(solution)/shard_map/ppermute | solution.py:900
  587.8 15.0 %collective-permute-done.83 = bf16[1552,128]{1,0:T(8,128)(2,1)S(1)} collective-permute-done((bf16[1552,128]{1,0:T(8,128)(2,1)S(1)}, bf16[1552,128]{1,0:T(8,128)(2,1)S(1)}, u32[]{:S(2)}, u32[]{:S(2)}) %collective-permute-start.83) | collective-permute-done | bytes 397344 | tf_op jit(solution)/shard_map/ppermute | solution.py:900
  640.6 11.5 %collective-permute-done.88 = bf16[12,24,768]{2,1,0:T(8,128)(2,1)} collective-permute-done((bf16[12,24,768]{2,1,0:T(8,128)(2,1)}, bf16[12,24,768]{2,1,0:T(8,128)(2,1)}, u32[]{:S(2)}, u32[]{:S(2)}) %collective-permute-start.88) | collective-permute-done | bytes 442400 | tf_op jit(solution)/shard_map/ppermute | solution.py:900
  652.2 11.5 %collective-permute-done.89 = bf16[12,24,768]{2,1,0:T(8,128)(2,1)} collective-permute-done((bf16[12,24,768]{2,1,0:T(8,128)(2,1)}, bf16[12,24,768]{2,1,0:T(8,128)(2,1)}, u32[]{:S(2)}, u32[]{:S(2)}) %collective-permute-start.89) | collective-permute-done | bytes 442400 | tf_op jit(solution)/shard_map/ppermute | solution.py:900
  685.0 9.7 %collective-permute-start.97 = (f32[360,128]{1,0:T(8,128)S(1)}, f32[360,128]{1,0:T(8,128)S(1)}, u32[]{:S(2)}, u32[]{:S(2)}) collective-permute-start(f32[360,128]{1,0:T(8,128)S(1)} %add.808), channel_id=1, source_target_pairs={{0,8},{1,9},{2,10},{3,11},{4,12},{5,13},{6,14},{7,15},{8,0},{9,1},... | collective-permute-start | bytes 552968 | tf_op jit(solution)/shard_map/ppermute | solution.py:900
  713.0 9.4 %shard_map.511 = (f32[8,128]{1,0:T(8,128)}, f32[2,24,10752]{2,1,0:T(8,128)}, f32[2,24,10752]{2,1,0:T(8,128)}, bf16[2,24,10752]{2,1,0:T(8,128)(2,1)}, f32[2,10752...) custom-call(f32[2,24,10752]{2,1,0:T(8,128)} %pad_maximum_fusion.raw_, ...), custom_call_target="tpu_custom_call" | custom-call | flops 12 | tf_op jit(solution)/shard_map/pallas_call | solution.py:697
  (832 shorter events, 385.8 us)
Async XLA Ops:
  94.5 50.2 %collective-permute-start.13 = (bf16[15,96,768]{2,1,0:T(8,128)(2,1)S(1)}, bf16[15,96,768]{2,1,0:T(8,128)(2,1)}, u32[]{:S(2)}, u32[]{:S(2)}) collective-permute-start(bf16[15,96,768]{2,1,0:T(8,128)(2,1)S(1)} %bitcast_dynamic-update-slice_fusion.4.refs_0_), channel_id=1, source_target_pairs={{0,2},{1,3},{2,0},{3,1},{4,6},{5,7},{6,4},{7,5},{8,10},{9,11},{10,... | collective-permute-start | bytes 6635528 | tf_op jit(solution)/shard_map/ppermute | solution.py:900
  95.1 49.8 %collective-permute-start.14 = (bf16[15,96,768]{2,1,0:T(8,128)(2,1)S(1)}, bf16[15,96,768]{2,1,0:T(8,128)(2,1)}, u32[]{:S(2)}, u32[]{:S(2)}) collective-permute-start(bf16[15,96,768]{2,1,0:T(8,128)(2,1)S(1)} %bitcast_dynamic-update-slice_fusion.4.refs_0_), channel_id=1, source_target_pairs={{0,4},{1,5},{2,6},{3,7},{4,0},{5,1},{6,2},{7,3},{8,12},{9,13},{10,... | collective-permute-start | bytes 6635528 | tf_op jit(solution)/shard_map/ppermute | solution.py:900
  150.7 37.2 %collective-permute-start.21 = (bf16[15,96,768]{2,1,0:T(8,128)(2,1)}, bf16[15,96,768]{2,1,0:T(8,128)(2,1)}, u32[]{:S(2)}, u32[]{:S(2)}) collective-permute-start(bf16[15,96,768]{2,1,0:T(8,128)(2,1)} %collective-permute-done.13.refs_1_), channel_id=1, source_target_pairs={{0,1},{1,0},{2,3},{3,2},{4,5},{5,4},{6,7},{7,6},{8,9},{9,8},{10,11... | collective-permute-start | bytes 6635528 | tf_op jit(solution)/shard_map/ppermute | solution.py:900
  151.2 36.7 %collective-permute-start.22 = (bf16[15,96,768]{2,1,0:T(8,128)(2,1)}, bf16[15,96,768]{2,1,0:T(8,128)(2,1)}, u32[]{:S(2)}, u32[]{:S(2)}) collective-permute-start(bf16[15,96,768]{2,1,0:T(8,128)(2,1)} %collective-permute-done.14.refs_2_), channel_id=1, source_target_pairs={{0,1},{1,0},{2,3},{3,2},{4,5},{5,4},{6,7},{7,6},{8,9},{9,8},{10,11... | collective-permute-start | bytes 6635528 | tf_op jit(solution)/shard_map/ppermute | solution.py:900
  181.1 40.1 %collective-permute-start.25 = (bf16[4,64,2816]{2,1,0:T(8,128)(2,1)}, bf16[4,64,2816]{2,1,0:T(8,128)(2,1)}, u32[]{:S(2)}, u32[]{:S(2)}) collective-permute-start(bf16[4,64,2816]{2,1,0:T(8,128)(2,1)} %constant_dynamic-update-slice_fusion.1.refs_10_), channel_id=1, source_target_pairs={{0,2},{1,3},{2,0},{3,1},{4,6},{5,7},{6,4},{7,5},{8,10},{9,11},{10,... | collective-permute-start | bytes 4325384 | tf_op jit(solution)/shard_map/ppermute | solution.py:900
  183.5 37.7 %collective-permute-start.26 = (bf16[4,64,2816]{2,1,0:T(8,128)(2,1)}, bf16[4,64,2816]{2,1,0:T(8,128)(2,1)S(1)}, u32[]{:S(2)}, u32[]{:S(2)}) collective-permute-start(bf16[4,64,2816]{2,1,0:T(8,128)(2,1)} %constant_dynamic-update-slice_fusion.1.refs_10_), channel_id=1, source_target_pairs={{0,4},{1,5},{2,6},{3,7},{4,0},{5,1},{6,2},{7,3},{8,12},{9,13},{10,... | collective-permute-start | bytes 4325384 | tf_op jit(solution)/shard_map/ppermute | solution.py:900
  188.0 33.2 %collective-permute-start.28 = (bf16[12,24,768]{2,1,0:T(8,128)(2,1)}, bf16[12,24,768]{2,1,0:T(8,128)(2,1)S(1)}, u32[]{:S(2)}, u32[]{:S(2)}) collective-permute-start(bf16[12,24,768]{2,1,0:T(8,128)(2,1)} %pad_maximum_fusion.7), channel_id=1, source_target_pairs={{0,16},{1,17},{2,18},{3,19},{4,20},{5,21},{6,22},{7,23},{8,24},{9,... | collective-permute-start | bytes 1327112 | tf_op jit(solution)/shard_map/ppermute | solution.py:900
  188.6 32.6 %collective-permute-start.29 = (bf16[12,24,768]{2,1,0:T(8,128)(2,1)}, bf16[12,24,768]{2,1,0:T(8,128)(2,1)S(1)}, u32[]{:S(2)}, u32[]{:S(2)}) collective-permute-start(bf16[12,24,768]{2,1,0:T(8,128)(2,1)} %pad_maximum_fusion.7), channel_id=1, source_target_pairs={{0,24},{1,25},{2,26},{3,27},{4,28},{5,29},{6,30},{7,31},{8,16},{9,... | collective-permute-start | bytes 1327112 | tf_op jit(solution)/shard_map/ppermute | solution.py:900
  242.0 40.6 %collective-permute-start.33 = (bf16[12,96,768]{2,1,0:T(8,128)(2,1)S(1)}, bf16[12,96,768]{2,1,0:T(8,128)(2,1)S(1)}, u32[]{:S(2)}, u32[]{:S(2)}) collective-permute-start(bf16[12,96,768]{2,1,0:T(8,128)(2,1)S(1)} %bitcast_dynamic-update-slice_fusion.refs_0_), channel_id=1, source_target_pairs={{0,4},{1,5},{2,6},{3,7},{4,0},{5,1},{6,2},{7,3},{8,12},{9,13},{10,... | collective-permute-start | bytes 5308424 | tf_op jit(solution)/shard_map/ppermute | solution.py:900
  243.1 41.1 %collective-permute-start.32 = (bf16[12,96,768]{2,1,0:T(8,128)(2,1)S(1)}, bf16[12,96,768]{2,1,0:T(8,128)(2,1)}, u32[]{:S(2)}, u32[]{:S(2)}) collective-permute-start(bf16[12,96,768]{2,1,0:T(8,128)(2,1)S(1)} %bitcast_dynamic-update-slice_fusion.refs_0_), channel_id=1, source_target_pairs={{0,2},{1,3},{2,0},{3,1},{4,6},{5,7},{6,4},{7,5},{8,10},{9,11},{10,... | collective-permute-start | bytes 5308424 | tf_op jit(solution)/shard_map/ppermute | solution.py:900
  327.8 62.6 %collective-permute-start.60 = (bf16[3,384,768]{2,1,0:T(8,128)(2,1)}, bf16[3,384,768]{2,1,0:T(8,128)(2,1)S(1)}, u32[]{:S(2)}, u32[]{:S(2)}) collective-permute-start(bf16[3,384,768]{2,1,0:T(8,128)(2,1)} %get-tuple-element.327), channel_id=1, source_target_pairs={{0,1},{1,0},{2,3},{3,2},{4,5},{5,4},{6,7},{7,6},{8,9},{9,8},{10,11... | collective-permute-start | bytes 5308424 | tf_op jit(solution)/shard_map/ppermute | solution.py:900
  355.2 34.5 %collective-permute-start.52 = (bf16[4,64,2816]{2,1,0:T(8,128)(2,1)}, bf16[4,64,2816]{2,1,0:T(8,128)(2,1)}, u32[]{:S(2)}, u32[]{:S(2)}) collective-permute-start(bf16[4,64,2816]{2,1,0:T(8,128)(2,1)} %get-tuple-element.317), channel_id=1, source_target_pairs={{0,2},{1,3},{2,0},{3,1},{4,6},{5,7},{6,4},{7,5},{8,10},{9,11},{10,... | collective-permute-start | bytes 4325384 | tf_op jit(solution)/shard_map/ppermute | solution.py:900
  356.1 34.0 %collective-permute-start.53 = (bf16[4,64,2816]{2,1,0:T(8,128)(2,1)}, bf16[4,64,2816]{2,1,0:T(8,128)(2,1)}, u32[]{:S(2)}, u32[]{:S(2)}) collective-permute-start(bf16[4,64,2816]{2,1,0:T(8,128)(2,1)} %get-tuple-element.318), channel_id=1, source_target_pairs={{0,4},{1,5},{2,6},{3,7},{4,0},{5,1},{6,2},{7,3},{8,12},{9,13},{10,... | collective-permute-start | bytes 4325384 | tf_op jit(solution)/shard_map/ppermute | solution.py:900
  401.9 44.8 %collective-permute-start.62 = (bf16[8,96,768]{2,1,0:T(8,128)(2,1)}, bf16[8,96,768]{2,1,0:T(8,128)(2,1)}, u32[]{:S(2)}, u32[]{:S(2)}) collective-permute-start(bf16[8,96,768]{2,1,0:T(8,128)(2,1)} %get-tuple-element.337), channel_id=1, source_target_pairs={{0,2},{1,3},{2,0},{3,1},{4,6},{5,7},{6,4},{7,5},{8,10},{9,11},{10,... | collective-permute-start | bytes 3538952 | tf_op jit(solution)/shard_map/ppermute | solution.py:900
  403.2 43.5 %collective-permute-start.61 = (bf16[7,96,768]{2,1,0:T(8,128)(2,1)}, bf16[7,96,768]{2,1,0:T(8,128)(2,1)}, u32[]{:S(2)}, u32[]{:S(2)}) collective-permute-start(bf16[7,96,768]{2,1,0:T(8,128)(2,1)} %get-tuple-element.336), channel_id=1, source_target_pairs={{0,4},{1,5},{2,6},{3,7},{4,0},{5,1},{6,2},{7,3},{8,12},{9,13},{10,... | collective-permute-start | bytes 3096584 | tf_op jit(solution)/shard_map/ppermute | solution.py:900
  436.7 36.8 %collective-permute-start.70 = (bf16[2,384,768]{2,1,0:T(8,128)(2,1)}, bf16[2,384,768]{2,1,0:T(8,128)(2,1)S(1)}, u32[]{:S(2)}, u32[]{:S(2)}) collective-permute-start(bf16[2,384,768]{2,1,0:T(8,128)(2,1)} %get-tuple-element.364), channel_id=1, source_target_pairs={{0,1},{1,0},{2,3},{3,2},{4,5},{5,4},{6,7},{7,6},{8,9},{9,8},{10,11... | collective-permute-start | bytes 3538952 | tf_op jit(solution)/shard_map/ppermute | solution.py:900
  455.3 50.5 %collective-permute-start.66 = (bf16[15,96,768]{2,1,0:T(8,128)(2,1)}, bf16[15,96,768]{2,1,0:T(8,128)(2,1)}, u32[]{:S(2)}, u32[]{:S(2)}) collective-permute-start(bf16[15,96,768]{2,1,0:T(8,128)(2,1)} %get-tuple-element.358), channel_id=1, source_target_pairs={{0,2},{1,3},{2,0},{3,1},{4,6},{5,7},{6,4},{7,5},{8,10},{9,11},{10,... | collective-permute-start | bytes 6635528 | tf_op jit(solution)/shard_map/ppermute | solution.py:900
  456.2 50.2 %collective-permute-start.67 = (bf16[15,96,768]{2,1,0:T(8,128)(2,1)}, bf16[15,96,768]{2,1,0:T(8,128)(2,1)}, u32[]{:S(2)}, u32[]{:S(2)}) collective-permute-start(bf16[15,96,768]{2,1,0:T(8,128)(2,1)} %get-tuple-element.359), channel_id=1, source_target_pairs={{0,4},{1,5},{2,6},{3,7},{4,0},{5,1},{6,2},{7,3},{8,12},{9,13},{10,... | collective-permute-start | bytes 6635528 | tf_op jit(solution)/shard_map/ppermute | solution.py:900
  510.1 32.3 %collective-permute-start.76 = (bf16[6,96,768]{2,1,0:T(8,128)(2,1)}, bf16[6,96,768]{2,1,0:T(8,128)(2,1)}, u32[]{:S(2)}, u32[]{:S(2)}) collective-permute-start(bf16[6,96,768]{2,1,0:T(8,128)(2,1)} %get-tuple-element.396), channel_id=1, source_target_pairs={{0,4},{1,5},{2,6},{3,7},{4,0},{5,1},{6,2},{7,3},{8,12},{9,13},{10,... | collective-permute-start | bytes 2654216 | tf_op jit(solution)/shard_map/ppermute | solution.py:900
  519.5 34.0 %collective-permute-start.79 = (bf16[15,24,768]{2,1,0:T(8,128)(2,1)}, bf16[15,24,768]{2,1,0:T(8,128)(2,1)}, u32[]{:S(2)}, u32[]{:S(2)}) collective-permute-start(bf16[15,24,768]{2,1,0:T(8,128)(2,1)} %get-tuple-element.401), channel_id=1, source_target_pairs={{0,8},{1,9},{2,10},{3,11},{4,12},{5,13},{6,14},{7,15},{8,0},{9,1},... | collective-permute-start | bytes 1658888 | tf_op jit(solution)/shard_map/ppermute | solution.py:900
  525.3 40.2 %collective-permute-start.80 = (bf16[15,24,768]{2,1,0:T(8,128)(2,1)}, bf16[15,24,768]{2,1,0:T(8,128)(2,1)}, u32[]{:S(2)}, u32[]{:S(2)}) collective-permute-start(bf16[15,24,768]{2,1,0:T(8,128)(2,1)} %get-tuple-element.402), channel_id=1, source_target_pairs={{0,16},{1,17},{2,18},{3,19},{4,20},{5,21},{6,22},{7,23},{8,24},{9,... | collective-permute-start | bytes 1658888 | tf_op jit(solution)/shard_map/ppermute | solution.py:900
  551.2 62.3 %collective-permute-start.86 = (bf16[12,96,768]{2,1,0:T(8,128)(2,1)}, bf16[12,96,768]{2,1,0:T(8,128)(2,1)}, u32[]{:S(2)}, u32[]{:S(2)}) collective-permute-start(bf16[12,96,768]{2,1,0:T(8,128)(2,1)} %get-tuple-element.407), channel_id=1, source_target_pairs={{0,2},{1,3},{2,0},{3,1},{4,6},{5,7},{6,4},{7,5},{8,10},{9,11},{10,... | collective-permute-start | bytes 5308424 | tf_op jit(solution)/shard_map/ppermute | solution.py:900
  552.1 61.4 %collective-permute-start.87 = (bf16[12,96,768]{2,1,0:T(8,128)(2,1)}, bf16[12,96,768]{2,1,0:T(8,128)(2,1)}, u32[]{:S(2)}, u32[]{:S(2)}) collective-permute-start(bf16[12,96,768]{2,1,0:T(8,128)(2,1)} %get-tuple-element.408), channel_id=1, source_target_pairs={{0,4},{1,5},{2,6},{3,7},{4,0},{5,1},{6,2},{7,3},{8,12},{9,13},{10,... | collective-permute-start | bytes 5308424 | tf_op jit(solution)/shard_map/ppermute | solution.py:900
  630.4 33.2 %collective-permute-start.89 = (bf16[12,24,768]{2,1,0:T(8,128)(2,1)}, bf16[12,24,768]{2,1,0:T(8,128)(2,1)}, u32[]{:S(2)}, u32[]{:S(2)}) collective-permute-start(bf16[12,24,768]{2,1,0:T(8,128)(2,1)} %get-tuple-element.413), channel_id=1, source_target_pairs={{0,16},{1,17},{2,18},{3,19},{4,20},{5,21},{6,22},{7,23},{8,24},{9,... | collective-permute-start | bytes 1327112 | tf_op jit(solution)/shard_map/ppermute | solution.py:900
  (222 other events, 2896.3 us)

commit v4 on v3

--- a/solution.py
+++ b/solution.py
@@ -583,7 +583,28 @@
     row_sums,
     late_bias,
     head_sum,
+    head_old,
+    head_row_old,
+    head_col_old,
+    flat_in,
+    flat_down,
+    flat_main,
+    flat_rest,
+    bias_raw,
+    bias_old,
+    bias_second,
     scales_out,
+    new_head,
+    clip_head,
+    new_head_rows,
+    new_head_cols,
+    new_rows_in,
+    new_rows_down,
+    new_rows_main,
+    new_rows_rest,
+    new_bias,
+    clip_bias,
+    new_second,
     new_in,
     clip_in,
     copy_in,
@@ -610,15 +631,43 @@
     scales_out[0:1] = jnp.broadcast_to(norm, (1, 128))
     scales_out[1:2] = jnp.broadcast_to(clip, (1, 128))
 
+    def decayed(old, squares, length):
+        return DECAY_RATE * old + (1.0 - DECAY_RATE) * (
+            clip * (clip * (squares / length)) + FACTOR_EPS
+        )
+
+    head_clip = clip * head_sum[...]
+    head_squares = head_sum[...] * head_sum[...]
+    head_rows = decayed(
+        head_row_old[...], jnp.sum(head_squares, axis=1, keepdims=True), head_sum.shape[1]
+    )
+    head_cols = decayed(head_col_old[...], row_sum(head_squares), head_sum.shape[0])
+    head_mean = row_sum(head_rows) / head_sum.shape[0]
+    clip_head[...] = head_clip
+    new_head_rows[...] = head_rows
+    new_head_cols[...] = head_cols
+    new_head[...] = head_old[...] - LEARN_RATE * head_clip * lax.rsqrt(
+        head_rows * head_cols / head_mean
+    )
+    half = flat_in.shape[0] // 2
+    new_rows_in[...] = decayed(flat_in[:half], flat_in[half:], raw_in.shape[2])
+    half = flat_down.shape[0] // 2
+    new_rows_down[...] = decayed(flat_down[:half], flat_down[half:], raw_down.shape[2])
+    new_rows_main[...] = decayed(flat_main[0:1], flat_main[1:2], raw_main.shape[1])
+    new_rows_rest[...] = decayed(flat_rest[0:1], flat_rest[1:2], raw_rest.shape[1])
+    bias_clip = clip * bias_raw[...]
+    second = DECAY_RATE * bias_second[...] + (1.0 - DECAY_RATE) * (
+        bias_clip * bias_clip + FACTOR_EPS
+    )
+    clip_bias[...] = bias_clip
+    new_second[...] = second
+    new_bias[...] = bias_old[...] - LEARN_RATE * bias_clip * lax.rsqrt(second)
+
     def step(place, old, raw, pair, col_old, squares):
         rows, columns = raw.shape
         rows_all = count * rows
-        row_new = DECAY_RATE * pair[:, 0:1] + (1.0 - DECAY_RATE) * (
-            clip * (clip * (pair[:, 1:2] / columns)) + FACTOR_EPS
-        )
-        col_new = DECAY_RATE * col_old + (1.0 - DECAY_RATE) * (
-            clip * (clip * (squares / rows_all)) + FACTOR_EPS
-        )
+        row_new = decayed(pair[:, 0:1], pair[:, 1:2], columns)
+        col_new = decayed(col_old, squares, rows_all)
         row_mean = (
             DECAY_RATE * row_sums[0:1, place : place + 1]
             + (1.0 - DECAY_RATE) * (clip * (clip * (full_sum(squares) / columns)))
@@ -985,9 +1034,11 @@
     def along_z(self):
         self.deep = [self.pack] + [self.move(self.pack, mask) for mask in (8, 16, 24)]
 
-    def along_xy(self):
+    def merge(self):
         self.quad = self.merged(self.deep)
         self.half = self.quad.shape[0] // 2
+
+    def along_xy(self):
         self.by_y = self.move(self.quad, 4)
         self.by_x = self.move(self.quad, 2)
 
@@ -1006,7 +1057,7 @@
     def along_z(self):
         pass
 
-    along_xy = across = along_z
+    merge = along_xy = across = along_z
 
     def finish(self):
         full = lax.all_gather(self.pack, "fsdp")
@@ -1277,23 +1328,6 @@
 
 def split_high(values):
     return (values // 32).astype(jnp.bfloat16), (values % 32).astype(jnp.bfloat16)
-
-
-def factored(weight, raw, row_old, col_old, row_square, col_square, row_old_sum, rows_all, clip):
-    columns = weight.shape[-1]
-    row_new = DECAY_RATE * row_old + (1.0 - DECAY_RATE) * (
-        clip * (clip * (row_square / columns)) + FACTOR_EPS
-    )
-    col_new = DECAY_RATE * col_old + (1.0 - DECAY_RATE) * (
-        clip * (clip * (col_square / rows_all)) + FACTOR_EPS
-    )
-    row_mean = (
-        DECAY_RATE * row_old_sum
-        + (1.0 - DECAY_RATE) * (clip * (clip * (jnp.sum(col_square) / columns)))
-    ) / rows_all + (1.0 - DECAY_RATE) * FACTOR_EPS
-    clipped = clip * raw
-    estimate = row_new[:, None] * col_new[None, :] / row_mean
-    return (weight - LEARN_RATE * clipped * lax.rsqrt(estimate), clipped, row_new, col_new)
 
 
 def body(
@@ -1380,9 +1414,7 @@
 
     def see_one(blocks):
         if count == 32:
-            blocks, layers[0].deep[1], layers[0].deep[3] = meet(
-                blocks, layers[0].deep[1], layers[0].deep[3]
-            )
+            blocks, layers[0].deep[2] = meet(blocks, layers[0].deep[2])
         return blocks
 
     small_all, time_out_mine = gather_and_turn(
@@ -1431,6 +1463,7 @@
 
         def start_near(pieces):
             pieces, layers[0].deep = meet(pieces, layers[0].deep)
+            layers[0].merge()
             layers[0].along_xy()
             return pieces
 
@@ -1450,8 +1483,9 @@
 
     layers[0].across()
     if count == 32:
-        layers[0].far, rest.deep, layers[1].pack = meet(
-            layers[0].far, rest.deep, layers[1].pack
+        rest.merge()
+        layers[0].far, rest.quad, layers[1].pack = meet(
+            layers[0].far, rest.quad, layers[1].pack
         )
     layers[0].finish()
     rest.along_xy()
@@ -1480,7 +1514,8 @@
     hidden, *kept[0] = forward(0, hidden)
     first_out = hidden
     if count == 32:
-        hidden, rest.far, layers[1].deep = meet(hidden, rest.far, layers[1].deep)
+        layers[1].merge()
+        hidden, rest.far, layers[1].quad = meet(hidden, rest.far, layers[1].quad)
     first_out = hidden
     layers[1].along_xy()
     rest.finish()
@@ -1526,10 +1561,10 @@
             grad_hidden, level_mods, kept[level][1], orders, layers[level]
         )
         if count == 32 and level == 0:
-            one_sum.far, rest_sum.deep = meet(one_sum.far, rest_sum.deep)
             one_sum.make_near()
             grad_middle, one_sum.to_near = meet(grad_middle, one_sum.to_near)
             one_sum.along_xy()
+            grad_middle, rest_sum.deep = meet(grad_middle, rest_sum.deep)
         grad_hidden, attn_mods, attn_bias, attn_mine, *attn_theirs = attn_backward(
             grad_middle, level_mods, kept[level][0], orders, layers[level]
         )
@@ -1724,7 +1759,26 @@
     ]
     olds = [block_in, block_down, stem_main, stem_proj]
     raw_list = [raw_in, raw_down, raw_main, raw_proj]
-    outputs = [shaped(FULL, 8, 128)]
+    late_flat = jnp.zeros((count * bias_part,), jnp.float32)
+    late_flat = lax.dynamic_update_slice(late_flat, late_bias, (L * VB,))
+    bias_raw = bias_shard + lax.dynamic_slice(late_flat, (position * bias_part,), (bias_part,))
+    flat_rows = [
+        jnp.stack(row_olds[0:2] + row_squares[0:2]),
+        jnp.stack(row_olds[2:4] + row_squares[2:4]),
+        jnp.stack([row_olds[4], row_squares[4]]),
+        jnp.stack([row_olds[5], row_squares[5]]),
+    ]
+    outputs = [
+        shaped(FULL, 8, 128),
+        shaped(FULL, *head_weight.shape),
+        shaped(FULL, *head_weight.shape),
+        shaped(FULL, head_weight.shape[0], 1),
+        shaped(FULL, 1, head_weight.shape[1]),
+        shaped(FULL, *block_in_rows.shape),
+        shaped(FULL, *block_down_rows.shape),
+        shaped(FULL, 1, *stem_main_rows.shape),
+        shaped(FULL, 1, *stem_proj_rows.shape),
+    ] + [shaped(FULL, 1, bias_part)] * 3
     col_old_list = [block_in_cols, block_down_cols, stem_main_cols[None], stem_proj_cols[None]]
     for old, col_old in zip(olds, col_old_list):
         outputs += [shaped(FULL, *old.shape), shaped(FULL, *old.shape), shaped(LOW, *old.shape)]
@@ -1746,6 +1800,13 @@
             row_sums,
             late_bias.reshape(2, D),
             head_sum,
+            head_weight,
+            head_rows[:, None],
+            head_cols[None],
+            *flat_rows,
+            bias_raw[None],
+            biases[None],
+            bias_second[None],
         ],
         [],
         outputs,
@@ -1754,43 +1815,16 @@
         12,
         0,
     )
-    grad_norm, clip = made[0][0, 0], made[0][1, 0]
+    grad_norm = made[0][0, 0]
+    new_head, head_clip, rows_head, cols_head = made[1], made[2], made[3][:, 0], made[4][0]
+    rows_in, rows_down, rows_main, rows_proj = made[5], made[6], made[7][0], made[8][0]
+    new_bias, clip_bias, second_new = (part[0] for part in made[9:12])
     (
         (new_in, clip_in, copy_in, cols_in),
         (new_down, clip_down, copy_down, cols_down),
         (new_main, clip_main, copy_main, cols_main),
         (new_proj, clip_proj, copy_proj, cols_proj),
-    ) = (made[1 + 4 * slot : 5 + 4 * slot] for slot in range(4))
-
-    def new_rows(row_old, row_square, columns):
-        return DECAY_RATE * row_old + (1.0 - DECAY_RATE) * (
-            clip * (clip * (row_square / columns)) + FACTOR_EPS
-        )
-
-    rows_in = new_rows(block_in_rows, jnp.stack(row_squares[0:2]), block_in.shape[-1])
-    rows_down = new_rows(block_down_rows, jnp.stack(row_squares[2:4]), D)
-    rows_main = new_rows(stem_main_rows, row_squares[4], stem_main.shape[-1])
-    rows_proj = new_rows(stem_proj_rows, row_squares[5], stem_proj.shape[-1])
-    head_square = head_sum * head_sum
-    new_head, head_clip, rows_head, cols_head = factored(
-        head_weight,
-        head_sum,
-        head_rows,
-        head_cols,
-        jnp.sum(head_square, axis=1),
-        jnp.sum(head_square, axis=0),
-        jnp.sum(head_rows),
-        D + 1,
-        clip,
-    )
-    late_flat = jnp.zeros((count * bias_part,), jnp.float32)
-    late_flat = lax.dynamic_update_slice(late_flat, late_bias, (L * VB,))
-    bias_raw = bias_shard + lax.dynamic_slice(late_flat, (position * bias_part,), (bias_part,))
-    clip_bias = clip * bias_raw
-    second_new = DECAY_RATE * bias_second + (1.0 - DECAY_RATE) * (
-        clip_bias * clip_bias + FACTOR_EPS
-    )
-    new_bias = biases - LEARN_RATE * clip_bias * lax.rsqrt(second_new)
+    ) = (made[12 + 4 * slot : 16 + 4 * slot] for slot in range(4))
     return (
         loss_total,
         grad_norm,

time: 751 us -> 728 us (0.969)
    unnamed x325 -> x280, local copies, waits for them, and re-layouts: 24.5 us -> 16.9 us
  transfers between devices with their start and end apart: 99 -> 99, of which waited for: 47 -> 50; matrix products, arithmetic and copies ran while one was open for 12% -> 12% of each run, Pallas kernels for 25% -> 26%
where the time goes in v4:
time: 728 us; the launch traced here: 720 us
  waiting for transfers between devices  251 us (34%)
  Pallas kernels  212 us (29%)
  starting transfers between devices  112 us (15%)
  local copies, waits for them, and re-layouts  79.9 us (11%)
  other arithmetic  50.2 us (7%)
  matrix products  8.91 us (1%)
    ppermute x99, waiting for transfers between devices, swap(): lax.ppermute(array, 'fsdp', [(place, place ^ mask) for place in range(cou...  251 us
    pallas_call x11, Pallas kernels, call(): pl.pallas_call(kernel, in_specs=[VMEM_WHOLE] * len(inputs) + [IN_PLACE] *...  159 us
    ppermute x99, starting transfers between devices, swap(): lax.ppermute(array, 'fsdp', [(place, place ^ mask) for place in range(cou...  112 us
    pallas_call x9, Pallas kernels, call(): pl.pallas_call(kernel, in_specs=[VMEM_WHOLE] * len(near) + [IN_PLACE] * l...  50.5 us
    unnamed x280, local copies, waits for them, and re-layouts  16.9 us
  transfers between devices with their start and end apart: 99, of which 50 were waited for; matrix products, arithmetic and copies ran while one was open for 12% of the time, Pallas kernels for 26%

profile of v4, /device:TPU:0, one launch (start us, length us, event | category | flops | bytes accessed | tf_op | source)
XLA Modules:
  0.0 720.1 jit_solution(9024022708831247975)
XLA Ops:
  33.2 13.8 %collective-permute-done.4 = bf16[15,24,768]{2,1,0:T(8,128)(2,1)S(1)} collective-permute-done((bf16[15,24,768]{2,1,0:T(8,128)(2,1)S(1)}, bf16[15,24,768]{2,1,0:T(8,128)(2,1)S(1)}, u32[]{:S(2)}, u32[]{:S(2)}) %collective-permute-start.4) | collective-permute-done | bytes 552992 | tf_op jit(solution)/shard_map/ppermute | solution.py:949
  79.5 10.5 %collective-permute-done.9 = bf16[15,24,768]{2,1,0:T(8,128)(2,1)} collective-permute-done((bf16[15,24,768]{2,1,0:T(8,128)(2,1)S(1)}, bf16[15,24,768]{2,1,0:T(8,128)(2,1)}, u32[]{:S(2)}, u32[]{:S(2)}) %collective-permute-start.9) | collective-permute-done | bytes 552992 | tf_op jit(solution)/shard_map/ppermute | solution.py:949
  127.2 12.9 %collective-permute-done.16 = bf16[1,64,2816]{2,1,0:T(8,128)(2,1)} collective-permute-done((bf16[1,64,2816]{2,1,0:T(8,128)(2,1)S(1)}, bf16[1,64,2816]{2,1,0:T(8,128)(2,1)}, u32[]{:S(2)}, u32[]{:S(2)}) %collective-permute-start.16) | collective-permute-done | bytes 360480 | tf_op jit(solution)/shard_map/ppermute | solution.py:949
  154.5 19.8 %collective-permute-done.18.refs_3_ = bf16[7,96,768]{2,1,0:T(8,128)(2,1)S(1)} collective-permute-done((bf16[7,96,768]{2,1,0:T(8,128)(2,1)S(1)}, bf16[7,96,768]{2,1,0:T(8,128)(2,1)S(1)}, u32[]{:S(2)}, u32[]{:S(2)}) %collective-permute-start.18) | collective-permute-done | bytes 1032224 | tf_op jit(solution)/shard_map/ppermute | solution.py:949
  189.9 13.4 %shard_map.492 = (bf16[256,768]{1,0:T(8,128)(2,1)}, bf16[3,256,768]{2,1,0:T(8,128)(2,1)}, f32[256,128]{1,0:T(8,128)}, bf16[256,768]{1,0:T(8,128)(2,1)}, f32[256,768]{1,0:T(8,128)}, /*index=5*/f32[256,768]{1,0:T(8,128)}) custom-call(f32[256,768]{1,0:T(8,128)} %fusion.1.hidden, f32[6,768]{1,0:T(8,128)} %get-tuple-element.670.mods, ...), custom_call_target="tpu_custom_call" | custom-call | flops 11 | tf_op jit(solution)/shard_map/pallas_call | solution.py:746
  204.0 13.9 %collective-permute-done.28 = bf16[12,24,768]{2,1,0:T(8,128)(2,1)S(1)} collective-permute-done((bf16[12,24,768]{2,1,0:T(8,128)(2,1)}, bf16[12,24,768]{2,1,0:T(8,128)(2,1)S(1)}, u32[]{:S(2)}, u32[]{:S(2)}) %collective-permute-start.28) | collective-permute-done | bytes 442400 | tf_op jit(solution)/shard_map/ppermute | solution.py:949
  225.8 14.3 %shard_map.493 = (bf16[256,768]{1,0:T(8,128)(2,1)}, bf16[4,256,768]{2,1,0:T(8,128)(2,1)}, bf16[4,256,768]{2,1,0:T(8,128)(2,1)}, f32[256,768]{1,0:T(8,128)}, f32[256,768]{1,0:T(8,128)}) custom-call(f32[256,768]{1,0:T(8,128)} %get-tuple-element.268.middle, f32[6,768]{1,0:T(8,128)} %get-tuple-element.670.mods, f32[15,768]{1,0:T(8,128)} %get-tuple-element.662.bias, ...), custom_call_target="tpu_custom_call" | custom-call | flops 11 | tf_op jit(solution)/shard_map/pallas_call | solution.py:746
  248.4 27.0 %shard_map.495 = (f32[256,768]{1,0:T(8,128)}, f32[8,128]{1,0:T(8,128)}, f32[1,2048]{1,0:T(1,128)}, f32[1,2048]{1,0:T(1,128)}, f32[1,768]{1,0:T(1,128)}, /*index=...) custom-call(f32[256,768]{1,0:T(8,128)} %get-tuple-element.277.hidden, ...), custom_call_target="tpu_custom_call" | custom-call | flops 27 | tf_op jit(solution)/shard_map/pallas_call | solution.py:746
  288.5 19.3 %collective-permute-done.34.refs_3_ = bf16[6,96,768]{2,1,0:T(8,128)(2,1)} collective-permute-done((bf16[6,96,768]{2,1,0:T(8,128)(2,1)S(1)}, bf16[6,96,768]{2,1,0:T(8,128)(2,1)}, u32[]{:S(2)}, u32[]{:S(2)}) %collective-permute-start.34) | collective-permute-done | bytes 884768 | tf_op jit(solution)/shard_map/ppermute | solution.py:949
  311.9 13.0 %shard_map.494 = (bf16[256,768]{1,0:T(8,128)(2,1)}, bf16[3,256,768]{2,1,0:T(8,128)(2,1)}, f32[256,128]{1,0:T(8,128)}, bf16[256,768]{1,0:T(8,128)(2,1)}, f32[256,768]{1,0:T(8,128)}, /*index=5*/f32[256,768]{1,0:T(8,128)}) custom-call(f32[256,768]{1,0:T(8,128)} %get-tuple-element.277.hidden.first, f32[6,768]{1,0:T(8,128)} %get-tuple-element.669.mods, ...), custom_call_target="tpu_custom_call" | custom-call | flops 11 | tf_op jit(solution)/shard_map/pallas_call | solution.py:746
  330.9 13.6 %shard_map.497 = (bf16[256,768]{1,0:T(8,128)(2,1)}, bf16[4,256,768]{2,1,0:T(8,128)(2,1)}, bf16[4,256,768]{2,1,0:T(8,128)(2,1)}, f32[256,768]{1,0:T(8,128)}, f32[256,768]{1,0:T(8,128)}) custom-call(f32[256,768]{1,0:T(8,128)} %get-tuple-element.290.middle, f32[6,768]{1,0:T(8,128)} %get-tuple-element.669.mods, f32[15,768]{1,0:T(8,128)} %get-tuple-element.661.bias, ...), custom_call_target="tpu_custom_call" | custom-call | flops 11 | tf_op jit(solution)/shard_map/pallas_call | solution.py:746
  356.5 16.4 %shard_map.500 = (f32[256,768]{1,0:T(8,128)}, f32[3,768]{1,0:T(4,128)}, f32[5,768]{1,0:T(8,128)}, bf16[8,384,768]{2,1,0:T(8,128)(2,1)}, bf16[2,384,768]{2,1,0:T(...) custom-call(f32[256,768]{1,0:T(8,128)} %get-tuple-element.297.grad_out, ...), custom_call_target="tpu_custom_call" | custom-call | flops 16 | tf_op jit(solution)/shard_map/pallas_call | solution.py:746
  373.5 16.1 %shard_map.501 = (f32[256,768]{1,0:T(8,128)}, f32[3,768]{1,0:T(4,128)}, f32[4,768]{1,0:T(4,128)}, bf16[4,384,768]{2,1,0:T(8,128)(2,1)}, bf16[2,384,768]{2,1,0:T(8,128)(2,1)}, /*index=5*/bf16[2,384,768]{2,1,0:T(8,128)(2,1)}) custom-call(f32[256,768]{1,0:T(8,128)} %get-tuple-element.302.grad_middle, f32[6,768]{1,0:T(8,128)} %get-tuple-element.669.mods, ...), custom_call_target="tpu_custom_call" | custom-call | flops 13 | tf_op jit(solution)/shard_map/pallas_call | solution.py:746
  409.3 8.8 %collective-permute-start.63 = (bf16[1,64,2816]{2,1,0:T(8,128)(2,1)}, bf16[1,64,2816]{2,1,0:T(8,128)(2,1)S(1)}, u32[]{:S(2)}, u32[]{:S(2)}) collective-permute-start(bf16[1,64,2816]{2,1,0:T(8,128)(2,1)} %get-tuple-element.339), channel_id=1, source_target_pairs={{0,8},{1,9},{2,10},{3,11},{4,12},{5,13},{6,14},{7,15},{8,0},{9,1},... | collective-permute-start | bytes 1081352 | tf_op jit(solution)/shard_map/ppermute | solution.py:949
  420.6 16.7 %shard_map.503 = (f32[256,768]{1,0:T(8,128)}, f32[3,768]{1,0:T(4,128)}, f32[5,768]{1,0:T(8,128)}, bf16[8,384,768]{2,1,0:T(8,128)(2,1)}, bf16[2,384,768]{2,1,0:T(...) custom-call(f32[256,768]{1,0:T(8,128)} %add.709.grad_out, ...), custom_call_target="tpu_custom_call" | custom-call | flops 16 | tf_op jit(solution)/shard_map/pallas_call | solution.py:746
  450.1 16.0 %shard_map.506 = (f32[256,768]{1,0:T(8,128)}, f32[3,768]{1,0:T(4,128)}, f32[4,768]{1,0:T(4,128)}, bf16[4,384,768]{2,1,0:T(8,128)(2,1)}, bf16[2,384,768]{2,1,0:T(8,128)(2,1)}, /*index=5*/bf16[2,384,768]{2,1,0:T(8,128)(2,1)}) custom-call(f32[256,768]{1,0:T(8,128)} %get-tuple-element.342.grad_middle, f32[6,768]{1,0:T(8,128)} %get-tuple-element.670.mods, ...), custom_call_target="tpu_custom_call" | custom-call | flops 13 | tf_op jit(solution)/shard_map/pallas_call | solution.py:746
  477.4 21.0 %collective-permute-done.66.by_x = bf16[15,96,768]{2,1,0:T(8,128)(2,1)} collective-permute-done((bf16[15,96,768]{2,1,0:T(8,128)(2,1)}, bf16[15,96,768]{2,1,0:T(8,128)(2,1)}, u32[]{:S(2)}, u32[]{:S(2)}) %collective-permute-start.66) | collective-permute-done | bytes 2211872 | tf_op jit(solution)/shard_map/ppermute | solution.py:949
  541.1 12.6 %collective-permute-done.80 = bf16[15,24,768]{2,1,0:T(8,128)(2,1)} collective-permute-done((bf16[15,24,768]{2,1,0:T(8,128)(2,1)}, bf16[15,24,768]{2,1,0:T(8,128)(2,1)}, u32[]{:S(2)}, u32[]{:S(2)}) %collective-permute-start.80) | collective-permute-done | bytes 552992 | tf_op jit(solution)/shard_map/ppermute | solution.py:949
  553.7 11.1 %collective-permute-start.82 = (bf16[800,128]{1,0:T(8,128)(2,1)S(1)}, bf16[800,128]{1,0:T(8,128)(2,1)S(1)}, u32[]{:S(2)}, u32[]{:S(2)}) collective-permute-start(bf16[800,128]{1,0:T(8,128)(2,1)S(1)} %pad_maximum_fusion.13), channel_id=1, source_target_pairs={{0,8},{1,9},{2,10},{3,11},{4,12},{5,13},{6,14},{7,15},{8,0},{9,1},... | collective-permute-start | bytes 614408 | tf_op jit(solution)/shard_map/ppermute | solution.py:949
  574.9 15.6 %collective-permute-done.83 = bf16[1552,128]{1,0:T(8,128)(2,1)} collective-permute-done((bf16[1552,128]{1,0:T(8,128)(2,1)}, bf16[1552,128]{1,0:T(8,128)(2,1)}, u32[]{:S(2)}, u32[]{:S(2)}) %collective-permute-start.83) | collective-permute-done | bytes 397344 | tf_op jit(solution)/shard_map/ppermute | solution.py:949
  626.5 12.3 %collective-permute-done.88 = bf16[12,24,768]{2,1,0:T(8,128)(2,1)} collective-permute-done((bf16[12,24,768]{2,1,0:T(8,128)(2,1)}, bf16[12,24,768]{2,1,0:T(8,128)(2,1)}, u32[]{:S(2)}, u32[]{:S(2)}) %collective-permute-start.88) | collective-permute-done | bytes 442400 | tf_op jit(solution)/shard_map/ppermute | solution.py:949
  638.8 11.5 %collective-permute-done.89 = bf16[12,24,768]{2,1,0:T(8,128)(2,1)} collective-permute-done((bf16[12,24,768]{2,1,0:T(8,128)(2,1)}, bf16[12,24,768]{2,1,0:T(8,128)(2,1)}, u32[]{:S(2)}, u32[]{:S(2)}) %collective-permute-start.89) | collective-permute-done | bytes 442400 | tf_op jit(solution)/shard_map/ppermute | solution.py:949
  672.4 9.7 %collective-permute-start.97 = (f32[360,128]{1,0:T(8,128)S(1)}, f32[360,128]{1,0:T(8,128)S(1)}, u32[]{:S(2)}, u32[]{:S(2)}) collective-permute-start(f32[360,128]{1,0:T(8,128)S(1)} %add.739), channel_id=1, source_target_pairs={{0,8},{1,9},{2,10},{3,11},{4,12},{5,13},{6,14},{7,15},{8,0},{9,1},... | collective-permute-start | bytes 552968 | tf_op jit(solution)/shard_map/ppermute | solution.py:949
  701.2 9.4 %shard_map.511 = (f32[8,128]{1,0:T(8,128)}, f32[769,16]{1,0:T(8,128)}, f32[769,16]{1,0:T(8,128)}, f32[769,1]{1,0:T(8,128)}, f32[1,16]{1,0:T(1,128)}, /*index=5*/...) custom-call(f32[2,24,10752]{2,1,0:T(8,128)} %pad_maximum_fusion.raw_, ...), custom_call_target="tpu_custom_call" | custom-call | flops 12 | tf_op jit(solution)/shard_map/pallas_call | solution.py:746
  (784 shorter events, 364.2 us)
Async XLA Ops:
  95.4 50.2 %collective-permute-start.13 = (bf16[15,96,768]{2,1,0:T(8,128)(2,1)S(1)}, bf16[15,96,768]{2,1,0:T(8,128)(2,1)}, u32[]{:S(2)}, u32[]{:S(2)}) collective-permute-start(bf16[15,96,768]{2,1,0:T(8,128)(2,1)S(1)} %bitcast_dynamic-update-slice_fusion.4.refs_0_), channel_id=1, source_target_pairs={{0,2},{1,3},{2,0},{3,1},{4,6},{5,7},{6,4},{7,5},{8,10},{9,11},{10,... | collective-permute-start | bytes 6635528 | tf_op jit(solution)/shard_map/ppermute | solution.py:949
  96.0 49.8 %collective-permute-start.14 = (bf16[15,96,768]{2,1,0:T(8,128)(2,1)S(1)}, bf16[15,96,768]{2,1,0:T(8,128)(2,1)}, u32[]{:S(2)}, u32[]{:S(2)}) collective-permute-start(bf16[15,96,768]{2,1,0:T(8,128)(2,1)S(1)} %bitcast_dynamic-update-slice_fusion.4.refs_0_), channel_id=1, source_target_pairs={{0,4},{1,5},{2,6},{3,7},{4,0},{5,1},{6,2},{7,3},{8,12},{9,13},{10,... | collective-permute-start | bytes 6635528 | tf_op jit(solution)/shard_map/ppermute | solution.py:949
  151.5 32.7 %collective-permute-start.21 = (bf16[15,96,768]{2,1,0:T(8,128)(2,1)}, bf16[15,96,768]{2,1,0:T(8,128)(2,1)}, u32[]{:S(2)}, u32[]{:S(2)}) collective-permute-start(bf16[15,96,768]{2,1,0:T(8,128)(2,1)} %collective-permute-done.13.refs_1_), channel_id=1, source_target_pairs={{0,1},{1,0},{2,3},{3,2},{4,5},{5,4},{6,7},{7,6},{8,9},{9,8},{10,11... | collective-permute-start | bytes 6635528 | tf_op jit(solution)/shard_map/ppermute | solution.py:949
  151.8 33.0 %collective-permute-start.22 = (bf16[15,96,768]{2,1,0:T(8,128)(2,1)}, bf16[15,96,768]{2,1,0:T(8,128)(2,1)}, u32[]{:S(2)}, u32[]{:S(2)}) collective-permute-start(bf16[15,96,768]{2,1,0:T(8,128)(2,1)} %collective-permute-done.14.refs_2_), channel_id=1, source_target_pairs={{0,1},{1,0},{2,3},{3,2},{4,5},{5,4},{6,7},{7,6},{8,9},{9,8},{10,11... | collective-permute-start | bytes 6635528 | tf_op jit(solution)/shard_map/ppermute | solution.py:949
  176.4 41.5 %collective-permute-start.25 = (bf16[4,64,2816]{2,1,0:T(8,128)(2,1)}, bf16[4,64,2816]{2,1,0:T(8,128)(2,1)}, u32[]{:S(2)}, u32[]{:S(2)}) collective-permute-start(bf16[4,64,2816]{2,1,0:T(8,128)(2,1)} %pad_maximum_fusion.2.refs_10_), channel_id=1, source_target_pairs={{0,2},{1,3},{2,0},{3,1},{4,6},{5,7},{6,4},{7,5},{8,10},{9,11},{10,... | collective-permute-start | bytes 4325384 | tf_op jit(solution)/shard_map/ppermute | solution.py:949
  178.9 39.1 %collective-permute-start.26 = (bf16[4,64,2816]{2,1,0:T(8,128)(2,1)}, bf16[4,64,2816]{2,1,0:T(8,128)(2,1)S(1)}, u32[]{:S(2)}, u32[]{:S(2)}) collective-permute-start(bf16[4,64,2816]{2,1,0:T(8,128)(2,1)} %pad_maximum_fusion.2.refs_10_), channel_id=1, source_target_pairs={{0,4},{1,5},{2,6},{3,7},{4,0},{5,1},{6,2},{7,3},{8,12},{9,13},{10,... | collective-permute-start | bytes 4325384 | tf_op jit(solution)/shard_map/ppermute | solution.py:949
  184.8 33.2 %collective-permute-start.28 = (bf16[12,24,768]{2,1,0:T(8,128)(2,1)}, bf16[12,24,768]{2,1,0:T(8,128)(2,1)S(1)}, u32[]{:S(2)}, u32[]{:S(2)}) collective-permute-start(bf16[12,24,768]{2,1,0:T(8,128)(2,1)} %pad_maximum_fusion.8), channel_id=1, source_target_pairs={{0,16},{1,17},{2,18},{3,19},{4,20},{5,21},{6,22},{7,23},{8,24},{9,... | collective-permute-start | bytes 1327112 | tf_op jit(solution)/shard_map/ppermute | solution.py:949
  185.2 32.8 %collective-permute-start.29 = (bf16[12,24,768]{2,1,0:T(8,128)(2,1)}, bf16[12,24,768]{2,1,0:T(8,128)(2,1)}, u32[]{:S(2)}, u32[]{:S(2)}) collective-permute-start(bf16[12,24,768]{2,1,0:T(8,128)(2,1)} %pad_maximum_fusion.8), channel_id=1, source_target_pairs={{0,24},{1,25},{2,26},{3,27},{4,28},{5,29},{6,30},{7,31},{8,16},{9,... | collective-permute-start | bytes 1327112 | tf_op jit(solution)/shard_map/ppermute | solution.py:949
  204.0 39.2 %collective-permute-start.41 = (bf16[4,64,2816]{2,1,0:T(8,128)(2,1)}, bf16[4,64,2816]{2,1,0:T(8,128)(2,1)}, u32[]{:S(2)}, u32[]{:S(2)}) collective-permute-start(bf16[4,64,2816]{2,1,0:T(8,128)(2,1)} %pad_maximum_fusion.2.refs_10_), channel_id=1, source_target_pairs={{0,1},{1,0},{2,3},{3,2},{4,5},{5,4},{6,7},{7,6},{8,9},{9,8},{10,11... | collective-permute-start | bytes 4325384 | tf_op jit(solution)/shard_map/ppermute | solution.py:949
  242.2 39.9 %collective-permute-start.33 = (bf16[12,96,768]{2,1,0:T(8,128)(2,1)S(1)}, bf16[12,96,768]{2,1,0:T(8,128)(2,1)S(1)}, u32[]{:S(2)}, u32[]{:S(2)}) collective-permute-start(bf16[12,96,768]{2,1,0:T(8,128)(2,1)S(1)} %bitcast_dynamic-update-slice_fusion.refs_0_), channel_id=1, source_target_pairs={{0,4},{1,5},{2,6},{3,7},{4,0},{5,1},{6,2},{7,3},{8,12},{9,13},{10,... | collective-permute-start | bytes 5308424 | tf_op jit(solution)/shard_map/ppermute | solution.py:949
  243.3 41.1 %collective-permute-start.32 = (bf16[12,96,768]{2,1,0:T(8,128)(2,1)S(1)}, bf16[12,96,768]{2,1,0:T(8,128)(2,1)}, u32[]{:S(2)}, u32[]{:S(2)}) collective-permute-start(bf16[12,96,768]{2,1,0:T(8,128)(2,1)S(1)} %bitcast_dynamic-update-slice_fusion.refs_0_), channel_id=1, source_target_pairs={{0,2},{1,3},{2,0},{3,1},{4,6},{5,7},{6,4},{7,5},{8,10},{9,11},{10,... | collective-permute-start | bytes 5308424 | tf_op jit(solution)/shard_map/ppermute | solution.py:949
  327.3 62.9 %collective-permute-start.60 = (bf16[3,384,768]{2,1,0:T(8,128)(2,1)}, bf16[3,384,768]{2,1,0:T(8,128)(2,1)S(1)}, u32[]{:S(2)}, u32[]{:S(2)}) collective-permute-start(bf16[3,384,768]{2,1,0:T(8,128)(2,1)} %get-tuple-element.323), channel_id=1, source_target_pairs={{0,1},{1,0},{2,3},{3,2},{4,5},{5,4},{6,7},{7,6},{8,9},{9,8},{10,11... | collective-permute-start | bytes 5308424 | tf_op jit(solution)/shard_map/ppermute | solution.py:949
  354.7 34.9 %collective-permute-start.52 = (bf16[4,64,2816]{2,1,0:T(8,128)(2,1)}, bf16[4,64,2816]{2,1,0:T(8,128)(2,1)}, u32[]{:S(2)}, u32[]{:S(2)}) collective-permute-start(bf16[4,64,2816]{2,1,0:T(8,128)(2,1)} %get-tuple-element.313), channel_id=1, source_target_pairs={{0,2},{1,3},{2,0},{3,1},{4,6},{5,7},{6,4},{7,5},{8,10},{9,11},{10,... | collective-permute-start | bytes 4325384 | tf_op jit(solution)/shard_map/ppermute | solution.py:949
  356.0 34.0 %collective-permute-start.53 = (bf16[4,64,2816]{2,1,0:T(8,128)(2,1)}, bf16[4,64,2816]{2,1,0:T(8,128)(2,1)}, u32[]{:S(2)}, u32[]{:S(2)}) collective-permute-start(bf16[4,64,2816]{2,1,0:T(8,128)(2,1)} %get-tuple-element.314), channel_id=1, source_target_pairs={{0,4},{1,5},{2,6},{3,7},{4,0},{5,1},{6,2},{7,3},{8,12},{9,13},{10,... | collective-permute-start | bytes 4325384 | tf_op jit(solution)/shard_map/ppermute | solution.py:949
  401.9 37.0 %collective-permute-start.62 = (bf16[8,96,768]{2,1,0:T(8,128)(2,1)}, bf16[8,96,768]{2,1,0:T(8,128)(2,1)}, u32[]{:S(2)}, u32[]{:S(2)}) collective-permute-start(bf16[8,96,768]{2,1,0:T(8,128)(2,1)} %get-tuple-element.333), channel_id=1, source_target_pairs={{0,2},{1,3},{2,0},{3,1},{4,6},{5,7},{6,4},{7,5},{8,10},{9,11},{10,... | collective-permute-start | bytes 3538952 | tf_op jit(solution)/shard_map/ppermute | solution.py:949
  402.8 34.5 %collective-permute-start.61 = (bf16[7,96,768]{2,1,0:T(8,128)(2,1)}, bf16[7,96,768]{2,1,0:T(8,128)(2,1)S(1)}, u32[]{:S(2)}, u32[]{:S(2)}) collective-permute-start(bf16[7,96,768]{2,1,0:T(8,128)(2,1)} %get-tuple-element.332), channel_id=1, source_target_pairs={{0,4},{1,5},{2,6},{3,7},{4,0},{5,1},{6,2},{7,3},{8,12},{9,13},{10,... | collective-permute-start | bytes 3096584 | tf_op jit(solution)/shard_map/ppermute | solution.py:949
  418.1 31.2 %collective-permute-start.65 = (bf16[1,64,2816]{2,1,0:T(8,128)(2,1)}, bf16[1,64,2816]{2,1,0:T(8,128)(2,1)S(1)}, u32[]{:S(2)}, u32[]{:S(2)}) collective-permute-start(bf16[1,64,2816]{2,1,0:T(8,128)(2,1)} %get-tuple-element.341), channel_id=1, source_target_pairs={{0,24},{1,25},{2,26},{3,27},{4,28},{5,29},{6,30},{7,31},{8,16},{9,... | collective-permute-start | bytes 1081352 | tf_op jit(solution)/shard_map/ppermute | solution.py:949
  448.0 50.4 %collective-permute-start.66 = (bf16[15,96,768]{2,1,0:T(8,128)(2,1)}, bf16[15,96,768]{2,1,0:T(8,128)(2,1)}, u32[]{:S(2)}, u32[]{:S(2)}) collective-permute-start(bf16[15,96,768]{2,1,0:T(8,128)(2,1)} %get-tuple-element.353), channel_id=1, source_target_pairs={{0,2},{1,3},{2,0},{3,1},{4,6},{5,7},{6,4},{7,5},{8,10},{9,11},{10,... | collective-permute-start | bytes 6635528 | tf_op jit(solution)/shard_map/ppermute | solution.py:949
  449.3 50.0 %collective-permute-start.67 = (bf16[15,96,768]{2,1,0:T(8,128)(2,1)}, bf16[15,96,768]{2,1,0:T(8,128)(2,1)}, u32[]{:S(2)}, u32[]{:S(2)}) collective-permute-start(bf16[15,96,768]{2,1,0:T(8,128)(2,1)} %get-tuple-element.354), channel_id=1, source_target_pairs={{0,4},{1,5},{2,6},{3,7},{4,0},{5,1},{6,2},{7,3},{8,12},{9,13},{10,... | collective-permute-start | bytes 6635528 | tf_op jit(solution)/shard_map/ppermute | solution.py:949
  513.4 40.3 %collective-permute-start.80 = (bf16[15,24,768]{2,1,0:T(8,128)(2,1)}, bf16[15,24,768]{2,1,0:T(8,128)(2,1)}, u32[]{:S(2)}, u32[]{:S(2)}) collective-permute-start(bf16[15,24,768]{2,1,0:T(8,128)(2,1)} %get-tuple-element.397), channel_id=1, source_target_pairs={{0,16},{1,17},{2,18},{3,19},{4,20},{5,21},{6,22},{7,23},{8,24},{9,... | collective-permute-start | bytes 1658888 | tf_op jit(solution)/shard_map/ppermute | solution.py:949
  539.6 62.5 %collective-permute-start.86 = (bf16[12,96,768]{2,1,0:T(8,128)(2,1)}, bf16[12,96,768]{2,1,0:T(8,128)(2,1)}, u32[]{:S(2)}, u32[]{:S(2)}) collective-permute-start(bf16[12,96,768]{2,1,0:T(8,128)(2,1)} %get-tuple-element.402), channel_id=1, source_target_pairs={{0,2},{1,3},{2,0},{3,1},{4,6},{5,7},{6,4},{7,5},{8,10},{9,11},{10,... | collective-permute-start | bytes 5308424 | tf_op jit(solution)/shard_map/ppermute | solution.py:949
  540.5 61.6 %collective-permute-start.87 = (bf16[12,96,768]{2,1,0:T(8,128)(2,1)}, bf16[12,96,768]{2,1,0:T(8,128)(2,1)}, u32[]{:S(2)}, u32[]{:S(2)}) collective-permute-start(bf16[12,96,768]{2,1,0:T(8,128)(2,1)} %get-tuple-element.403), channel_id=1, source_target_pairs={{0,4},{1,5},{2,6},{3,7},{4,0},{5,1},{6,2},{7,3},{8,12},{9,13},{10,... | collective-permute-start | bytes 5308424 | tf_op jit(solution)/shard_map/ppermute | solution.py:949
  617.1 33.2 %collective-permute-start.89 = (bf16[12,24,768]{2,1,0:T(8,128)(2,1)}, bf16[12,24,768]{2,1,0:T(8,128)(2,1)}, u32[]{:S(2)}, u32[]{:S(2)}) collective-permute-start(bf16[12,24,768]{2,1,0:T(8,128)(2,1)} %get-tuple-element.408), channel_id=1, source_target_pairs={{0,16},{1,17},{2,18},{3,19},{4,20},{5,21},{6,22},{7,23},{8,24},{9,... | collective-permute-start | bytes 1327112 | tf_op jit(solution)/shard_map/ppermute | solution.py:949
  620.0 30.3 %collective-permute-start.90 = (bf16[12,24,768]{2,1,0:T(8,128)(2,1)}, bf16[12,24,768]{2,1,0:T(8,128)(2,1)}, u32[]{:S(2)}, u32[]{:S(2)}) collective-permute-start(bf16[12,24,768]{2,1,0:T(8,128)(2,1)} %get-tuple-element.409), channel_id=1, source_target_pairs={{0,24},{1,25},{2,26},{3,27},{4,28},{5,29},{6,30},{7,31},{8,16},{9,... | collective-permute-start | bytes 1327112 | tf_op jit(solution)/shard_map/ppermute | solution.py:949
  (200 other events, 2697.1 us)
